TPU v7x, 32 devices: a whole 2x2x4 slice. The times are simulated.
32 devices in a mesh: group: 4 (over z), local: 4 (over y, x), rep: 2 (over core).
Axes of the slice: x: 2, y: 2, z: 4, core: 2. Of those that a mesh axis runs over, the one named last changes fastest.
Arguments:
- tokens: bfloat16 [2048, 2560], P(('rep', 'group', 'local')), parts along dimension 0, may hold values from -6 to 6
- gates: bfloat16 [2048, 8], P(('rep', 'group', 'local')), parts along dimension 0, may hold values from 0.049804688 to 1
- expert_ids: int32 [2048, 8], P(('rep', 'group', 'local')), parts along dimension 0, may hold values from 0 to 15, as said below
- w_gate: bfloat16 [16, 2560, 768], P(('group', 'local')), may hold values from -0.125 to 0.125
- w_up: bfloat16 [16, 2560, 768], P(('group', 'local')), may hold values from -0.125 to 0.125
- w_down: bfloat16 [16, 768, 2560], P(('group', 'local')), may hold values from -0.21875 to 0.21875
Outputs:
- mixed: bfloat16 [2048, 2560], P(('rep', 'group', 'local')), parts along dimension 0
There are 2 independent parts, one for each index of `rep`. A program takes and returns all parts, laid end to end along the dimension named above; an argument that names none is the same for every part. Nothing has to cross between parts.
Inputs may be any that keep to these rules, and one draw needn't show every extreme that they name: `expert_ids`: each row names 8 different experts, which lie in at most 4 groups (expert // 4).
All inputs are finite; a program needn't handle non-finite values.
Results may differ from a plain program's by a relative error of at most 0.0057.
Values may be sent and summed in bfloat16 or wider, within the bound.
No kernel may reach another device: no remote copies, remote signals or barrier semaphores. Data moves between devices by JAX's collectives and lax.ppermute only.
A program may use at most 64 MiB of HBM per device.

v0:
```python
import jax
import jax.numpy as jnp
from jax import lax
from jax.sharding import PartitionSpec as P

GROUPS_TOK = 4


def expert_rows(rows, gate_mat, up_mat, down_mat):
    gate = jnp.dot(rows, gate_mat, preferred_element_type=jnp.float32)
    up = jnp.dot(rows, up_mat, preferred_element_type=jnp.float32)
    hidden = (jax.nn.silu(gate) * up).astype(jnp.bfloat16)
    return jnp.dot(hidden, down_mat, preferred_element_type=jnp.float32).astype(jnp.bfloat16)


def shards(tokens, gates, expert_ids, w_gate, w_up, w_down):
    tok_rows, width = tokens.shape
    n_group = lax.axis_size("group")
    local_expert_count = lax.axis_size("local")
    capacity = min(tok_rows, tok_rows * GROUPS_TOK // n_group)
    expert_iota = jnp.arange(n_group * local_expert_count, dtype=jnp.int32)
    hits = expert_ids[:, :, None] == expert_iota
    weights = jnp.sum(
        jnp.where(hits, gates.astype(jnp.float32)[:, :, None], jnp.float32(0.0)), axis=1
    )
    member = jnp.any(
        jnp.any(hits, axis=1).reshape(tok_rows, n_group, local_expert_count), axis=2
    ).astype(jnp.int32)
    rank = jnp.cumsum(member, axis=0) - member
    slot_iota = jnp.arange(capacity, dtype=jnp.int32)
    place = (member[:, :, None] == 1) & (rank[:, :, None] == slot_iota)
    place_f = place.astype(jnp.float32)
    outgoing = jnp.einsum(
        "tgc,td->gcd", place.astype(jnp.bfloat16), tokens, preferred_element_type=jnp.float32
    ).astype(jnp.bfloat16)
    slot_weights = jnp.einsum(
        "tgc,tgl->gcl",
        place_f,
        weights.reshape(tok_rows, n_group, local_expert_count),
        precision=lax.Precision.HIGHEST,
    ).astype(jnp.bfloat16)
    send_rows = jnp.broadcast_to(
        outgoing[:, None], (n_group, local_expert_count, capacity, width)
    ).reshape(n_group * local_expert_count, capacity, width)
    send_weights = jnp.transpose(slot_weights, (0, 2, 1)).reshape(
        n_group * local_expert_count, capacity
    )
    received_rows, got_weights = (
        lax.all_to_all(send_rows, ("group", "local"), split_axis=0, concat_axis=0, tiled=True),
        lax.all_to_all(send_weights, ("group", "local"), split_axis=0, concat_axis=0, tiled=True),
    )
    arrived = received_rows.reshape(n_group, local_expert_count, capacity, width)
    own_weights = got_weights.reshape(n_group, local_expert_count, capacity)
    outputs = expert_rows(
        arrived.reshape(n_group * local_expert_count * capacity, width),
        w_gate[0],
        w_up[0],
        w_down[0],
    )
    outputs = outputs.reshape(n_group, local_expert_count, capacity, width)
    masked = jnp.where(own_weights[..., None] > 0, outputs, jnp.zeros_like(outputs))
    returned_rows = lax.all_to_all(
        masked.reshape(n_group * local_expert_count, capacity, width),
        ("group", "local"),
        split_axis=0,
        concat_axis=0,
        tiled=True,
    )
    returned_rows = returned_rows.reshape(n_group, local_expert_count, capacity, width)
    sender_weights = jnp.transpose(slot_weights, (0, 2, 1))
    combined = jnp.einsum(
        "zqa,zqap->zap", sender_weights, returned_rows, preferred_element_type=jnp.float32
    )
    mixed = jnp.einsum("tgc,gcd->td", place_f, combined, precision=lax.Precision.HIGHEST)
    return mixed.astype(jnp.bfloat16)


def solution(mesh):
    in_specs = (
        P(("rep", "group", "local"), None),
        P(("rep", "group", "local"), None),
        P(("rep", "group", "local"), None),
        P(("group", "local"), None, None),
        P(("group", "local"), None, None),
        P(("group", "local"), None, None),
    )
    out_specs = P(("rep", "group", "local"), None)
    return jax.shard_map(shards, mesh=mesh, in_specs=in_specs, out_specs=out_specs, check_vma=False)
```

profile of v0, /device:TPU:14, one launch (start us, length us, event | category | flops | bytes accessed | tf_op | source)
XLA Modules:
  0.0 292.6 jit_solution(16855475369945980648)
XLA Ops:
  0.0 0.0 copy-start
  0.0 0.8 fusion.20
  0.8 0.1 copy.32
  0.9 0.1 reduce_window_sum.11
  1.0 0.1 copy.34
  1.1 0.1 copy.33
  1.2 0.7 convert_element_type.36
  1.9 0.7 select_reduce_fusion
  2.6 0.3 convolution_convert_fusion.2
  2.9 0.6 copy.35
  3.5 7.1 %all-to-all-start = ((bf16[16,1,64]{2,1,0:T(2,128)(2,1)}), bf16[16,1,64]{2,1,0:T(2,128)(2,1)S(1)}, u32[]{:S(2)}, u32[]{:S(2)}) async-start(bf16[16,1,64]{2,1,0:T(2,128)(2,1)} %copy.35), calls=%async_computation | async-start | bytes 16384 | tf_op jit(solution)/shard_map/all_to_all | solution.py:50
  10.6 0.0 copy-done
  10.6 0.6 convolution_convert_fusion.1
  11.3 3.4 %all-to-all-done = bf16[16,1,64]{2,1,0:T(2,128)(2,1)S(1)} async-done(((bf16[16,1,64]{2,1,0:T(2,128)(2,1)}), bf16[16,1,64]{2,1,0:T(2,128)(2,1)S(1)}, u32[]{:S(2)}, u32[]{:S(2)}) %all-to-all-start) | async-done | bytes 2080 | tf_op jit(solution)/shard_map/all_to_all | solution.py:50
  14.7 2.9 broadcast_in_dim.38
  17.5 7.6 %all-to-all-start.1 = ((bf16[16,64,2560]{2,1,0:T(8,128)(2,1)}), bf16[16,64,2560]{2,1,0:T(8,128)(2,1)}, u32[]{:S(2)}, u32[]{:S(2)}) async-start(bf16[16,64,2560]{2,1,0:T(8,128)(2,1)} %bitcast.36), calls=%async_computation.1 | async-start | bytes 10485760 | tf_op jit(solution)/shard_map/all_to_all | solution.py:49
  25.1 115.2 %all-to-all-done.1 = bf16[16,64,2560]{2,1,0:T(8,128)(2,1)} async-done(((bf16[16,64,2560]{2,1,0:T(8,128)(2,1)}), bf16[16,64,2560]{2,1,0:T(8,128)(2,1)}, u32[]{:S(2)}, u32[]{:S(2)}) %all-to-all-start.1) | async-done | bytes 5242912 | tf_op jit(solution)/shard_map/all_to_all | solution.py:49
  140.3 0.0 copy-start.1
  140.3 7.5 %fusion.3 = f32[1024,768]{1,0:T(8,128)S(1)} fusion(bf16[1024,2560]{1,0:T(8,128)(2,1)} %bitcast.7, bf16[1,2560,768]{2,1,0:T(8,128)(2,1)} %param.10), kind=kOutput, calls=%fused_computation.5 | convolution fusion | flops 4026531840 | bytes 12320768 | tf_op jit(solution)/shard_map/dot_general | solution.py:11
  147.8 0.0 copy-done.1
  147.8 0.0 copy-start.2
  147.8 7.2 %multiply_convert_fusion = bf16[1024,768]{1,0:T(8,128)(2,1)S(1)} fusion(f32[1024,768]{1,0:T(8,128)S(1)} %fusion.3, bf16[1024,2560]{1,0:T(8,128)(2,1)} %bitcast.7, bf16[1,2560,768]{2,1,0:T(8,128)(2,1)S(1)} %copy-done.1), kind=kOutput, calls=%fused_computation.12 | convolution fusion | flops 4031250432 | bytes 13893632 | tf_op jit(solution)/shard_map/dot_general | solution.py:10
  155.0 0.0 copy-done.2
  155.0 4.5 %convolution_convert_fusion = bf16[1024,2560]{1,0:T(8,128)(2,1)S(1)} fusion(bf16[1024,768]{1,0:T(8,128)(2,1)S(1)} %multiply_convert_fusion, bf16[1,768,2560]{2,1,0:T(8,128)(2,1)S(1)} %copy-done.2), kind=kOutput, calls=%fused_computation | convolution fusion | flops 4029153280 | bytes 10747904 | tf_op jit(solution)/shard_map/dot_general | solution.py:13
  159.5 2.8 broadcast_select_fusion
  162.3 5.1 %all-to-all-start.2 = ((bf16[16,64,2560]{2,1,0:T(8,128)(2,1)}), bf16[16,64,2560]{2,1,0:T(8,128)(2,1)}, u32[]{:S(2)}, u32[]{:S(2)}) async-start(bf16[16,64,2560]{2,1,0:T(8,128)(2,1)} %broadcast_select_fusion), calls=%async_computation.2 | async-start | bytes 10485760 | tf_op jit(solution)/shard_map/all_to_all | solution.py:62
  167.4 0.1 copy.39
  167.5 115.7 %all-to-all-done.2 = bf16[16,64,2560]{2,1,0:T(8,128)(2,1)} async-done(((bf16[16,64,2560]{2,1,0:T(8,128)(2,1)}), bf16[16,64,2560]{2,1,0:T(8,128)(2,1)}, u32[]{:S(2)}, u32[]{:S(2)}) %all-to-all-start.2) | async-done | bytes 5242912 | tf_op jit(solution)/shard_map/all_to_all | solution.py:62
  283.2 7.5 %fusion = f32[4,64,1,2560]{3,2,1,0:T(1,128)S(1)} fusion(bf16[4,4,64,1]{1,3,2,0:T(2,128)(2,1)S(1)} %copy.39, bf16[4,4,64,2560]{3,2,1,0:T(8,128)(2,1)} %bitcast.12), kind=kOutput, calls=%fused_computation.1 | convolution fusion | flops 5242880 | bytes 7866368 | tf_op jit(solution)/shard_map/zqa,zqap->zap/dot_general | solution.py:71
  290.7 1.9 fusion.7
  (4 shorter events, 0.1 us)
Async XLA Ops:
  0.0 10.6 %copy-start = (bf16[64,2560]{1,0:T(8,128)(2,1)S(1)}, bf16[64,2560]{1,0:T(8,128)(2,1)}, u32[]{:S(2)}) copy-start(bf16[64,2560]{1,0:T(8,128)(2,1)} %param.6) | copy-start | bytes 983044
  3.5 11.2 %all-to-all-start = ((bf16[16,1,64]{2,1,0:T(2,128)(2,1)}), bf16[16,1,64]{2,1,0:T(2,128)(2,1)S(1)}, u32[]{:S(2)}, u32[]{:S(2)}) async-start(bf16[16,1,64]{2,1,0:T(2,128)(2,1)} %copy.35), calls=%async_computation | async-start | bytes 16384 | tf_op jit(solution)/shard_map/all_to_all | solution.py:50
  17.5 122.8 %all-to-all-start.1 = ((bf16[16,64,2560]{2,1,0:T(8,128)(2,1)}), bf16[16,64,2560]{2,1,0:T(8,128)(2,1)}, u32[]{:S(2)}, u32[]{:S(2)}) async-start(bf16[16,64,2560]{2,1,0:T(8,128)(2,1)} %bitcast.36), calls=%async_computation.1 | async-start | bytes 10485760 | tf_op jit(solution)/shard_map/all_to_all | solution.py:49
  140.3 7.5 %copy-start.1 = (bf16[1,2560,768]{2,1,0:T(8,128)(2,1)S(1)}, bf16[1,2560,768]{2,1,0:T(8,128)(2,1)}, u32[]{:S(2)}) copy-start(bf16[1,2560,768]{2,1,0:T(8,128)(2,1)} %param.9) | copy-start | bytes 11796484
  147.8 7.2 %copy-start.2 = (bf16[1,768,2560]{2,1,0:T(8,128)(2,1)S(1)}, bf16[1,768,2560]{2,1,0:T(8,128)(2,1)}, u32[]{:S(2)}) copy-start(bf16[1,768,2560]{2,1,0:T(8,128)(2,1)} %param.11) | copy-start | bytes 11796484
  162.3 120.9 %all-to-all-start.2 = ((bf16[16,64,2560]{2,1,0:T(8,128)(2,1)}), bf16[16,64,2560]{2,1,0:T(8,128)(2,1)}, u32[]{:S(2)}, u32[]{:S(2)}) async-start(bf16[16,64,2560]{2,1,0:T(8,128)(2,1)} %broadcast_select_fusion), calls=%async_computation.2 | async-start | bytes 10485760 | tf_op jit(solution)/shard_map/all_to_all | solution.py:62
where the time goes:
time: 293 us
  waiting for transfers between devices  234 us (80%)
  matrix products  29.4 us (10%)
  starting transfers between devices  19.8 us (7%)
  other arithmetic  5.08 us (2%)
  local copies, waits for them, and re-layouts  3.91 us (1%)
    all_to_all x1, waiting for transfers between devices, shards(): lax.all_to_all(masked.reshape(n_group * local_expert_count, capacity, wid...  116 us
    all_to_all x1, waiting for transfers between devices, shards(): lax.all_to_all(send_rows, ('group', 'local'), split_axis=0, concat_axis=0...  115 us
    all_to_all x1, starting transfers between devices, shards(): lax.all_to_all(send_rows, ('group', 'local'), split_axis=0, concat_axis=0...  7.59 us
    dot_general x1, matrix products, expert_rows(): up = jnp.dot(rows, up_mat, preferred_element_type=jnp.float32)  7.46 us
    dot_general x1, matrix products, shards(): jnp.einsum('zqa,zqap->zap', sender_weights, returned_rows, preferred_elem...  7.46 us
    dot_general x1, matrix products, expert_rows(): gate = jnp.dot(rows, gate_mat, preferred_element_type=jnp.float32)  7.19 us
    all_to_all x1, starting transfers between devices, shards(): lax.all_to_all(send_weights, ('group', 'local'), split_axis=0, concat_axi...  7.14 us
  transfers between devices with their start and end apart: 3, of which 3 were waited for; matrix products, arithmetic and copies ran while one was open for 0% of the time, Pallas kernels for 0%

commit v1 on v0

--- a/solution.py
+++ b/solution.py
@@ -1,9 +1,14 @@
+import functools
+
 import jax
 import jax.numpy as jnp
 from jax import lax
+from jax.experimental import pallas as pl
+from jax.experimental.pallas import tpu as pltpu
 from jax.sharding import PartitionSpec as P
 
 GROUPS_TOK = 4
+VMEM_LIMIT = 60 * 2**20
 
 
 def expert_rows(rows, gate_mat, up_mat, down_mat):
@@ -13,7 +18,7 @@
     return jnp.dot(hidden, down_mat, preferred_element_type=jnp.float32).astype(jnp.bfloat16)
 
 
-def shards(tokens, gates, expert_ids, w_gate, w_up, w_down):
+def routed_shards(tokens, gates, expert_ids, w_gate, w_up, w_down):
     tok_rows, width = tokens.shape
     n_group = lax.axis_size("group")
     local_expert_count = lax.axis_size("local")
@@ -75,6 +80,174 @@
     return mixed.astype(jnp.bfloat16)
 
 
+def over(axis, mask):
+    pairs = [(i, i ^ mask) for i in range(4)]
+    return lambda v: lax.ppermute(v, axis, pairs)
+
+
+def expert_kernel(n_pieces, ff_tile, out_tile, me_ref, *refs):
+    pieces = refs[:n_pieces]
+    wg_hbm, wu_hbm, wd_hbm = refs[n_pieces : n_pieces + 3]
+    outs = refs[n_pieces + 3 : n_pieces + 7]
+    rows, wg, wu, wd, hidden, send, keep, sems = refs[n_pieces + 7 :]
+    ff, width = wd.shape
+    n_ff, n_out = ff // ff_tile, width // out_tile
+    n_rows = rows.shape[0]
+    block = n_rows // 8
+
+    row_copies, at = [], 0
+    for piece in pieces:
+        size = piece.shape[0]
+        row_copies.append((piece, rows.at[pl.ds(at, size)]))
+        at += size
+    ff_copies = []
+    for f in range(n_ff):
+        cols = pl.ds(f * ff_tile, ff_tile)
+        ff_copies.append((wg_hbm.at[0, :, cols], wg.at[f]))
+        ff_copies.append((wu_hbm.at[0, :, cols], wu.at[f]))
+    down_copies = [(wd_hbm.at[0], wd)]
+    loads = [
+        pltpu.make_async_copy(src, dst, sems.at[i])
+        for i, (src, dst) in enumerate(ff_copies[:2] + row_copies + ff_copies[2:] + down_copies)
+    ]
+    for load in loads:
+        load.start()
+
+    head = 2 + n_pieces
+    for load in loads[:head]:
+        load.wait()
+    table = rows[:, pl.ds(width, 128)].astype(jnp.float32)
+    lane = lax.broadcasted_iota(jnp.int32, table.shape, 1)
+    scale = jnp.sum(jnp.where(lane == me_ref[0], table, 0.0), axis=1, keepdims=True)
+    for f in range(n_ff):
+        if f:
+            loads[head + 2 * f - 2].wait()
+            loads[head + 2 * f - 1].wait()
+        x = rows[:, pl.ds(0, width)]
+        gate = jnp.dot(x, wg[f], preferred_element_type=jnp.float32)
+        up = jnp.dot(x, wu[f], preferred_element_type=jnp.float32)
+        hidden[:, pl.ds(f * ff_tile, ff_tile)] = (jax.nn.silu(gate) * up).astype(jnp.bfloat16)
+    for load in loads[head + 2 * n_ff - 2 :]:
+        load.wait()
+    stores = []
+    for n in range(n_out):
+        cols = pl.ds(n * out_tile, out_tile)
+        out = jnp.dot(hidden[...], wd[:, cols], preferred_element_type=jnp.float32) * scale
+        for stage in range(2):
+            at = 4 * stage * block
+            keep[stage, :, cols] = out[at : at + 2 * block]
+            send[stage, :, cols] = out[at + 2 * block : at + 4 * block].astype(jnp.bfloat16)
+            for src, dst in ((send, outs[stage]), (keep, outs[2 + stage])):
+                store = pltpu.make_async_copy(
+                    src.at[stage, :, cols], dst.at[:, cols], sems.at[len(loads) + len(stores)]
+                )
+                store.start()
+                stores.append(store)
+    for store in stores:
+        store.wait()
+
+
+def experts(first, second, me, w_gate, w_up, w_down):
+    pieces = [*first, *second]
+    n_rows = sum(p.shape[0] for p in pieces)
+    wide = pieces[0].shape[1]
+    _, width, ff = w_gate.shape
+    ff_tile, out_tile = ff // 3, width // 5
+    half = n_rows // 4
+    n_sems = len(pieces) + 7 + 4 * (width // out_tile)
+    hbm = pl.BlockSpec(memory_space=pltpu.HBM)
+    return pl.pallas_call(
+        functools.partial(expert_kernel, len(pieces), ff_tile, out_tile),
+        out_shape=[
+            jax.ShapeDtypeStruct((half, width), jnp.bfloat16),
+            jax.ShapeDtypeStruct((half, width), jnp.bfloat16),
+            jax.ShapeDtypeStruct((half, width), jnp.float32),
+            jax.ShapeDtypeStruct((half, width), jnp.float32),
+        ],
+        in_specs=[
+            pl.BlockSpec(memory_space=pltpu.SMEM),
+            *([hbm] * (len(pieces) + 3)),
+        ],
+        out_specs=[hbm] * 4,
+        scratch_shapes=[
+            pltpu.VMEM((n_rows, wide), jnp.bfloat16),
+            pltpu.VMEM((3, width, ff_tile), jnp.bfloat16),
+            pltpu.VMEM((3, width, ff_tile), jnp.bfloat16),
+            pltpu.VMEM((ff, width), jnp.bfloat16),
+            pltpu.VMEM((n_rows, ff), jnp.bfloat16),
+            pltpu.VMEM((2, half, width), jnp.bfloat16),
+            pltpu.VMEM((2, half, width), jnp.float32),
+            pltpu.SemaphoreType.DMA((n_sems,)),
+        ],
+        compiler_params=pltpu.CompilerParams(vmem_limit_bytes=VMEM_LIMIT),
+        cost_estimate=pl.CostEstimate(
+            flops=6 * n_rows * width * ff,
+            bytes_accessed=6 * width * ff + 5 * n_rows * width,
+            transcendentals=n_rows * ff,
+        ),
+    )(me, *pieces, w_gate, w_up, w_down)
+
+
+def after(value, *done):
+    return lax.optimization_barrier((value, *done))[0]
+
+
+def gathered_shards(tokens, gates, expert_ids, w_gate, w_up, w_down):
+    block = tokens.shape[0]
+    X, Y = over("local", 1), over("local", 2)
+    Z1, Z2 = over("group", 1), over("group", 2)
+    me = lax.axis_index("group") * 4 + lax.axis_index("local")
+
+    lanes = jnp.arange(128, dtype=jnp.int32)
+    hits = expert_ids[:, :, None] == lanes
+    weights = jnp.sum(jnp.where(hits, gates[:, :, None], jnp.bfloat16(0.0)), axis=1)
+    own = jnp.concatenate([tokens, weights], axis=1)
+
+    e1, e2 = Z1(own), Z2(own)
+    own_x, own_y = X(own), Y(own)
+    own_d = Y(own_x)
+    e3 = Z1(e2)
+    e2_x, e2_y = X(after(e2, own_x)), Y(after(e2, own_y))
+    e2_d = Y(e2_x)
+    e3_y, e3_x = Y(after(e3, e2_y)), X(after(e3, e2_x))
+    e3_d = X(e3_y)
+    e1_ = after(e1, e3_x, e2_d)
+    e1_y, e1_x = Y(e1_), X(e1_)
+    e1_d = X(e1_y)
+
+    me = me.astype(jnp.int32).reshape(1)
+    far = experts((e2, e2_x, e2_y, e2_d), (e3, e3_y, e3_x, e3_d), me, w_gate, w_up, w_down)
+    near = experts((own, own_x, own_y, own_d), (after(e1, far[0]), e1_y, e1_x, e1_d), me, w_gate, w_up, w_down)
+
+    f32 = jnp.float32
+
+    def summed(outs):
+        send_p, send_q, keep_p, keep_q = outs
+        got_p, got_q = Y(send_p), X(send_q)
+        last_p = X((keep_p[block:] + got_p[block:].astype(f32)).astype(jnp.bfloat16))
+        last_q = Y((keep_q[block:] + got_q[block:].astype(f32)).astype(jnp.bfloat16))
+        return (
+            keep_p[:block] + got_p[:block].astype(f32) + last_p.astype(f32),
+            keep_q[:block] + got_q[:block].astype(f32) + last_q.astype(f32),
+        )
+
+    r2, r3 = summed(far)
+    r2 = r2 + Z1(r3.astype(jnp.bfloat16)).astype(f32)
+    b2 = Z2(r2.astype(jnp.bfloat16))
+    r0, r1 = summed(near)
+    b1 = Z1(r1.astype(jnp.bfloat16))
+    return (r0 + b1.astype(f32) + b2.astype(f32)).astype(jnp.bfloat16)
+
+
+def shards(tokens, *rest):
+    tok_rows = tokens.shape[0]
+    n_group, n_local = lax.axis_size("group"), lax.axis_size("local")
+    capacity = min(tok_rows, tok_rows * GROUPS_TOK // n_group)
+    if capacity == tok_rows and n_group == 4 and n_local == 4:
+        return gathered_shards(tokens, *rest)
+    return routed_shards(tokens, *rest)
+
+
 def solution(mesh):
     in_specs = (
         P(("rep", "group", "local"), None),

time: 293 us -> 136 us (0.46)
  the two profiles are of different devices: /device:TPU:14 before, /device:TPU:0 now
where the time goes in v1:
time: 136 us
  waiting for transfers between devices  67.9 us (50%)
  starting transfers between devices  42.6 us (31%)
  Pallas kernels  21 us (15%)
  other arithmetic  2.7 us (2%)
  local copies, waits for them, and re-layouts  1.6 us (1%)
    ppermute x26, waiting for transfers between devices, over(): return lambda v: lax.ppermute(v, axis, pairs)  67.9 us
    ppermute x26, starting transfers between devices, over(): return lambda v: lax.ppermute(v, axis, pairs)  42.6 us
    pallas_call x2, Pallas kernels, experts(): pl.pallas_call(functools.partial(expert_kernel, len(pieces), ff_tile, out...  21 us
  transfers between devices with their start and end apart: 26, of which 13 were waited for; matrix products, arithmetic and copies ran while one was open for 0% of the time, Pallas kernels for 15%

profile of v1, /device:TPU:0, one launch (start us, length us, event | category | flops | bytes accessed | tf_op | source)
XLA Modules:
  0.0 136.0 jit_solution(11956061883328246701)
XLA Ops:
  2.8 4.1 %collective-permute-start.4 = (bf16[64,2688]{1,0:T(8,128)(2,1)S(1)}, bf16[64,2688]{1,0:T(8,128)(2,1)S(1)}, u32[]{:S(2)}, u32[]{:S(2)}) collective-permute-start(bf16[64,2688]{1,0:T(8,128)(2,1)S(1)} %pad_maximum_fusion.refs_0_), channel_id=1, source_target_pairs={{0,16},{8,24},{16,0},{24,8},{1,17},{9,25},{17,1},{25,9},{2,18},{10... | collective-permute-start | bytes 1032200 | tf_op jit(solution)/shard_map/ppermute | solution.py:85
  6.9 1.5 %collective-permute-start = (bf16[64,2688]{1,0:T(8,128)(2,1)S(1)}, bf16[64,2688]{1,0:T(8,128)(2,1)S(1)}, u32[]{:S(2)}, u32[]{:S(2)}) collective-permute-start(bf16[64,2688]{1,0:T(8,128)(2,1)S(1)} %pad_maximum_fusion.refs_0_), channel_id=1, source_target_pairs={{0,2},{2,0},{4,6},{6,4},{1,3},{3,1},{5,7},{7,5},{8,10},{10,8},{12,... | collective-permute-start | bytes 1032200 | tf_op jit(solution)/shard_map/ppermute | solution.py:85
  8.4 1.5 %collective-permute-start.1 = (bf16[64,2688]{1,0:T(8,128)(2,1)S(1)}, bf16[64,2688]{1,0:T(8,128)(2,1)S(1)}, u32[]{:S(2)}, u32[]{:S(2)}) collective-permute-start(bf16[64,2688]{1,0:T(8,128)(2,1)S(1)} %pad_maximum_fusion.refs_0_), channel_id=1, source_target_pairs={{0,4},{2,6},{4,0},{6,2},{1,5},{3,7},{5,1},{7,3},{8,12},{10,14},{12... | collective-permute-start | bytes 1032200 | tf_op jit(solution)/shard_map/ppermute | solution.py:85
  9.9 12.4 %collective-permute-done.4.refs_0_ = bf16[64,2688]{1,0:T(8,128)(2,1)S(1)} collective-permute-done((bf16[64,2688]{1,0:T(8,128)(2,1)S(1)}, bf16[64,2688]{1,0:T(8,128)(2,1)S(1)}, u32[]{:S(2)}, u32[]{:S(2)}) %collective-permute-start.4) | collective-permute-done | bytes 344096 | tf_op jit(solution)/shard_map/ppermute | solution.py:85
  22.3 1.6 %collective-permute-start.5 = (bf16[64,2688]{1,0:T(8,128)(2,1)S(1)}, bf16[64,2688]{1,0:T(8,128)(2,1)S(1)}, u32[]{:S(2)}, u32[]{:S(2)}) collective-permute-start(bf16[64,2688]{1,0:T(8,128)(2,1)S(1)} %collective-permute-done.4.refs_0_), channel_id=1, source_target_pairs={{0,2},{2,0},{4,6},{6,4},{1,3},{3,1},{5,7},{7,5},{8,10},{10,8},{12,... | collective-permute-start | bytes 1032200 | tf_op jit(solution)/shard_map/ppermute | solution.py:85
  24.5 1.5 %collective-permute-start.6 = (bf16[64,2688]{1,0:T(8,128)(2,1)S(1)}, bf16[64,2688]{1,0:T(8,128)(2,1)S(1)}, u32[]{:S(2)}, u32[]{:S(2)}) collective-permute-start(bf16[64,2688]{1,0:T(8,128)(2,1)S(1)} %collective-permute-done.4.refs_0_), channel_id=1, source_target_pairs={{0,4},{2,6},{4,0},{6,2},{1,5},{3,7},{5,1},{7,3},{8,12},{10,14},{12... | collective-permute-start | bytes 1032200 | tf_op jit(solution)/shard_map/ppermute | solution.py:85
  26.1 1.4 %collective-permute-start.3 = (bf16[64,2688]{1,0:T(8,128)(2,1)S(1)}, bf16[64,2688]{1,0:T(8,128)(2,1)S(1)}, u32[]{:S(2)}, u32[]{:S(2)}) collective-permute-start(bf16[64,2688]{1,0:T(8,128)(2,1)S(1)} %pad_maximum_fusion.refs_0_), channel_id=1, source_target_pairs={{0,8},{8,0},{16,24},{24,16},{1,9},{9,1},{17,25},{25,17},{2,10},{10... | collective-permute-start | bytes 1032200 | tf_op jit(solution)/shard_map/ppermute | solution.py:85
  27.5 4.2 %collective-permute-done.5.refs_1_ = bf16[64,2688]{1,0:T(8,128)(2,1)S(1)} collective-permute-done((bf16[64,2688]{1,0:T(8,128)(2,1)S(1)}, bf16[64,2688]{1,0:T(8,128)(2,1)S(1)}, u32[]{:S(2)}, u32[]{:S(2)}) %collective-permute-start.5) | collective-permute-done | bytes 344096 | tf_op jit(solution)/shard_map/ppermute | solution.py:85
  31.6 3.3 %collective-permute-done.8.refs_4_ = bf16[64,2688]{1,0:T(8,128)(2,1)S(1)} collective-permute-done((bf16[64,2688]{1,0:T(8,128)(2,1)S(1)}, bf16[64,2688]{1,0:T(8,128)(2,1)S(1)}, u32[]{:S(2)}, u32[]{:S(2)}) %collective-permute-start.8) | collective-permute-done | bytes 344096 | tf_op jit(solution)/shard_map/ppermute | solution.py:85
  34.9 1.5 %collective-permute-start.7 = (bf16[64,2688]{1,0:T(8,128)(2,1)S(1)}, bf16[64,2688]{1,0:T(8,128)(2,1)S(1)}, u32[]{:S(2)}, u32[]{:S(2)}) collective-permute-start(bf16[64,2688]{1,0:T(8,128)(2,1)S(1)} %collective-permute-done.5.refs_1_), channel_id=1, source_target_pairs={{0,4},{2,6},{4,0},{6,2},{1,5},{3,7},{5,1},{7,3},{8,12},{10,14},{12... | collective-permute-start | bytes 1032200 | tf_op jit(solution)/shard_map/ppermute | solution.py:85
  37.4 2.5 %collective-permute-done.3.refs_4_ = bf16[64,2688]{1,0:T(8,128)(2,1)S(1)} collective-permute-done((bf16[64,2688]{1,0:T(8,128)(2,1)S(1)}, bf16[64,2688]{1,0:T(8,128)(2,1)S(1)}, u32[]{:S(2)}, u32[]{:S(2)}) %collective-permute-start.3) | collective-permute-done | bytes 344096 | tf_op jit(solution)/shard_map/ppermute | solution.py:85
  40.0 6.0 %collective-permute-done.7.refs_3_ = bf16[64,2688]{1,0:T(8,128)(2,1)S(1)} collective-permute-done((bf16[64,2688]{1,0:T(8,128)(2,1)S(1)}, bf16[64,2688]{1,0:T(8,128)(2,1)S(1)}, u32[]{:S(2)}, u32[]{:S(2)}) %collective-permute-start.7) | collective-permute-done | bytes 344096 | tf_op jit(solution)/shard_map/ppermute | solution.py:85
  45.9 1.6 %collective-permute-start.12 = (bf16[64,2688]{1,0:T(8,128)(2,1)S(1)}, bf16[64,2688]{1,0:T(8,128)(2,1)}, u32[]{:S(2)}, u32[]{:S(2)}) collective-permute-start(bf16[64,2688]{1,0:T(8,128)(2,1)S(1)} %collective-permute-done.3.refs_4_), channel_id=1, source_target_pairs={{0,4},{2,6},{4,0},{6,2},{1,5},{3,7},{5,1},{7,3},{8,12},{10,14},{12... | collective-permute-start | bytes 1032200 | tf_op jit(solution)/shard_map/ppermute | solution.py:85
  47.5 5.9 %collective-permute-done.9.refs_5_ = bf16[64,2688]{1,0:T(8,128)(2,1)} collective-permute-done((bf16[64,2688]{1,0:T(8,128)(2,1)S(1)}, bf16[64,2688]{1,0:T(8,128)(2,1)}, u32[]{:S(2)}, u32[]{:S(2)}) %collective-permute-start.9) | collective-permute-done | bytes 344096 | tf_op jit(solution)/shard_map/ppermute | solution.py:85
  53.9 1.6 %collective-permute-start.2 = (bf16[64,2688]{1,0:T(8,128)(2,1)S(1)}, bf16[64,2688]{1,0:T(8,128)(2,1)}, u32[]{:S(2)}, u32[]{:S(2)}) collective-permute-start(bf16[64,2688]{1,0:T(8,128)(2,1)S(1)} %collective-permute-done.refs_1_), channel_id=1, source_target_pairs={{0,4},{2,6},{4,0},{6,2},{1,5},{3,7},{5,1},{7,3},{8,12},{10,14},{12... | collective-permute-start | bytes 1032200 | tf_op jit(solution)/shard_map/ppermute | solution.py:85
  55.5 1.5 %collective-permute-start.13 = (bf16[64,2688]{1,0:T(8,128)(2,1)S(1)}, bf16[64,2688]{1,0:T(8,128)(2,1)}, u32[]{:S(2)}, u32[]{:S(2)}) collective-permute-start(bf16[64,2688]{1,0:T(8,128)(2,1)S(1)} %collective-permute-done.3.refs_4_), channel_id=1, source_target_pairs={{0,2},{2,0},{4,6},{6,4},{1,3},{3,1},{5,7},{7,5},{8,10},{10,8},{12,... | collective-permute-start | bytes 1032200 | tf_op jit(solution)/shard_map/ppermute | solution.py:85
  57.0 2.9 %collective-permute-done.12.refs_5_ = bf16[64,2688]{1,0:T(8,128)(2,1)} collective-permute-done((bf16[64,2688]{1,0:T(8,128)(2,1)S(1)}, bf16[64,2688]{1,0:T(8,128)(2,1)}, u32[]{:S(2)}, u32[]{:S(2)}) %collective-permute-start.12) | collective-permute-done | bytes 344096 | tf_op jit(solution)/shard_map/ppermute | solution.py:85
  60.4 1.6 %collective-permute-done.11.refs_7_ = bf16[64,2688]{1,0:T(8,128)(2,1)} collective-permute-done((bf16[64,2688]{1,0:T(8,128)(2,1)}, bf16[64,2688]{1,0:T(8,128)(2,1)}, u32[]{:S(2)}, u32[]{:S(2)}) %collective-permute-start.11) | collective-permute-done | bytes 344096 | tf_op jit(solution)/shard_map/ppermute | solution.py:85
  62.0 10.6 %shard_map.64 = (bf16[128,2560]{1,0:T(8,128)(2,1)}, bf16[128,2560]{1,0:T(8,128)(2,1)}, f32[128,2560]{1,0:T(8,128)}, f32[128,2560]{1,0:T(8,128)}) custom-call(s32[1]{0:T(128)} %bitcast.me_ref, bf16[64,2688]{1,0:T(8,128)(2,1)} %copy-done.7, bf16[64,2688]{1,0:T(8,128)(2,1)} %copy-done.9, bf16[64,2688]{1,0:T(8,128)(2,1)} %copy-done.11, ...), custom_call_target="tpu_custom_call" | custom-call | flops 6039797760 | bytes 18350080 | tf_op jit(solution)/shard_map/pallas_call | solution.py:159
  73.3 1.5 %collective-permute-start.20 = (bf16[128,2560]{1,0:T(8,128)(2,1)}, bf16[128,2560]{1,0:T(8,128)(2,1)S(1)}, u32[]{:S(2)}, u32[]{:S(2)}) collective-permute-start(bf16[128,2560]{1,0:T(8,128)(2,1)} %get-tuple-element.23), channel_id=1, source_target_pairs={{0,4},{2,6},{4,0},{6,2},{1,5},{3,7},{5,1},{7,3},{8,12},{10,14},{12... | collective-permute-start | bytes 1966088 | tf_op jit(solution)/shard_map/ppermute | solution.py:85
  74.8 10.5 %shard_map.65 = (bf16[128,2560]{1,0:T(8,128)(2,1)}, bf16[128,2560]{1,0:T(8,128)(2,1)}, f32[128,2560]{1,0:T(8,128)}, f32[128,2560]{1,0:T(8,128)}) custom-call(s32[1]{0:T(128)} %bitcast.me_ref, bf16[64,2688]{1,0:T(8,128)(2,1)} %copy-done.4, bf16[64,2688]{1,0:T(8,128)(2,1)} %copy-done.5, bf16[64,2688]{1,0:T(8,128)(2,1)} %copy-done.6, ...), custom_call_target="tpu_custom_call" | custom-call | flops 6039797760 | bytes 18350080 | tf_op jit(solution)/shard_map/pallas_call | solution.py:159
  85.3 1.6 %collective-permute-start.17 = (bf16[128,2560]{1,0:T(8,128)(2,1)}, bf16[128,2560]{1,0:T(8,128)(2,1)S(1)}, u32[]{:S(2)}, u32[]{:S(2)}) collective-permute-start(bf16[128,2560]{1,0:T(8,128)(2,1)} %get-tuple-element.29), channel_id=1, source_target_pairs={{0,2},{2,0},{4,6},{6,4},{1,3},{3,1},{5,7},{7,5},{8,10},{10,8},{12,... | collective-permute-start | bytes 1966088 | tf_op jit(solution)/shard_map/ppermute | solution.py:85
  87.3 1.1 collective-permute-done.22
  88.5 2.5 %collective-permute-start.23 = (bf16[64,2560]{1,0:T(8,128)(2,1)S(1)}, bf16[64,2560]{1,0:T(8,128)(2,1)S(1)}, u32[]{:S(2)}, u32[]{:S(2)}) collective-permute-start(bf16[64,2560]{1,0:T(8,128)(2,1)S(1)} %add_convert_fusion.3), channel_id=1, source_target_pairs={{0,4},{2,6},{4,0},{6,2},{1,5},{3,7},{5,1},{7,3},{8,12},{10,14},{12... | collective-permute-start | bytes 983048 | tf_op jit(solution)/shard_map/ppermute | solution.py:85
  91.7 14.0 %collective-permute-done.23 = bf16[64,2560]{1,0:T(8,128)(2,1)S(1)} collective-permute-done((bf16[64,2560]{1,0:T(8,128)(2,1)S(1)}, bf16[64,2560]{1,0:T(8,128)(2,1)S(1)}, u32[]{:S(2)}, u32[]{:S(2)}) %collective-permute-start.23) | collective-permute-done | bytes 327712 | tf_op jit(solution)/shard_map/ppermute | solution.py:85
  105.7 5.9 %collective-permute-start.24 = (bf16[64,2560]{1,0:T(8,128)(2,1)S(1)}, bf16[64,2560]{1,0:T(8,128)(2,1)S(1)}, u32[]{:S(2)}, u32[]{:S(2)}) collective-permute-start(bf16[64,2560]{1,0:T(8,128)(2,1)S(1)} %add_convert_fusion.2), channel_id=1, source_target_pairs={{0,8},{8,0},{16,24},{24,16},{1,9},{9,1},{17,25},{25,17},{2,10},{10... | collective-permute-start | bytes 983048 | tf_op jit(solution)/shard_map/ppermute | solution.py:85
  111.7 1.4 %collective-permute-start.18 = (bf16[64,2560]{1,0:T(8,128)(2,1)S(1)}, bf16[64,2560]{1,0:T(8,128)(2,1)S(1)}, u32[]{:S(2)}, u32[]{:S(2)}) collective-permute-start(bf16[64,2560]{1,0:T(8,128)(2,1)S(1)} %add_convert_fusion.6), channel_id=1, source_target_pairs={{0,4},{2,6},{4,0},{6,2},{1,5},{3,7},{5,1},{7,3},{8,12},{10,14},{12... | collective-permute-start | bytes 983048 | tf_op jit(solution)/shard_map/ppermute | solution.py:85
  113.2 1.3 collective-permute-start.16
  114.5 7.5 %collective-permute-done.24 = bf16[64,2560]{1,0:T(8,128)(2,1)S(1)} collective-permute-done((bf16[64,2560]{1,0:T(8,128)(2,1)S(1)}, bf16[64,2560]{1,0:T(8,128)(2,1)S(1)}, u32[]{:S(2)}, u32[]{:S(2)}) %collective-permute-start.24) | collective-permute-done | bytes 327712 | tf_op jit(solution)/shard_map/ppermute | solution.py:85
  122.2 3.7 %collective-permute-start.25 = (bf16[64,2560]{1,0:T(8,128)(2,1)S(1)}, bf16[64,2560]{1,0:T(8,128)(2,1)S(1)}, u32[]{:S(2)}, u32[]{:S(2)}) collective-permute-start(bf16[64,2560]{1,0:T(8,128)(2,1)S(1)} %add_convert_fusion.1), channel_id=1, source_target_pairs={{0,16},{8,24},{16,0},{24,8},{1,17},{9,25},{17,1},{25,9},{2,18},{10... | collective-permute-start | bytes 983048 | tf_op jit(solution)/shard_map/ppermute | solution.py:85
  126.0 2.5 %collective-permute-start.19 = (bf16[64,2560]{1,0:T(8,128)(2,1)S(1)}, bf16[64,2560]{1,0:T(8,128)(2,1)S(1)}, u32[]{:S(2)}, u32[]{:S(2)}) collective-permute-start(bf16[64,2560]{1,0:T(8,128)(2,1)S(1)} %add_convert_fusion.5), channel_id=1, source_target_pairs={{0,8},{8,0},{16,24},{24,16},{1,9},{9,1},{17,25},{25,17},{2,10},{10... | collective-permute-start | bytes 983048 | tf_op jit(solution)/shard_map/ppermute | solution.py:85
  128.6 6.0 %collective-permute-done.25 = bf16[64,2560]{1,0:T(8,128)(2,1)S(1)} collective-permute-done((bf16[64,2560]{1,0:T(8,128)(2,1)S(1)}, bf16[64,2560]{1,0:T(8,128)(2,1)S(1)}, u32[]{:S(2)}, u32[]{:S(2)}) %collective-permute-start.25) | collective-permute-done | bytes 327712 | tf_op jit(solution)/shard_map/ppermute | solution.py:85
  (62 shorter events, 9.2 us)
Async XLA Ops:
  2.8 69.8 %copy-start.4 = (bf16[64,2688]{1,0:T(8,128)(2,1)}, bf16[64,2688]{1,0:T(8,128)(2,1)S(1)}, u32[]{:S(2)}) copy-start(bf16[64,2688]{1,0:T(8,128)(2,1)S(1)} %pad_maximum_fusion.refs_0_) | copy-start | bytes 1032196
  2.8 19.5 %collective-permute-start.4 = (bf16[64,2688]{1,0:T(8,128)(2,1)S(1)}, bf16[64,2688]{1,0:T(8,128)(2,1)S(1)}, u32[]{:S(2)}, u32[]{:S(2)}) collective-permute-start(bf16[64,2688]{1,0:T(8,128)(2,1)S(1)} %pad_maximum_fusion.refs_0_), channel_id=1, source_target_pairs={{0,16},{8,24},{16,0},{24,8},{1,17},{9,25},{17,1},{25,9},{2,18},{10... | collective-permute-start | bytes 1032200 | tf_op jit(solution)/shard_map/ppermute | solution.py:85
  6.9 15.4 %collective-permute-start = (bf16[64,2688]{1,0:T(8,128)(2,1)S(1)}, bf16[64,2688]{1,0:T(8,128)(2,1)S(1)}, u32[]{:S(2)}, u32[]{:S(2)}) collective-permute-start(bf16[64,2688]{1,0:T(8,128)(2,1)S(1)} %pad_maximum_fusion.refs_0_), channel_id=1, source_target_pairs={{0,2},{2,0},{4,6},{6,4},{1,3},{3,1},{5,7},{7,5},{8,10},{10,8},{12,... | collective-permute-start | bytes 1032200 | tf_op jit(solution)/shard_map/ppermute | solution.py:85
  8.4 16.2 %collective-permute-start.1 = (bf16[64,2688]{1,0:T(8,128)(2,1)S(1)}, bf16[64,2688]{1,0:T(8,128)(2,1)S(1)}, u32[]{:S(2)}, u32[]{:S(2)}) collective-permute-start(bf16[64,2688]{1,0:T(8,128)(2,1)S(1)} %pad_maximum_fusion.refs_0_), channel_id=1, source_target_pairs={{0,4},{2,6},{4,0},{6,2},{1,5},{3,7},{5,1},{7,3},{8,12},{10,14},{12... | collective-permute-start | bytes 1032200 | tf_op jit(solution)/shard_map/ppermute | solution.py:85
  22.3 39.7 %copy-start.7 = (bf16[64,2688]{1,0:T(8,128)(2,1)}, bf16[64,2688]{1,0:T(8,128)(2,1)S(1)}, u32[]{:S(2)}) copy-start(bf16[64,2688]{1,0:T(8,128)(2,1)S(1)} %collective-permute-done.4.refs_0_) | copy-start | bytes 1032196
  22.3 50.3 %copy-start.5 = (bf16[64,2688]{1,0:T(8,128)(2,1)}, bf16[64,2688]{1,0:T(8,128)(2,1)S(1)}, u32[]{:S(2)}) copy-start(bf16[64,2688]{1,0:T(8,128)(2,1)S(1)} %collective-permute-done.refs_1_) | copy-start | bytes 1032196
  22.3 9.3 %collective-permute-start.5 = (bf16[64,2688]{1,0:T(8,128)(2,1)S(1)}, bf16[64,2688]{1,0:T(8,128)(2,1)S(1)}, u32[]{:S(2)}, u32[]{:S(2)}) collective-permute-start(bf16[64,2688]{1,0:T(8,128)(2,1)S(1)} %collective-permute-done.4.refs_0_), channel_id=1, source_target_pairs={{0,2},{2,0},{4,6},{6,4},{1,3},{3,1},{5,7},{7,5},{8,10},{10,8},{12,... | collective-permute-start | bytes 1032200 | tf_op jit(solution)/shard_map/ppermute | solution.py:85
  23.9 11.0 %collective-permute-start.8 = (bf16[64,2688]{1,0:T(8,128)(2,1)S(1)}, bf16[64,2688]{1,0:T(8,128)(2,1)S(1)}, u32[]{:S(2)}, u32[]{:S(2)}) collective-permute-start(bf16[64,2688]{1,0:T(8,128)(2,1)S(1)} %collective-permute-done.4.refs_0_), channel_id=1, source_target_pairs={{0,8},{8,0},{16,24},{24,16},{1,9},{9,1},{17,25},{25,17},{2,10},{10... | collective-permute-start | bytes 1032200 | tf_op jit(solution)/shard_map/ppermute | solution.py:85
  24.5 48.1 %copy-start.6 = (bf16[64,2688]{1,0:T(8,128)(2,1)}, bf16[64,2688]{1,0:T(8,128)(2,1)S(1)}, u32[]{:S(2)}) copy-start(bf16[64,2688]{1,0:T(8,128)(2,1)S(1)} %collective-permute-done.1.refs_2_) | copy-start | bytes 1032196
  24.5 12.4 %collective-permute-start.6 = (bf16[64,2688]{1,0:T(8,128)(2,1)S(1)}, bf16[64,2688]{1,0:T(8,128)(2,1)S(1)}, u32[]{:S(2)}, u32[]{:S(2)}) collective-permute-start(bf16[64,2688]{1,0:T(8,128)(2,1)S(1)} %collective-permute-done.4.refs_0_), channel_id=1, source_target_pairs={{0,4},{2,6},{4,0},{6,2},{1,5},{3,7},{5,1},{7,3},{8,12},{10,14},{12... | collective-permute-start | bytes 1032200 | tf_op jit(solution)/shard_map/ppermute | solution.py:85
  26.1 13.9 %collective-permute-start.3 = (bf16[64,2688]{1,0:T(8,128)(2,1)S(1)}, bf16[64,2688]{1,0:T(8,128)(2,1)S(1)}, u32[]{:S(2)}, u32[]{:S(2)}) collective-permute-start(bf16[64,2688]{1,0:T(8,128)(2,1)S(1)} %pad_maximum_fusion.refs_0_), channel_id=1, source_target_pairs={{0,8},{8,0},{16,24},{24,16},{1,9},{9,1},{17,25},{25,17},{2,10},{10... | collective-permute-start | bytes 1032200 | tf_op jit(solution)/shard_map/ppermute | solution.py:85
  31.6 30.4 %copy-start.9 = (bf16[64,2688]{1,0:T(8,128)(2,1)}, bf16[64,2688]{1,0:T(8,128)(2,1)S(1)}, u32[]{:S(2)}) copy-start(bf16[64,2688]{1,0:T(8,128)(2,1)S(1)} %collective-permute-done.5.refs_1_) | copy-start | bytes 1032196
  34.9 11.0 %collective-permute-start.7 = (bf16[64,2688]{1,0:T(8,128)(2,1)S(1)}, bf16[64,2688]{1,0:T(8,128)(2,1)S(1)}, u32[]{:S(2)}, u32[]{:S(2)}) collective-permute-start(bf16[64,2688]{1,0:T(8,128)(2,1)S(1)} %collective-permute-done.5.refs_1_), channel_id=1, source_target_pairs={{0,4},{2,6},{4,0},{6,2},{1,5},{3,7},{5,1},{7,3},{8,12},{10,14},{12... | collective-permute-start | bytes 1032200 | tf_op jit(solution)/shard_map/ppermute | solution.py:85
  36.4 9.5 %collective-permute-start.10 = (bf16[64,2688]{1,0:T(8,128)(2,1)S(1)}, bf16[64,2688]{1,0:T(8,128)(2,1)S(1)}, u32[]{:S(2)}, u32[]{:S(2)}) collective-permute-start(bf16[64,2688]{1,0:T(8,128)(2,1)S(1)} %collective-permute-done.8.refs_4_), channel_id=1, source_target_pairs={{0,2},{2,0},{4,6},{6,4},{1,3},{3,1},{5,7},{7,5},{8,10},{10,8},{12,... | collective-permute-start | bytes 1032200 | tf_op jit(solution)/shard_map/ppermute | solution.py:85
  37.0 16.4 %collective-permute-start.9 = (bf16[64,2688]{1,0:T(8,128)(2,1)S(1)}, bf16[64,2688]{1,0:T(8,128)(2,1)}, u32[]{:S(2)}, u32[]{:S(2)}) collective-permute-start(bf16[64,2688]{1,0:T(8,128)(2,1)S(1)} %collective-permute-done.8.refs_4_), channel_id=1, source_target_pairs={{0,4},{2,6},{4,0},{6,2},{1,5},{3,7},{5,1},{7,3},{8,12},{10,14},{12... | collective-permute-start | bytes 1032200 | tf_op jit(solution)/shard_map/ppermute | solution.py:85
  40.0 32.7 %copy-start.8 = (bf16[64,2688]{1,0:T(8,128)(2,1)}, bf16[64,2688]{1,0:T(8,128)(2,1)S(1)}, u32[]{:S(2)}) copy-start(bf16[64,2688]{1,0:T(8,128)(2,1)S(1)} %collective-permute-done.3.refs_4_) | copy-start | bytes 1032196
  45.9 13.9 %collective-permute-start.12 = (bf16[64,2688]{1,0:T(8,128)(2,1)S(1)}, bf16[64,2688]{1,0:T(8,128)(2,1)}, u32[]{:S(2)}, u32[]{:S(2)}) collective-permute-start(bf16[64,2688]{1,0:T(8,128)(2,1)S(1)} %collective-permute-done.3.refs_4_), channel_id=1, source_target_pairs={{0,4},{2,6},{4,0},{6,2},{1,5},{3,7},{5,1},{7,3},{8,12},{10,14},{12... | collective-permute-start | bytes 1032200 | tf_op jit(solution)/shard_map/ppermute | solution.py:85
  53.4 8.6 %collective-permute-start.11 = (bf16[64,2688]{1,0:T(8,128)(2,1)}, bf16[64,2688]{1,0:T(8,128)(2,1)}, u32[]{:S(2)}, u32[]{:S(2)}) collective-permute-start(bf16[64,2688]{1,0:T(8,128)(2,1)} %collective-permute-done.9.refs_5_), channel_id=1, source_target_pairs={{0,2},{2,0},{4,6},{6,4},{1,3},{3,1},{5,7},{7,5},{8,10},{10,8},{12,... | collective-permute-start | bytes 1032200 | tf_op jit(solution)/shard_map/ppermute | solution.py:85
  53.9 20.9 %collective-permute-start.2 = (bf16[64,2688]{1,0:T(8,128)(2,1)S(1)}, bf16[64,2688]{1,0:T(8,128)(2,1)}, u32[]{:S(2)}, u32[]{:S(2)}) collective-permute-start(bf16[64,2688]{1,0:T(8,128)(2,1)S(1)} %collective-permute-done.refs_1_), channel_id=1, source_target_pairs={{0,4},{2,6},{4,0},{6,2},{1,5},{3,7},{5,1},{7,3},{8,12},{10,14},{12... | collective-permute-start | bytes 1032200 | tf_op jit(solution)/shard_map/ppermute | solution.py:85
  55.5 19.3 %collective-permute-start.13 = (bf16[64,2688]{1,0:T(8,128)(2,1)S(1)}, bf16[64,2688]{1,0:T(8,128)(2,1)}, u32[]{:S(2)}, u32[]{:S(2)}) collective-permute-start(bf16[64,2688]{1,0:T(8,128)(2,1)S(1)} %collective-permute-done.3.refs_4_), channel_id=1, source_target_pairs={{0,2},{2,0},{4,6},{6,4},{1,3},{3,1},{5,7},{7,5},{8,10},{10,8},{12,... | collective-permute-start | bytes 1032200 | tf_op jit(solution)/shard_map/ppermute | solution.py:85
  59.9 14.9 %collective-permute-start.14 = (bf16[64,2688]{1,0:T(8,128)(2,1)}, bf16[64,2688]{1,0:T(8,128)(2,1)}, u32[]{:S(2)}, u32[]{:S(2)}) collective-permute-start(bf16[64,2688]{1,0:T(8,128)(2,1)} %collective-permute-done.12.refs_5_), channel_id=1, source_target_pairs={{0,2},{2,0},{4,6},{6,4},{1,3},{3,1},{5,7},{7,5},{8,10},{10,8},{12,... | collective-permute-start | bytes 1032200 | tf_op jit(solution)/shard_map/ppermute | solution.py:85
  72.6 15.8 %collective-permute-start.22 = (bf16[128,2560]{1,0:T(8,128)(2,1)}, bf16[128,2560]{1,0:T(8,128)(2,1)S(1)}, u32[]{:S(2)}, u32[]{:S(2)}) collective-permute-start(bf16[128,2560]{1,0:T(8,128)(2,1)} %get-tuple-element.32), channel_id=1, source_target_pairs={{0,2},{2,0},{4,6},{6,4},{1,3},{3,1},{5,7},{7,5},{8,10},{10,8},{12,... | collective-permute-start | bytes 1966088 | tf_op jit(solution)/shard_map/ppermute | solution.py:85
  73.3 17.7 %collective-permute-start.20 = (bf16[128,2560]{1,0:T(8,128)(2,1)}, bf16[128,2560]{1,0:T(8,128)(2,1)S(1)}, u32[]{:S(2)}, u32[]{:S(2)}) collective-permute-start(bf16[128,2560]{1,0:T(8,128)(2,1)} %get-tuple-element.23), channel_id=1, source_target_pairs={{0,4},{2,6},{4,0},{6,2},{1,5},{3,7},{5,1},{7,3},{8,12},{10,14},{12... | collective-permute-start | bytes 1966088 | tf_op jit(solution)/shard_map/ppermute | solution.py:85
  85.3 26.4 %collective-permute-start.17 = (bf16[128,2560]{1,0:T(8,128)(2,1)}, bf16[128,2560]{1,0:T(8,128)(2,1)S(1)}, u32[]{:S(2)}, u32[]{:S(2)}) collective-permute-start(bf16[128,2560]{1,0:T(8,128)(2,1)} %get-tuple-element.29), channel_id=1, source_target_pairs={{0,2},{2,0},{4,6},{6,4},{1,3},{3,1},{5,7},{7,5},{8,10},{10,8},{12,... | collective-permute-start | bytes 1966088 | tf_op jit(solution)/shard_map/ppermute | solution.py:85
  86.8 26.3 %collective-permute-start.15 = (bf16[128,2560]{1,0:T(8,128)(2,1)}, bf16[128,2560]{1,0:T(8,128)(2,1)S(1)}, u32[]{:S(2)}, u32[]{:S(2)}) collective-permute-start(bf16[128,2560]{1,0:T(8,128)(2,1)} %get-tuple-element.27), channel_id=1, source_target_pairs={{0,4},{2,6},{4,0},{6,2},{1,5},{3,7},{5,1},{7,3},{8,12},{10,14},{12... | collective-permute-start | bytes 1966088 | tf_op jit(solution)/shard_map/ppermute | solution.py:85
  88.5 17.1 %collective-permute-start.23 = (bf16[64,2560]{1,0:T(8,128)(2,1)S(1)}, bf16[64,2560]{1,0:T(8,128)(2,1)S(1)}, u32[]{:S(2)}, u32[]{:S(2)}) collective-permute-start(bf16[64,2560]{1,0:T(8,128)(2,1)S(1)} %add_convert_fusion.3), channel_id=1, source_target_pairs={{0,4},{2,6},{4,0},{6,2},{1,5},{3,7},{5,1},{7,3},{8,12},{10,14},{12... | collective-permute-start | bytes 983048 | tf_op jit(solution)/shard_map/ppermute | solution.py:85
  91.1 23.4 %collective-permute-start.21 = (bf16[64,2560]{1,0:T(8,128)(2,1)S(1)}, bf16[64,2560]{1,0:T(8,128)(2,1)S(1)}, u32[]{:S(2)}, u32[]{:S(2)}) collective-permute-start(bf16[64,2560]{1,0:T(8,128)(2,1)S(1)} %add_convert_fusion.4), channel_id=1, source_target_pairs={{0,2},{2,0},{4,6},{6,4},{1,3},{3,1},{5,7},{7,5},{8,10},{10,8},{12,... | collective-permute-start | bytes 983048 | tf_op jit(solution)/shard_map/ppermute | solution.py:85
  105.7 16.3 %collective-permute-start.24 = (bf16[64,2560]{1,0:T(8,128)(2,1)S(1)}, bf16[64,2560]{1,0:T(8,128)(2,1)S(1)}, u32[]{:S(2)}, u32[]{:S(2)}) collective-permute-start(bf16[64,2560]{1,0:T(8,128)(2,1)S(1)} %add_convert_fusion.2), channel_id=1, source_target_pairs={{0,8},{8,0},{16,24},{24,16},{1,9},{9,1},{17,25},{25,17},{2,10},{10... | collective-permute-start | bytes 983048 | tf_op jit(solution)/shard_map/ppermute | solution.py:85
  111.7 14.2 %collective-permute-start.18 = (bf16[64,2560]{1,0:T(8,128)(2,1)S(1)}, bf16[64,2560]{1,0:T(8,128)(2,1)S(1)}, u32[]{:S(2)}, u32[]{:S(2)}) collective-permute-start(bf16[64,2560]{1,0:T(8,128)(2,1)S(1)} %add_convert_fusion.6), channel_id=1, source_target_pairs={{0,4},{2,6},{4,0},{6,2},{1,5},{3,7},{5,1},{7,3},{8,12},{10,14},{12... | collective-permute-start | bytes 983048 | tf_op jit(solution)/shard_map/ppermute | solution.py:85
  113.2 15.4 %collective-permute-start.16 = (bf16[64,2560]{1,0:T(8,128)(2,1)S(1)}, bf16[64,2560]{1,0:T(8,128)(2,1)S(1)}, u32[]{:S(2)}, u32[]{:S(2)}) collective-permute-start(bf16[64,2560]{1,0:T(8,128)(2,1)S(1)} %add_convert_fusion.7), channel_id=1, source_target_pairs={{0,2},{2,0},{4,6},{6,4},{1,3},{3,1},{5,7},{7,5},{8,10},{10,8},{12,... | collective-permute-start | bytes 983048 | tf_op jit(solution)/shard_map/ppermute | solution.py:85
  122.2 12.4 %collective-permute-start.25 = (bf16[64,2560]{1,0:T(8,128)(2,1)S(1)}, bf16[64,2560]{1,0:T(8,128)(2,1)S(1)}, u32[]{:S(2)}, u32[]{:S(2)}) collective-permute-start(bf16[64,2560]{1,0:T(8,128)(2,1)S(1)} %add_convert_fusion.1), channel_id=1, source_target_pairs={{0,16},{8,24},{16,0},{24,8},{1,17},{9,25},{17,1},{25,9},{2,18},{10... | collective-permute-start | bytes 983048 | tf_op jit(solution)/shard_map/ppermute | solution.py:85
  126.0 9.1 %collective-permute-start.19 = (bf16[64,2560]{1,0:T(8,128)(2,1)S(1)}, bf16[64,2560]{1,0:T(8,128)(2,1)S(1)}, u32[]{:S(2)}, u32[]{:S(2)}) collective-permute-start(bf16[64,2560]{1,0:T(8,128)(2,1)S(1)} %add_convert_fusion.5), channel_id=1, source_target_pairs={{0,8},{8,0},{16,24},{24,16},{1,9},{9,1},{17,25},{25,17},{2,10},{10... | collective-permute-start | bytes 983048 | tf_op jit(solution)/shard_map/ppermute | solution.py:85
  (8 other events, 139.3 us)

commit v2 on v0

--- a/solution.py
+++ b/solution.py
@@ -1,9 +1,14 @@
+import functools
+
 import jax
 import jax.numpy as jnp
 from jax import lax
+from jax.experimental import pallas as pl
+from jax.experimental.pallas import tpu as pltpu
 from jax.sharding import PartitionSpec as P
 
 GROUPS_TOK = 4
+VMEM_LIMIT = 16 * 2**20
 
 
 def expert_rows(rows, gate_mat, up_mat, down_mat):
@@ -13,7 +18,7 @@
     return jnp.dot(hidden, down_mat, preferred_element_type=jnp.float32).astype(jnp.bfloat16)
 
 
-def shards(tokens, gates, expert_ids, w_gate, w_up, w_down):
+def routed_shards(tokens, gates, expert_ids, w_gate, w_up, w_down):
     tok_rows, width = tokens.shape
     n_group = lax.axis_size("group")
     local_expert_count = lax.axis_size("local")
@@ -75,6 +80,168 @@
     return mixed.astype(jnp.bfloat16)
 
 
+def over(axis, mask):
+    pairs = [(i, i ^ mask) for i in range(4)]
+    return lambda v: lax.ppermute(v, axis, pairs)
+
+
+def expert_kernel(n_pieces, ff_tile, out_tile, me_ref, *refs, loads=()):
+    pieces = refs[:n_pieces]
+    wg, wu, wd = refs[n_pieces : n_pieces + 3]
+    *outs, hidden = refs[n_pieces + 3 :]
+    _, ff, width = wd.shape
+
+    table = jnp.concatenate([p[:, pl.ds(width, 128)] for p in pieces], axis=0).astype(jnp.float32)
+    lane = lax.broadcasted_iota(jnp.int32, table.shape, 1)
+    scale = jnp.sum(jnp.where(lane == me_ref[0], table, 0.0), axis=1, keepdims=True)
+    for f in range(ff // ff_tile):
+        cols = pl.ds(f * ff_tile, ff_tile)
+        for load in loads[2 * f : 2 * f + 2]:
+            load.wait()
+        x = jnp.concatenate([p[:, pl.ds(0, width)] for p in pieces], axis=0)
+        gate = jnp.dot(x, wg[0, :, cols], preferred_element_type=jnp.float32)
+        up = jnp.dot(x, wu[0, :, cols], preferred_element_type=jnp.float32)
+        hidden[:, cols] = (jax.nn.silu(gate) * up).astype(jnp.bfloat16)
+    for load in loads[2 * (ff // ff_tile) :]:
+        load.wait()
+    for n in range(width // out_tile):
+        cols = pl.ds(n * out_tile, out_tile)
+        out = jnp.dot(hidden[...], wd[0, :, cols], preferred_element_type=jnp.float32) * scale
+        at = 0
+        for buf in outs:
+            size = buf.shape[0]
+            buf[:, cols] = out[at : at + size].astype(buf.dtype)
+            at += size
+
+
+def first_kernel(n_pieces, ff_tile, out_tile, me_ref, *refs):
+    weights_hbm = refs[n_pieces : n_pieces + 3]
+    weights = refs[n_pieces + 3 : n_pieces + 6]
+    load_sems = refs[-1]
+    ff = weights[0].shape[2]
+    loads, pairs = [], []
+    for f in range(ff // ff_tile):
+        cols = pl.ds(f * ff_tile, ff_tile)
+        pairs += [(w_hbm.at[0, :, cols], w.at[0, :, cols]) for w_hbm, w in zip(weights_hbm[:2], weights[:2])]
+    pairs.append((weights_hbm[2], weights[2]))
+    for i, (src, dst) in enumerate(pairs):
+        loads.append(pltpu.make_async_copy(src, dst, load_sems.at[i]))
+        loads[-1].start()
+    expert_kernel(
+        n_pieces, ff_tile, out_tile, me_ref, *refs[:n_pieces], *weights, *refs[n_pieces + 6 : -1], loads=loads
+    )
+
+
+def experts(pieces, outs, me, weights, first=False):
+    n_rows = sum(p.shape[0] for p in pieces)
+    _, width, ff = weights[0].shape
+    ff_tile, out_tile = ff // 3, width // 5
+    vmem = pl.BlockSpec(memory_space=pltpu.VMEM)
+    if first:
+        weights = [pltpu.with_memory_space_constraint(w, pltpu.HBM) for w in weights]
+    return pl.pallas_call(
+        functools.partial(first_kernel if first else expert_kernel, len(pieces), ff_tile, out_tile),
+        out_shape=[
+            *(pltpu.VMEM(w.shape, w.dtype) for w in weights if first),
+            *(pltpu.VMEM((rows, width), dtype) for rows, dtype in outs),
+        ],
+        in_specs=[
+            pl.BlockSpec(memory_space=pltpu.SMEM),
+            *([vmem] * len(pieces)),
+            *([pl.BlockSpec(memory_space=pltpu.HBM) if first else vmem] * 3),
+        ],
+        out_specs=[vmem] * (len(outs) + 3 * first),
+        scratch_shapes=[
+            pltpu.VMEM((n_rows, ff), jnp.bfloat16),
+            *([pltpu.SemaphoreType.DMA((7,))] if first else []),
+        ],
+        compiler_params=pltpu.CompilerParams(vmem_limit_bytes=VMEM_LIMIT),
+        cost_estimate=pl.CostEstimate(
+            flops=6 * n_rows * width * ff,
+            bytes_accessed=8 * n_rows * width,
+            transcendentals=n_rows * ff,
+        ),
+    )(me, *pieces, *weights)
+
+
+def after(value, *done):
+    return lax.optimization_barrier((value, *done))[0]
+
+
+def gathered_shards(tokens, gates, expert_ids, w_gate, w_up, w_down):
+    block = tokens.shape[0]
+    X, Y = over("local", 1), over("local", 2)
+    Z1, Z2 = over("group", 1), over("group", 2)
+    me = lax.axis_index("group") * 4 + lax.axis_index("local")
+
+    lanes = jnp.arange(128, dtype=jnp.int32)
+    hits = expert_ids[:, :, None] == lanes
+    weights = jnp.sum(jnp.where(hits, gates[:, :, None], jnp.bfloat16(0.0)), axis=1)
+    own = jnp.concatenate([tokens, weights], axis=1)
+
+    half = block // 2
+    f32, bf16 = jnp.float32, jnp.bfloat16
+    me = me.astype(jnp.int32).reshape(1)
+
+    e1, own_x, own_y, e2 = Z1(own), X(own), Y(own), Z2(own)
+    own_a, own_b = Y(own_x[:half]), X(own_y[half:])
+    *weights, k0, k0_x, k0_y = experts(
+        (own, own_x, own_y), ((block, f32),) * 3, me, (w_gate, w_up, w_down), first=True
+    )
+    e1_y = Y(after(e1, own_a, own_b))
+    e2_ = after(e2, own_a, own_b, e1, k0_x)
+    e2_x, e2_y, e3 = X(e2_), Y(e2_), Z1(e2_)
+    e3_ = after(e3)
+    e3_x, e3_y = X(e3_), Y(e3_)
+    e1_xd = Z1(after(jnp.concatenate([own_x, own_a, own_b]), e3))
+    e2_d = X(after(e2_y, e2_x))
+    k0_d, k1, send_1 = experts(
+        (own_a, own_b, e1, e1_y), ((block, f32), (block, f32), (block, bf16)), me, weights
+    )
+    e3_x, e3_y = lax.optimization_barrier((e3_x, e3_y, k1))[:2]
+    e3_a, e3_b = Y(e3_x[:half]), X(e3_y[half:])
+    k2, k2_y, send_2 = experts(
+        (e2, e2_y, e2_x, e2_d), ((block, f32), (block, f32), (2 * block, bf16)), me, weights
+    )
+    k3, k3_x, k3_y, send_a, send_b, to_own = experts(
+        (after(e3, send_2), e3_x, e3_y, e3_a, e3_b, e1_xd),
+        (*(((block, f32),) * 3), *(((half, bf16),) * 2), (2 * block, bf16)),
+        me,
+        weights,
+    )
+
+    def joined(part_x, part_y, got_a, got_b):
+        part_x = jnp.concatenate([part_x[:half] + got_a.astype(f32), part_x[half:]])
+        part_y = jnp.concatenate([part_y[:half], part_y[half:] + got_b.astype(f32)])
+        return X(part_x.astype(bf16)), Y(part_y.astype(bf16))
+
+    got_2 = X(send_2)
+    got_a, got_b = Y(send_a), X(send_b)
+    got_x, got_y = joined(k3_x, k3_y, got_a, got_b)
+    r3 = (k3 + got_x.astype(f32) + got_y.astype(f32)).astype(bf16)
+    last_2 = Y((k2_y + got_2[block:].astype(f32)).astype(bf16))
+    r2 = k2 + got_2[:block].astype(f32) + last_2.astype(f32)
+    r2 = r2 + Z1(r3).astype(f32)
+    from_far = Z2(r2.astype(bf16))
+    from_1 = Z1(to_own)
+    r1 = k1 + Y(after(send_1, got_a, got_b)).astype(f32)
+    from_near = Z1(r1.astype(bf16))
+    k0_x = k0_x + from_1[:block].astype(f32)
+    k0_d = (k0_d + from_1[block:].astype(f32)).astype(bf16)
+    got_x, got_y = joined(k0_x, k0_y, Y(k0_d[:half]), X(k0_d[half:]))
+    r0 = k0 + got_x.astype(f32) + got_y.astype(f32)
+    return (r0 + from_near.astype(f32) + from_far.astype(f32)).astype(bf16)
+
+
+def shards(tokens, *rest):
+    tok_rows = tokens.shape[0]
+    n_group, n_local = lax.axis_size("group"), lax.axis_size("local")
+    capacity = min(tok_rows, tok_rows * GROUPS_TOK // n_group)
+    if capacity == tok_rows and n_group == 4 and n_local == 4:
+        return gathered_shards(tokens, *rest)
+    return routed_shards(tokens, *rest)
+
+
 def solution(mesh):
     in_specs = (
         P(("rep", "group", "local"), None),

time: 293 us -> 108 us (0.37)
  the two profiles are of different devices: /device:TPU:14 before, /device:TPU:0 now
where the time goes in v2:
time: 108 us
  starting transfers between devices  44.6 us (41%)
  waiting for transfers between devices  42.3 us (39%)
  Pallas kernels  16.1 us (15%)
  other arithmetic  2.87 us (3%)
  local copies, waits for them, and re-layouts  1.7 us (2%)
    ppermute x31, starting transfers between devices, over(): return lambda v: lax.ppermute(v, axis, pairs)  44.6 us
    ppermute x31, waiting for transfers between devices, over(): return lambda v: lax.ppermute(v, axis, pairs)  42.3 us
    pallas_call x4, Pallas kernels, experts(): pl.pallas_call(functools.partial(first_kernel if first else expert_kernel...  16.1 us
  transfers between devices with their start and end apart: 31, of which 14 were waited for; matrix products, arithmetic and copies ran while one was open for 1% of the time, Pallas kernels for 11%

profile of v2, /device:TPU:0, one launch (start us, length us, event | category | flops | bytes accessed | tf_op | source)
XLA Modules:
  0.0 107.7 jit_solution(4170388593748812235)
XLA Ops:
  2.8 3.0 %collective-permute-start.1 = (bf16[64,2688]{1,0:T(8,128)(2,1)S(1)}, bf16[64,2688]{1,0:T(8,128)(2,1)S(1)}, u32[]{:S(2)}, u32[]{:S(2)}) collective-permute-start(bf16[64,2688]{1,0:T(8,128)(2,1)S(1)} %pad_maximum_fusion.1.refs_0_), channel_id=1, source_target_pairs={{0,4},{2,6},{4,0},{6,2},{1,5},{3,7},{5,1},{7,3},{8,12},{10,14},{12... | collective-permute-start | bytes 1032200 | tf_op jit(solution)/shard_map/ppermute | solution.py:85
  5.8 1.5 %collective-permute-start = (bf16[64,2688]{1,0:T(8,128)(2,1)S(1)}, bf16[64,2688]{1,0:T(8,128)(2,1)S(1)}, u32[]{:S(2)}, u32[]{:S(2)}) collective-permute-start(bf16[64,2688]{1,0:T(8,128)(2,1)S(1)} %pad_maximum_fusion.1.refs_0_), channel_id=1, source_target_pairs={{0,2},{2,0},{4,6},{6,4},{1,3},{3,1},{5,7},{7,5},{8,10},{10,8},{12,... | collective-permute-start | bytes 1032200 | tf_op jit(solution)/shard_map/ppermute | solution.py:85
  7.3 1.6 %collective-permute-start.5 = (bf16[64,2688]{1,0:T(8,128)(2,1)S(1)}, bf16[64,2688]{1,0:T(8,128)(2,1)S(1)}, u32[]{:S(2)}, u32[]{:S(2)}) collective-permute-start(bf16[64,2688]{1,0:T(8,128)(2,1)S(1)} %pad_maximum_fusion.1.refs_0_), channel_id=1, source_target_pairs={{0,8},{8,0},{16,24},{24,16},{1,9},{9,1},{17,25},{25,17},{2,10},{10... | collective-permute-start | bytes 1032200 | tf_op jit(solution)/shard_map/ppermute | solution.py:85
  8.9 2.6 %collective-permute-start.2 = (bf16[64,2688]{1,0:T(8,128)(2,1)S(1)}, bf16[64,2688]{1,0:T(8,128)(2,1)S(1)}, u32[]{:S(2)}, u32[]{:S(2)}) collective-permute-start(bf16[64,2688]{1,0:T(8,128)(2,1)S(1)} %pad_maximum_fusion.1.refs_0_), channel_id=1, source_target_pairs={{0,16},{8,24},{16,0},{24,8},{1,17},{9,25},{17,1},{25,9},{2,18},{10... | collective-permute-start | bytes 1032200 | tf_op jit(solution)/shard_map/ppermute | solution.py:85
  11.5 2.4 %collective-permute-done.1.refs_2_ = bf16[64,2688]{1,0:T(8,128)(2,1)S(1)} collective-permute-done((bf16[64,2688]{1,0:T(8,128)(2,1)S(1)}, bf16[64,2688]{1,0:T(8,128)(2,1)S(1)}, u32[]{:S(2)}, u32[]{:S(2)}) %collective-permute-start.1) | collective-permute-done | bytes 344096 | tf_op jit(solution)/shard_map/ppermute | solution.py:85
  13.9 1.8 %collective-permute-start.4 = (bf16[32,2688]{1,0:T(8,128)(2,1)S(1)}, bf16[32,2688]{1,0:T(8,128)(2,1)S(1)}, u32[]{:S(2)}, u32[]{:S(2)}) collective-permute-start(bf16[32,2688]{1,0:T(8,128)(2,1)S(1)} %slice.77), channel_id=1, source_target_pairs={{0,2},{2,0},{4,6},{6,4},{1,3},{3,1},{5,7},{7,5},{8,10},{10,8},{12,... | collective-permute-start | bytes 516104 | tf_op jit(solution)/shard_map/ppermute | solution.py:85
  15.7 1.6 %collective-permute-start.3 = (bf16[32,2688]{1,0:T(8,128)(2,1)S(1)}, bf16[32,2688]{1,0:T(8,128)(2,1)S(1)}, u32[]{:S(2)}, u32[]{:S(2)}) collective-permute-start(bf16[32,2688]{1,0:T(8,128)(2,1)S(1)} %slice.76), channel_id=1, source_target_pairs={{0,4},{2,6},{4,0},{6,2},{1,5},{3,7},{5,1},{7,3},{8,12},{10,14},{12... | collective-permute-start | bytes 516104 | tf_op jit(solution)/shard_map/ppermute | solution.py:85
  17.3 5.6 %shard_map.64 = (bf16[1,2560,768]{2,1,0:T(8,128)(2,1)S(1)}, bf16[1,2560,768]{2,1,0:T(8,128)(2,1)S(1)}, bf16[1,768,2560]{2,1,0:T(8,128)(2,1)S(1)}, f32[64,2560]{1...) custom-call(s32[1]{0:T(128)} %bitcast.me_ref, bf16[64,2688]{1,0:T(8,128)(2,1)S(1)} %pad_maximum_fusion.1.refs_0_, ...), custom_call_target="tpu_custom_call" | custom-call | flops 2264924160 | bytes 3932160 | tf_op jit(solution)/shard_map/pallas_call | solution.py:142
  23.8 2.4 %collective-permute-done.2.refs_0_ = bf16[64,2688]{1,0:T(8,128)(2,1)S(1)} collective-permute-done((bf16[64,2688]{1,0:T(8,128)(2,1)S(1)}, bf16[64,2688]{1,0:T(8,128)(2,1)S(1)}, u32[]{:S(2)}, u32[]{:S(2)}) %collective-permute-start.2) | collective-permute-done | bytes 344096 | tf_op jit(solution)/shard_map/ppermute | solution.py:85
  27.7 1.5 %collective-permute-start.12 = (bf16[64,2688]{1,0:T(8,128)(2,1)S(1)}, bf16[64,2688]{1,0:T(8,128)(2,1)S(1)}, u32[]{:S(2)}, u32[]{:S(2)}) collective-permute-start(bf16[64,2688]{1,0:T(8,128)(2,1)S(1)} %collective-permute-done.5.refs_2_), channel_id=1, source_target_pairs={{0,4},{2,6},{4,0},{6,2},{1,5},{3,7},{5,1},{7,3},{8,12},{10,14},{12... | collective-permute-start | bytes 1032200 | tf_op jit(solution)/shard_map/ppermute | solution.py:85
  29.2 6.6 %collective-permute-done.6.refs_0_ = bf16[64,2688]{1,0:T(8,128)(2,1)S(1)} collective-permute-done((bf16[64,2688]{1,0:T(8,128)(2,1)S(1)}, bf16[64,2688]{1,0:T(8,128)(2,1)S(1)}, u32[]{:S(2)}, u32[]{:S(2)}) %collective-permute-start.6) | collective-permute-done | bytes 344096 | tf_op jit(solution)/shard_map/ppermute | solution.py:85
  35.9 1.5 %collective-permute-start.11 = (bf16[64,2688]{1,0:T(8,128)(2,1)S(1)}, bf16[64,2688]{1,0:T(8,128)(2,1)S(1)}, u32[]{:S(2)}, u32[]{:S(2)}) collective-permute-start(bf16[64,2688]{1,0:T(8,128)(2,1)S(1)} %collective-permute-done.6.refs_0_), channel_id=1, source_target_pairs={{0,4},{2,6},{4,0},{6,2},{1,5},{3,7},{5,1},{7,3},{8,12},{10,14},{12... | collective-permute-start | bytes 1032200 | tf_op jit(solution)/shard_map/ppermute | solution.py:85
  37.4 1.5 %collective-permute-start.10 = (bf16[64,2688]{1,0:T(8,128)(2,1)S(1)}, bf16[64,2688]{1,0:T(8,128)(2,1)S(1)}, u32[]{:S(2)}, u32[]{:S(2)}) collective-permute-start(bf16[64,2688]{1,0:T(8,128)(2,1)S(1)} %collective-permute-done.6.refs_0_), channel_id=1, source_target_pairs={{0,2},{2,0},{4,6},{6,4},{1,3},{3,1},{5,7},{7,5},{8,10},{10,8},{12,... | collective-permute-start | bytes 1032200 | tf_op jit(solution)/shard_map/ppermute | solution.py:85
  39.4 4.1 %collective-permute-done.12.refs_3_ = bf16[64,2688]{1,0:T(8,128)(2,1)S(1)} collective-permute-done((bf16[64,2688]{1,0:T(8,128)(2,1)S(1)}, bf16[64,2688]{1,0:T(8,128)(2,1)S(1)}, u32[]{:S(2)}, u32[]{:S(2)}) %collective-permute-start.12) | collective-permute-done | bytes 344096 | tf_op jit(solution)/shard_map/ppermute | solution.py:85
  43.5 2.5 %shard_map.66 = (f32[64,2560]{1,0:T(8,128)S(1)}, f32[64,2560]{1,0:T(8,128)S(1)}, bf16[64,2560]{1,0:T(8,128)(2,1)S(1)}) custom-call(s32[1]{0:T(128)} %bitcast.me_ref, bf16[32,2688]{1,0:T(8,128)(2,1)S(1)} %collective-permute-done.3.refs_0_, bf16[32,2688]{1,0:T(8,128)(2,1)S(1)} %collective-permute-done.4.refs_1_, ...), custom_call_target="tpu_custom_call" | custom-call | flops 2264924160 | bytes 3932160 | tf_op jit(solution)/shard_map/pallas_call | solution.py:142
  46.0 2.3 %collective-permute-done.11.refs_2_ = bf16[64,2688]{1,0:T(8,128)(2,1)S(1)} collective-permute-done((bf16[64,2688]{1,0:T(8,128)(2,1)S(1)}, bf16[64,2688]{1,0:T(8,128)(2,1)S(1)}, u32[]{:S(2)}, u32[]{:S(2)}) %collective-permute-start.11) | collective-permute-done | bytes 344096 | tf_op jit(solution)/shard_map/ppermute | solution.py:85
  48.4 2.2 %collective-permute-start.14 = (bf16[32,2688]{1,0:T(8,128)(2,1)S(1)}, bf16[32,2688]{1,0:T(8,128)(2,1)S(1)}, u32[]{:S(2)}, u32[]{:S(2)}) collective-permute-start(bf16[32,2688]{1,0:T(8,128)(2,1)S(1)} %slice.61), channel_id=1, source_target_pairs={{0,2},{2,0},{4,6},{6,4},{1,3},{3,1},{5,7},{7,5},{8,10},{10,8},{12,... | collective-permute-start | bytes 516104 | tf_op jit(solution)/shard_map/ppermute | solution.py:85
  50.6 1.7 %collective-permute-done.9.refs_3_ = bf16[64,2688]{1,0:T(8,128)(2,1)S(1)} collective-permute-done((bf16[64,2688]{1,0:T(8,128)(2,1)S(1)}, bf16[64,2688]{1,0:T(8,128)(2,1)S(1)}, u32[]{:S(2)}, u32[]{:S(2)}) %collective-permute-start.9) | collective-permute-done | bytes 344096 | tf_op jit(solution)/shard_map/ppermute | solution.py:85
  52.3 3.3 %shard_map.65 = (f32[64,2560]{1,0:T(8,128)S(1)}, f32[64,2560]{1,0:T(8,128)S(1)}, bf16[128,2560]{1,0:T(8,128)(2,1)S(1)}) custom-call(s32[1]{0:T(128)} %bitcast.me_ref, bf16[64,2688]{1,0:T(8,128)(2,1)S(1)} %collective-permute-done.2.refs_0_, bf16[64,2688]{1,0:T(8,128)(2,1)S(1)} %collective-permute-done.7.refs_1_, ...), custom_call_target="tpu_custom_call" | custom-call | flops 3019898880 | bytes 5242880 | tf_op jit(solution)/shard_map/pallas_call | solution.py:142
  56.0 4.8 %shard_map.67 = (f32[64,2560]{1,0:T(8,128)S(1)}, f32[64,2560]{1,0:T(8,128)S(1)}, f32[64,2560]{1,0:T(8,128)S(1)}, bf16[32,2560]{1,0:T(8,128)(2,1)S(1)}, bf16[32,2...) custom-call(s32[1]{0:T(128)} %bitcast.me_ref, bf16[64,2688]{1,0:T(8,128)(2,1)S(1)} %collective-permute-done.6.refs_0_, ...), custom_call_target="tpu_custom_call" | custom-call | flops 4529848320 | bytes 7864320 | tf_op jit(solution)/shard_map/pallas_call | solution.py:142
  61.0 1.5 %collective-permute-start.22 = (bf16[32,2560]{1,0:T(8,128)(2,1)S(1)}, bf16[32,2560]{1,0:T(8,128)(2,1)S(1)}, u32[]{:S(2)}, u32[]{:S(2)}) collective-permute-start(bf16[32,2560]{1,0:T(8,128)(2,1)S(1)} %get-tuple-element.50), channel_id=1, source_target_pairs={{0,2},{2,0},{4,6},{6,4},{1,3},{3,1},{5,7},{7,5},{8,10},{10,8},{12,... | collective-permute-start | bytes 491528 | tf_op jit(solution)/shard_map/ppermute | solution.py:85
  64.5 3.6 %collective-permute-done.21 = bf16[32,2560]{1,0:T(8,128)(2,1)S(1)} collective-permute-done((bf16[32,2560]{1,0:T(8,128)(2,1)S(1)}, bf16[32,2560]{1,0:T(8,128)(2,1)S(1)}, u32[]{:S(2)}, u32[]{:S(2)}) %collective-permute-start.21) | collective-permute-done | bytes 163872 | tf_op jit(solution)/shard_map/ppermute | solution.py:85
  68.1 1.9 %collective-permute-start.23 = (bf16[64,2560]{1,0:T(8,128)(2,1)S(1)}, bf16[64,2560]{1,0:T(8,128)(2,1)S(1)}, u32[]{:S(2)}, u32[]{:S(2)}) collective-permute-start(bf16[64,2560]{1,0:T(8,128)(2,1)S(1)} %get-tuple-element.51), channel_id=1, source_target_pairs={{0,4},{2,6},{4,0},{6,2},{1,5},{3,7},{5,1},{7,3},{8,12},{10,14},{12... | collective-permute-start | bytes 983048 | tf_op jit(solution)/shard_map/ppermute | solution.py:85
  70.3 1.6 %collective-permute-start.27 = (bf16[64,2560]{1,0:T(8,128)(2,1)S(1)}, bf16[64,2560]{1,0:T(8,128)(2,1)S(1)}, u32[]{:S(2)}, u32[]{:S(2)}) collective-permute-start(bf16[64,2560]{1,0:T(8,128)(2,1)S(1)} %pad_maximum_fusion.4), channel_id=1, source_target_pairs={{0,2},{2,0},{4,6},{6,4},{1,3},{3,1},{5,7},{7,5},{8,10},{10,8},{12,... | collective-permute-start | bytes 983048 | tf_op jit(solution)/shard_map/ppermute | solution.py:85
  71.9 6.4 %collective-permute-done.25 = bf16[128,2560]{1,0:T(8,128)(2,1)S(1)} collective-permute-done((bf16[128,2560]{1,0:T(8,128)(2,1)S(1)}, bf16[128,2560]{1,0:T(8,128)(2,1)S(1)}, u32[]{:S(2)}, u32[]{:S(2)}) %collective-permute-start.25) | collective-permute-done | bytes 655392 | tf_op jit(solution)/shard_map/ppermute | solution.py:85
  79.6 3.5 %collective-permute-start.24 = (bf16[64,2560]{1,0:T(8,128)(2,1)S(1)}, bf16[64,2560]{1,0:T(8,128)(2,1)S(1)}, u32[]{:S(2)}, u32[]{:S(2)}) collective-permute-start(bf16[64,2560]{1,0:T(8,128)(2,1)S(1)} %add_convert_fusion.4), channel_id=1, source_target_pairs={{0,8},{8,0},{16,24},{24,16},{1,9},{9,1},{17,25},{25,17},{2,10},{10... | collective-permute-start | bytes 983048 | tf_op jit(solution)/shard_map/ppermute | solution.py:85
  83.2 3.2 %collective-permute-start.29 = (bf16[64,2560]{1,0:T(8,128)(2,1)S(1)}, bf16[64,2560]{1,0:T(8,128)(2,1)S(1)}, u32[]{:S(2)}, u32[]{:S(2)}) collective-permute-start(bf16[64,2560]{1,0:T(8,128)(2,1)S(1)} %add_convert_fusion.2), channel_id=1, source_target_pairs={{0,8},{8,0},{16,24},{24,16},{1,9},{9,1},{17,25},{25,17},{2,10},{10... | collective-permute-start | bytes 983048 | tf_op jit(solution)/shard_map/ppermute | solution.py:85
  86.5 1.8 %collective-permute-start.17 = (bf16[32,2560]{1,0:T(8,128)(2,1)S(1)}, bf16[32,2560]{1,0:T(8,128)(2,1)S(1)}, u32[]{:S(2)}, u32[]{:S(2)}) collective-permute-start(bf16[32,2560]{1,0:T(8,128)(2,1)S(1)} %get-tuple-element.59), channel_id=1, source_target_pairs={{0,4},{2,6},{4,0},{6,2},{1,5},{3,7},{5,1},{7,3},{8,12},{10,14},{12... | collective-permute-start | bytes 491528 | tf_op jit(solution)/shard_map/ppermute | solution.py:85
  89.5 5.7 %collective-permute-done.29 = bf16[64,2560]{1,0:T(8,128)(2,1)S(1)} collective-permute-done((bf16[64,2560]{1,0:T(8,128)(2,1)S(1)}, bf16[64,2560]{1,0:T(8,128)(2,1)S(1)}, u32[]{:S(2)}, u32[]{:S(2)}) %collective-permute-start.29) | collective-permute-done | bytes 327712 | tf_op jit(solution)/shard_map/ppermute | solution.py:85
  95.3 3.0 %collective-permute-start.30 = (bf16[64,2560]{1,0:T(8,128)(2,1)S(1)}, bf16[64,2560]{1,0:T(8,128)(2,1)S(1)}, u32[]{:S(2)}, u32[]{:S(2)}) collective-permute-start(bf16[64,2560]{1,0:T(8,128)(2,1)S(1)} %add_convert_fusion.1), channel_id=1, source_target_pairs={{0,16},{8,24},{16,0},{24,8},{1,17},{9,25},{17,1},{25,9},{2,18},{10... | collective-permute-start | bytes 983048 | tf_op jit(solution)/shard_map/ppermute | solution.py:85
  99.4 1.9 %collective-permute-start.18 = (bf16[64,2560]{1,0:T(8,128)(2,1)S(1)}, bf16[64,2560]{1,0:T(8,128)(2,1)S(1)}, u32[]{:S(2)}, u32[]{:S(2)}) collective-permute-start(bf16[64,2560]{1,0:T(8,128)(2,1)S(1)} %pad_maximum_fusion.2), channel_id=1, source_target_pairs={{0,2},{2,0},{4,6},{6,4},{1,3},{3,1},{5,7},{7,5},{8,10},{10,8},{12,... | collective-permute-start | bytes 983048 | tf_op jit(solution)/shard_map/ppermute | solution.py:85
  101.2 5.6 %collective-permute-done.30 = bf16[64,2560]{1,0:T(8,128)(2,1)S(1)} collective-permute-done((bf16[64,2560]{1,0:T(8,128)(2,1)S(1)}, bf16[64,2560]{1,0:T(8,128)(2,1)S(1)}, u32[]{:S(2)}, u32[]{:S(2)}) %collective-permute-start.30) | collective-permute-done | bytes 327712 | tf_op jit(solution)/shard_map/ppermute | solution.py:85
  (62 shorter events, 13.7 us)
Async XLA Ops:
  2.8 11.1 %collective-permute-start.1 = (bf16[64,2688]{1,0:T(8,128)(2,1)S(1)}, bf16[64,2688]{1,0:T(8,128)(2,1)S(1)}, u32[]{:S(2)}, u32[]{:S(2)}) collective-permute-start(bf16[64,2688]{1,0:T(8,128)(2,1)S(1)} %pad_maximum_fusion.1.refs_0_), channel_id=1, source_target_pairs={{0,4},{2,6},{4,0},{6,2},{1,5},{3,7},{5,1},{7,3},{8,12},{10,14},{12... | collective-permute-start | bytes 1032200 | tf_op jit(solution)/shard_map/ppermute | solution.py:85
  5.8 9.9 %collective-permute-start = (bf16[64,2688]{1,0:T(8,128)(2,1)S(1)}, bf16[64,2688]{1,0:T(8,128)(2,1)S(1)}, u32[]{:S(2)}, u32[]{:S(2)}) collective-permute-start(bf16[64,2688]{1,0:T(8,128)(2,1)S(1)} %pad_maximum_fusion.1.refs_0_), channel_id=1, source_target_pairs={{0,2},{2,0},{4,6},{6,4},{1,3},{3,1},{5,7},{7,5},{8,10},{10,8},{12,... | collective-permute-start | bytes 1032200 | tf_op jit(solution)/shard_map/ppermute | solution.py:85
  7.3 16.5 %collective-permute-start.5 = (bf16[64,2688]{1,0:T(8,128)(2,1)S(1)}, bf16[64,2688]{1,0:T(8,128)(2,1)S(1)}, u32[]{:S(2)}, u32[]{:S(2)}) collective-permute-start(bf16[64,2688]{1,0:T(8,128)(2,1)S(1)} %pad_maximum_fusion.1.refs_0_), channel_id=1, source_target_pairs={{0,8},{8,0},{16,24},{24,16},{1,9},{9,1},{17,25},{25,17},{2,10},{10... | collective-permute-start | bytes 1032200 | tf_op jit(solution)/shard_map/ppermute | solution.py:85
  8.9 17.3 %collective-permute-start.2 = (bf16[64,2688]{1,0:T(8,128)(2,1)S(1)}, bf16[64,2688]{1,0:T(8,128)(2,1)S(1)}, u32[]{:S(2)}, u32[]{:S(2)}) collective-permute-start(bf16[64,2688]{1,0:T(8,128)(2,1)S(1)} %pad_maximum_fusion.1.refs_0_), channel_id=1, source_target_pairs={{0,16},{8,24},{16,0},{24,8},{1,17},{9,25},{17,1},{25,9},{2,18},{10... | collective-permute-start | bytes 1032200 | tf_op jit(solution)/shard_map/ppermute | solution.py:85
  13.9 12.3 %collective-permute-start.4 = (bf16[32,2688]{1,0:T(8,128)(2,1)S(1)}, bf16[32,2688]{1,0:T(8,128)(2,1)S(1)}, u32[]{:S(2)}, u32[]{:S(2)}) collective-permute-start(bf16[32,2688]{1,0:T(8,128)(2,1)S(1)} %slice.77), channel_id=1, source_target_pairs={{0,2},{2,0},{4,6},{6,4},{1,3},{3,1},{5,7},{7,5},{8,10},{10,8},{12,... | collective-permute-start | bytes 516104 | tf_op jit(solution)/shard_map/ppermute | solution.py:85
  15.7 10.5 %collective-permute-start.3 = (bf16[32,2688]{1,0:T(8,128)(2,1)S(1)}, bf16[32,2688]{1,0:T(8,128)(2,1)S(1)}, u32[]{:S(2)}, u32[]{:S(2)}) collective-permute-start(bf16[32,2688]{1,0:T(8,128)(2,1)S(1)} %slice.76), channel_id=1, source_target_pairs={{0,4},{2,6},{4,0},{6,2},{1,5},{3,7},{5,1},{7,3},{8,12},{10,14},{12... | collective-permute-start | bytes 516104 | tf_op jit(solution)/shard_map/ppermute | solution.py:85
  26.2 11.2 %collective-permute-start.8 = (bf16[64,2688]{1,0:T(8,128)(2,1)S(1)}, bf16[64,2688]{1,0:T(8,128)(2,1)S(1)}, u32[]{:S(2)}, u32[]{:S(2)}) collective-permute-start(bf16[64,2688]{1,0:T(8,128)(2,1)S(1)} %collective-permute-done.2.refs_0_), channel_id=1, source_target_pairs={{0,2},{2,0},{4,6},{6,4},{1,3},{3,1},{5,7},{7,5},{8,10},{10,8},{12,... | collective-permute-start | bytes 1032200 | tf_op jit(solution)/shard_map/ppermute | solution.py:85
  26.7 12.2 %collective-permute-start.7 = (bf16[64,2688]{1,0:T(8,128)(2,1)S(1)}, bf16[64,2688]{1,0:T(8,128)(2,1)S(1)}, u32[]{:S(2)}, u32[]{:S(2)}) collective-permute-start(bf16[64,2688]{1,0:T(8,128)(2,1)S(1)} %collective-permute-done.2.refs_0_), channel_id=1, source_target_pairs={{0,4},{2,6},{4,0},{6,2},{1,5},{3,7},{5,1},{7,3},{8,12},{10,14},{12... | collective-permute-start | bytes 1032200 | tf_op jit(solution)/shard_map/ppermute | solution.py:85
  27.2 8.6 %collective-permute-start.6 = (bf16[64,2688]{1,0:T(8,128)(2,1)S(1)}, bf16[64,2688]{1,0:T(8,128)(2,1)S(1)}, u32[]{:S(2)}, u32[]{:S(2)}) collective-permute-start(bf16[64,2688]{1,0:T(8,128)(2,1)S(1)} %collective-permute-done.2.refs_0_), channel_id=1, source_target_pairs={{0,8},{8,0},{16,24},{24,16},{1,9},{9,1},{17,25},{25,17},{2,10},{10... | collective-permute-start | bytes 1032200 | tf_op jit(solution)/shard_map/ppermute | solution.py:85
  27.7 15.8 %collective-permute-start.12 = (bf16[64,2688]{1,0:T(8,128)(2,1)S(1)}, bf16[64,2688]{1,0:T(8,128)(2,1)S(1)}, u32[]{:S(2)}, u32[]{:S(2)}) collective-permute-start(bf16[64,2688]{1,0:T(8,128)(2,1)S(1)} %collective-permute-done.5.refs_2_), channel_id=1, source_target_pairs={{0,4},{2,6},{4,0},{6,2},{1,5},{3,7},{5,1},{7,3},{8,12},{10,14},{12... | collective-permute-start | bytes 1032200 | tf_op jit(solution)/shard_map/ppermute | solution.py:85
  35.8 20.2 %collective-permute-start.15 = (bf16[128,2688]{1,0:T(8,128)(2,1)S(1)}, bf16[128,2688]{1,0:T(8,128)(2,1)S(1)}, u32[]{:S(2)}, u32[]{:S(2)}) collective-permute-start(bf16[128,2688]{1,0:T(8,128)(2,1)S(1)} %pad_maximum_fusion), channel_id=1, source_target_pairs={{0,8},{8,0},{16,24},{24,16},{1,9},{9,1},{17,25},{25,17},{2,10},{10... | collective-permute-start | bytes 2064392 | tf_op jit(solution)/shard_map/ppermute | solution.py:85
  35.9 12.5 %collective-permute-start.11 = (bf16[64,2688]{1,0:T(8,128)(2,1)S(1)}, bf16[64,2688]{1,0:T(8,128)(2,1)S(1)}, u32[]{:S(2)}, u32[]{:S(2)}) collective-permute-start(bf16[64,2688]{1,0:T(8,128)(2,1)S(1)} %collective-permute-done.6.refs_0_), channel_id=1, source_target_pairs={{0,4},{2,6},{4,0},{6,2},{1,5},{3,7},{5,1},{7,3},{8,12},{10,14},{12... | collective-permute-start | bytes 1032200 | tf_op jit(solution)/shard_map/ppermute | solution.py:85
  37.4 11.0 %collective-permute-start.10 = (bf16[64,2688]{1,0:T(8,128)(2,1)S(1)}, bf16[64,2688]{1,0:T(8,128)(2,1)S(1)}, u32[]{:S(2)}, u32[]{:S(2)}) collective-permute-start(bf16[64,2688]{1,0:T(8,128)(2,1)S(1)} %collective-permute-done.6.refs_0_), channel_id=1, source_target_pairs={{0,2},{2,0},{4,6},{6,4},{1,3},{3,1},{5,7},{7,5},{8,10},{10,8},{12,... | collective-permute-start | bytes 1032200 | tf_op jit(solution)/shard_map/ppermute | solution.py:85
  38.9 13.4 %collective-permute-start.9 = (bf16[64,2688]{1,0:T(8,128)(2,1)S(1)}, bf16[64,2688]{1,0:T(8,128)(2,1)S(1)}, u32[]{:S(2)}, u32[]{:S(2)}) collective-permute-start(bf16[64,2688]{1,0:T(8,128)(2,1)S(1)} %collective-permute-done.7.refs_1_), channel_id=1, source_target_pairs={{0,2},{2,0},{4,6},{6,4},{1,3},{3,1},{5,7},{7,5},{8,10},{10,8},{12,... | collective-permute-start | bytes 1032200 | tf_op jit(solution)/shard_map/ppermute | solution.py:85
  48.4 7.2 %collective-permute-start.14 = (bf16[32,2688]{1,0:T(8,128)(2,1)S(1)}, bf16[32,2688]{1,0:T(8,128)(2,1)S(1)}, u32[]{:S(2)}, u32[]{:S(2)}) collective-permute-start(bf16[32,2688]{1,0:T(8,128)(2,1)S(1)} %slice.61), channel_id=1, source_target_pairs={{0,2},{2,0},{4,6},{6,4},{1,3},{3,1},{5,7},{7,5},{8,10},{10,8},{12,... | collective-permute-start | bytes 516104 | tf_op jit(solution)/shard_map/ppermute | solution.py:85
  50.6 5.4 %collective-permute-start.13 = (bf16[32,2688]{1,0:T(8,128)(2,1)S(1)}, bf16[32,2688]{1,0:T(8,128)(2,1)S(1)}, u32[]{:S(2)}, u32[]{:S(2)}) collective-permute-start(bf16[32,2688]{1,0:T(8,128)(2,1)S(1)} %slice.60), channel_id=1, source_target_pairs={{0,4},{2,6},{4,0},{6,2},{1,5},{3,7},{5,1},{7,3},{8,12},{10,14},{12... | collective-permute-start | bytes 516104 | tf_op jit(solution)/shard_map/ppermute | solution.py:85
  60.8 7.2 %collective-permute-start.21 = (bf16[32,2560]{1,0:T(8,128)(2,1)S(1)}, bf16[32,2560]{1,0:T(8,128)(2,1)S(1)}, u32[]{:S(2)}, u32[]{:S(2)}) collective-permute-start(bf16[32,2560]{1,0:T(8,128)(2,1)S(1)} %get-tuple-element.49), channel_id=1, source_target_pairs={{0,4},{2,6},{4,0},{6,2},{1,5},{3,7},{5,1},{7,3},{8,12},{10,14},{12... | collective-permute-start | bytes 491528 | tf_op jit(solution)/shard_map/ppermute | solution.py:85
  61.0 7.1 %collective-permute-start.22 = (bf16[32,2560]{1,0:T(8,128)(2,1)S(1)}, bf16[32,2560]{1,0:T(8,128)(2,1)S(1)}, u32[]{:S(2)}, u32[]{:S(2)}) collective-permute-start(bf16[32,2560]{1,0:T(8,128)(2,1)S(1)} %get-tuple-element.50), channel_id=1, source_target_pairs={{0,2},{2,0},{4,6},{6,4},{1,3},{3,1},{5,7},{7,5},{8,10},{10,8},{12,... | collective-permute-start | bytes 491528 | tf_op jit(solution)/shard_map/ppermute | solution.py:85
  62.5 15.8 %collective-permute-start.25 = (bf16[128,2560]{1,0:T(8,128)(2,1)S(1)}, bf16[128,2560]{1,0:T(8,128)(2,1)S(1)}, u32[]{:S(2)}, u32[]{:S(2)}) collective-permute-start(bf16[128,2560]{1,0:T(8,128)(2,1)S(1)} %get-tuple-element.38), channel_id=1, source_target_pairs={{0,2},{2,0},{4,6},{6,4},{1,3},{3,1},{5,7},{7,5},{8,10},{10,8},{12,... | collective-permute-start | bytes 1966088 | tf_op jit(solution)/shard_map/ppermute | solution.py:85
  63.1 23.2 %collective-permute-start.16 = (bf16[128,2560]{1,0:T(8,128)(2,1)S(1)}, bf16[128,2560]{1,0:T(8,128)(2,1)S(1)}, u32[]{:S(2)}, u32[]{:S(2)}) collective-permute-start(bf16[128,2560]{1,0:T(8,128)(2,1)S(1)} %get-tuple-element.45), channel_id=1, source_target_pairs={{0,8},{8,0},{16,24},{24,16},{1,9},{9,1},{17,25},{25,17},{2,10},{10... | collective-permute-start | bytes 1966088 | tf_op jit(solution)/shard_map/ppermute | solution.py:85
  68.1 11.4 %collective-permute-start.23 = (bf16[64,2560]{1,0:T(8,128)(2,1)S(1)}, bf16[64,2560]{1,0:T(8,128)(2,1)S(1)}, u32[]{:S(2)}, u32[]{:S(2)}) collective-permute-start(bf16[64,2560]{1,0:T(8,128)(2,1)S(1)} %get-tuple-element.51), channel_id=1, source_target_pairs={{0,4},{2,6},{4,0},{6,2},{1,5},{3,7},{5,1},{7,3},{8,12},{10,14},{12... | collective-permute-start | bytes 983048 | tf_op jit(solution)/shard_map/ppermute | solution.py:85
  70.1 12.9 %collective-permute-start.28 = (bf16[64,2560]{1,0:T(8,128)(2,1)S(1)}, bf16[64,2560]{1,0:T(8,128)(2,1)S(1)}, u32[]{:S(2)}, u32[]{:S(2)}) collective-permute-start(bf16[64,2560]{1,0:T(8,128)(2,1)S(1)} %pad_maximum_fusion.5), channel_id=1, source_target_pairs={{0,4},{2,6},{4,0},{6,2},{1,5},{3,7},{5,1},{7,3},{8,12},{10,14},{12... | collective-permute-start | bytes 983048 | tf_op jit(solution)/shard_map/ppermute | solution.py:85
  70.3 12.7 %collective-permute-start.27 = (bf16[64,2560]{1,0:T(8,128)(2,1)S(1)}, bf16[64,2560]{1,0:T(8,128)(2,1)S(1)}, u32[]{:S(2)}, u32[]{:S(2)}) collective-permute-start(bf16[64,2560]{1,0:T(8,128)(2,1)S(1)} %pad_maximum_fusion.4), channel_id=1, source_target_pairs={{0,2},{2,0},{4,6},{6,4},{1,3},{3,1},{5,7},{7,5},{8,10},{10,8},{12,... | collective-permute-start | bytes 983048 | tf_op jit(solution)/shard_map/ppermute | solution.py:85
  78.4 11.1 %collective-permute-start.26 = (bf16[64,2560]{1,0:T(8,128)(2,1)S(1)}, bf16[64,2560]{1,0:T(8,128)(2,1)S(1)}, u32[]{:S(2)}, u32[]{:S(2)}) collective-permute-start(bf16[64,2560]{1,0:T(8,128)(2,1)S(1)} %add_convert_fusion.3), channel_id=1, source_target_pairs={{0,4},{2,6},{4,0},{6,2},{1,5},{3,7},{5,1},{7,3},{8,12},{10,14},{12... | collective-permute-start | bytes 983048 | tf_op jit(solution)/shard_map/ppermute | solution.py:85
  79.6 21.6 %collective-permute-start.24 = (bf16[64,2560]{1,0:T(8,128)(2,1)S(1)}, bf16[64,2560]{1,0:T(8,128)(2,1)S(1)}, u32[]{:S(2)}, u32[]{:S(2)}) collective-permute-start(bf16[64,2560]{1,0:T(8,128)(2,1)S(1)} %add_convert_fusion.4), channel_id=1, source_target_pairs={{0,8},{8,0},{16,24},{24,16},{1,9},{9,1},{17,25},{25,17},{2,10},{10... | collective-permute-start | bytes 983048 | tf_op jit(solution)/shard_map/ppermute | solution.py:85
  83.2 12.0 %collective-permute-start.29 = (bf16[64,2560]{1,0:T(8,128)(2,1)S(1)}, bf16[64,2560]{1,0:T(8,128)(2,1)S(1)}, u32[]{:S(2)}, u32[]{:S(2)}) collective-permute-start(bf16[64,2560]{1,0:T(8,128)(2,1)S(1)} %add_convert_fusion.2), channel_id=1, source_target_pairs={{0,8},{8,0},{16,24},{24,16},{1,9},{9,1},{17,25},{25,17},{2,10},{10... | collective-permute-start | bytes 983048 | tf_op jit(solution)/shard_map/ppermute | solution.py:85
  86.5 12.8 %collective-permute-start.17 = (bf16[32,2560]{1,0:T(8,128)(2,1)S(1)}, bf16[32,2560]{1,0:T(8,128)(2,1)S(1)}, u32[]{:S(2)}, u32[]{:S(2)}) collective-permute-start(bf16[32,2560]{1,0:T(8,128)(2,1)S(1)} %get-tuple-element.59), channel_id=1, source_target_pairs={{0,4},{2,6},{4,0},{6,2},{1,5},{3,7},{5,1},{7,3},{8,12},{10,14},{12... | collective-permute-start | bytes 491528 | tf_op jit(solution)/shard_map/ppermute | solution.py:85
  88.3 9.9 %collective-permute-start.19 = (bf16[32,2560]{1,0:T(8,128)(2,1)S(1)}, bf16[32,2560]{1,0:T(8,128)(2,1)S(1)}, u32[]{:S(2)}, u32[]{:S(2)}) collective-permute-start(bf16[32,2560]{1,0:T(8,128)(2,1)S(1)} %get-tuple-element.60), channel_id=1, source_target_pairs={{0,2},{2,0},{4,6},{6,4},{1,3},{3,1},{5,7},{7,5},{8,10},{10,8},{12,... | collective-permute-start | bytes 491528 | tf_op jit(solution)/shard_map/ppermute | solution.py:85
  95.3 11.6 %collective-permute-start.30 = (bf16[64,2560]{1,0:T(8,128)(2,1)S(1)}, bf16[64,2560]{1,0:T(8,128)(2,1)S(1)}, u32[]{:S(2)}, u32[]{:S(2)}) collective-permute-start(bf16[64,2560]{1,0:T(8,128)(2,1)S(1)} %add_convert_fusion.1), channel_id=1, source_target_pairs={{0,16},{8,24},{16,0},{24,8},{1,17},{9,25},{17,1},{25,9},{2,18},{10... | collective-permute-start | bytes 983048 | tf_op jit(solution)/shard_map/ppermute | solution.py:85
  98.3 8.5 %collective-permute-start.20 = (bf16[64,2560]{1,0:T(8,128)(2,1)S(1)}, bf16[64,2560]{1,0:T(8,128)(2,1)S(1)}, u32[]{:S(2)}, u32[]{:S(2)}) collective-permute-start(bf16[64,2560]{1,0:T(8,128)(2,1)S(1)} %pad_maximum_fusion.3), channel_id=1, source_target_pairs={{0,4},{2,6},{4,0},{6,2},{1,5},{3,7},{5,1},{7,3},{8,12},{10,14},{12... | collective-permute-start | bytes 983048 | tf_op jit(solution)/shard_map/ppermute | solution.py:85
  99.4 7.5 %collective-permute-start.18 = (bf16[64,2560]{1,0:T(8,128)(2,1)S(1)}, bf16[64,2560]{1,0:T(8,128)(2,1)S(1)}, u32[]{:S(2)}, u32[]{:S(2)}) collective-permute-start(bf16[64,2560]{1,0:T(8,128)(2,1)S(1)} %pad_maximum_fusion.2), channel_id=1, source_target_pairs={{0,2},{2,0},{4,6},{6,4},{1,3},{3,1},{5,7},{7,5},{8,10},{10,8},{12,... | collective-permute-start | bytes 983048 | tf_op jit(solution)/shard_map/ppermute | solution.py:85

commit v3 on v2

--- a/solution.py
+++ b/solution.py
@@ -164,6 +164,30 @@
     )(me, *pieces, *weights)
 
 
+def label_kernel(tokens_ref, gates_ref, ids_ref, out_ref, sem):
+    width = tokens_ref.shape[1]
+    copy = pltpu.make_async_copy(tokens_ref, out_ref.at[:, pl.ds(0, width)], sem)
+    copy.start()
+    top, rows = gates_ref.shape
+    expert = lax.broadcasted_iota(jnp.int32, (128, rows), 0)
+    table = jnp.zeros((128, rows), jnp.float32)
+    for k in range(top):
+        table += jnp.where(ids_ref[k : k + 1] == expert, gates_ref[k : k + 1].astype(jnp.float32), 0.0)
+    out_ref[:, pl.ds(width, 128)] = table.T.astype(jnp.bfloat16)
+    copy.wait()
+
+
+def labelled(tokens, gates, expert_ids):
+    rows, width = tokens.shape
+    return pl.pallas_call(
+        label_kernel,
+        out_shape=pltpu.VMEM((rows, width + 128), jnp.bfloat16),
+        in_specs=[pl.BlockSpec(memory_space=pltpu.HBM)] + [pl.BlockSpec(memory_space=pltpu.VMEM)] * 2,
+        out_specs=pl.BlockSpec(memory_space=pltpu.VMEM),
+        scratch_shapes=[pltpu.SemaphoreType.DMA],
+    )(pltpu.with_memory_space_constraint(tokens, pltpu.HBM), gates.T, expert_ids.T)
+
+
 def after(value, *done):
     return lax.optimization_barrier((value, *done))[0]
 
@@ -174,63 +198,78 @@
     Z1, Z2 = over("group", 1), over("group", 2)
     me = lax.axis_index("group") * 4 + lax.axis_index("local")
 
-    lanes = jnp.arange(128, dtype=jnp.int32)
-    hits = expert_ids[:, :, None] == lanes
-    weights = jnp.sum(jnp.where(hits, gates[:, :, None], jnp.bfloat16(0.0)), axis=1)
-    own = jnp.concatenate([tokens, weights], axis=1)
+    own = labelled(tokens, gates, expert_ids)
 
     half = block // 2
     f32, bf16 = jnp.float32, jnp.bfloat16
     me = me.astype(jnp.int32).reshape(1)
 
     e1, own_x, own_y, e2 = Z1(own), X(own), Y(own), Z2(own)
-    own_a, own_b = Y(own_x[:half]), X(own_y[half:])
+    own_a = Y(own_x[:half])
+    own_b = X(own_y[half:])
     *weights, k0, k0_x, k0_y = experts(
         (own, own_x, own_y), ((block, f32),) * 3, me, (w_gate, w_up, w_down), first=True
     )
-    e1_y = Y(after(e1, own_a, own_b))
-    e2_ = after(e2, own_a, own_b, e1, k0_x)
-    e2_x, e2_y, e3 = X(e2_), Y(e2_), Z1(e2_)
-    e3_ = after(e3)
-    e3_x, e3_y = X(e3_), Y(e3_)
-    e1_xd = Z1(after(jnp.concatenate([own_x, own_a, own_b]), e3))
-    e2_d = X(after(e2_y, e2_x))
-    k0_d, k1, send_1 = experts(
-        (own_a, own_b, e1, e1_y), ((block, f32), (block, f32), (block, bf16)), me, weights
-    )
-    e3_x, e3_y = lax.optimization_barrier((e3_x, e3_y, k1))[:2]
-    e3_a, e3_b = Y(e3_x[:half]), X(e3_y[half:])
-    k2, k2_y, send_2 = experts(
-        (e2, e2_y, e2_x, e2_d), ((block, f32), (block, f32), (2 * block, bf16)), me, weights
-    )
-    k3, k3_x, k3_y, send_a, send_b, to_own = experts(
-        (after(e3, send_2), e3_x, e3_y, e3_a, e3_b, e1_xd),
-        (*(((block, f32),) * 3), *(((half, bf16),) * 2), (2 * block, bf16)),
+    e2 = after(e2, own_a, own_b, e1, k0_x)
+    e2_x = X(e2)
+    e2_y = Y(e2)
+    e3 = Z1(e2)
+    e2_a = Y(e2_x[:half])
+    e2_b = X(e2_y[half:])
+    e3 = after(e3, e2_x, e2_y)
+    e3_x = X(e3)
+    e3_y = Y(e3)
+    e1_yx = Z1(after(jnp.concatenate([own_y, own_x]), e3))
+    e1_d = Z1(after(jnp.concatenate([own_a, own_b]), e3))
+    k2, k2_l, send_2, k0_d = experts(
+        (e2, e2_y, e2_x, e2_a, e2_b, own_a, own_b),
+        ((block, f32), (block, f32), (2 * block, bf16), (block, f32)),
         me,
         weights,
     )
-
-    def joined(part_x, part_y, got_a, got_b):
-        part_x = jnp.concatenate([part_x[:half] + got_a.astype(f32), part_x[half:]])
-        part_y = jnp.concatenate([part_y[:half], part_y[half:] + got_b.astype(f32)])
-        return X(part_x.astype(bf16)), Y(part_y.astype(bf16))
-
     got_2 = X(send_2)
-    got_a, got_b = Y(send_a), X(send_b)
-    got_x, got_y = joined(k3_x, k3_y, got_a, got_b)
+    e3_a = Y(after(e3_x, e3_y, k2)[:half])
+    e3_b = X(after(e3_y, e3_x, k2)[half:])
+    k3, k3_x, k3_y, send_a, send_b = experts(
+        (after(e3, e1_yx), e3_x, e3_y, e3_a, e3_b),
+        (*(((block, f32),) * 3), (half, bf16), (half, bf16)),
+        me,
+        weights,
+    )
+
+    def for_x(part, got):
+        return jnp.concatenate([part[:half] + got.astype(f32), part[half:]]).astype(bf16)
+
+    def for_y(part, got):
+        return jnp.concatenate([part[:half], part[half:] + got.astype(f32)]).astype(bf16)
+
+    got_a = Y(send_a)
+    got_b = X(send_b)
+    k1, send_1, to_own = experts(
+        (after(e1, send_a), e1_yx, e1_d),
+        ((block, f32), (block, bf16), (2 * block, bf16)),
+        me,
+        weights,
+    )
+    got_x = X(after(for_x(k3_x, got_a), got_b, k1))
+    got_y = Y(after(for_y(k3_y, got_b), got_a, k1))
     r3 = (k3 + got_x.astype(f32) + got_y.astype(f32)).astype(bf16)
-    last_2 = Y((k2_y + got_2[block:].astype(f32)).astype(bf16))
+    last_2 = Y((k2_l + got_2[block:].astype(f32)).astype(bf16))
     r2 = k2 + got_2[:block].astype(f32) + last_2.astype(f32)
-    r2 = r2 + Z1(r3).astype(f32)
-    from_far = Z2(r2.astype(bf16))
     from_1 = Z1(to_own)
-    r1 = k1 + Y(after(send_1, got_a, got_b)).astype(f32)
-    from_near = Z1(r1.astype(bf16))
+    got_1 = Y(after(send_1, got_x, got_y))
+    r1 = (k1 + got_1.astype(f32)).astype(bf16)
+    got_3 = Z1(r3)
+    from_far = Z2((r2 + got_3.astype(f32)).astype(bf16))
+    near = Z1(after(r1, got_3))
     k0_x = k0_x + from_1[:block].astype(f32)
     k0_d = (k0_d + from_1[block:].astype(f32)).astype(bf16)
-    got_x, got_y = joined(k0_x, k0_y, Y(k0_d[:half]), X(k0_d[half:]))
-    r0 = k0 + got_x.astype(f32) + got_y.astype(f32)
-    return (r0 + from_near.astype(f32) + from_far.astype(f32)).astype(bf16)
+    n_a = Y(after(k0_d, got_x, got_y)[:half])
+    n_b = X(after(k0_d, got_x, got_y)[half:])
+    n_x = X(for_x(k0_x, n_a))
+    n_y = Y(for_y(k0_y, n_b))
+    r0 = k0 + n_x.astype(f32) + n_y.astype(f32)
+    return (r0 + near.astype(f32) + from_far.astype(f32)).astype(bf16)
 
 
 def shards(tokens, *rest):

time: 108 us -> 105 us (0.972)
  waiting for transfers between devices: 42.3 us -> 37.8 us
  starting transfers between devices: 44.6 us -> 46.8 us
  Pallas kernels: 16.1 us -> 17.8 us
  local copies, waits for them, and re-layouts: 1.7 us -> 0.17 us
  other arithmetic: 2.87 us -> 1.73 us
    ppermute x31 -> x32, waiting for transfers between devices: 42.3 us -> 37.8 us  [over(): return lambda v: lax.ppermute(v, axis, pairs)]
    ppermute x31 -> x32, starting transfers between devices: 44.6 us -> 46.8 us  [over(): return lambda v: lax.ppermute(v, axis, pairs)]
    pallas_call x0 -> x1, Pallas kernels: none -> 1.69 us  [labelled(): pl.pallas_call(label_kernel, out_shape=pltpu.VMEM((rows, width + 128), jn...]
    unnamed x2 -> x0, local copies, waits for them, and re-layouts: 1.55 us -> none
  transfers between devices with their start and end apart: 31 -> 32, of which waited for: 14 -> 14; matrix products, arithmetic and copies ran while one was open for 1% -> 1% of each run, Pallas kernels for 11% -> 15%
where the time goes in v3:
time: 105 us
  starting transfers between devices  46.8 us (45%)
  waiting for transfers between devices  37.8 us (36%)
  Pallas kernels  17.8 us (17%)
  other arithmetic  1.73 us (2%)
    ppermute x32, starting transfers between devices, over(): return lambda v: lax.ppermute(v, axis, pairs)  46.8 us
    ppermute x32, waiting for transfers between devices, over(): return lambda v: lax.ppermute(v, axis, pairs)  37.8 us
    pallas_call x4, Pallas kernels, experts(): pl.pallas_call(functools.partial(first_kernel if first else expert_kernel...  16.1 us
  transfers between devices with their start and end apart: 32, of which 14 were waited for; matrix products, arithmetic and copies ran while one was open for 1% of the time, Pallas kernels for 15%

profile of v3, /device:TPU:0, one launch (start us, length us, event | category | flops | bytes accessed | tf_op | source)
XLA Modules:
  0.0 104.6 jit_solution(14620574241774886684)
XLA Ops:
  0.0 1.7 %shard_map.64.refs_0_ = bf16[64,2688]{1,0:T(8,128)(2,1)S(1)} custom-call(bf16[64,2560]{1,0:T(8,128)(2,1)} %tokens_ref.1, bf16[8,64]{1,0:T(8,128)(2,1)} %bitcast.4, s32[8,64]{1,0:T(8,128)} %bitcast.3), custom_call_target="tpu_custom_call" | custom-call | tf_op jit(solution)/shard_map/pallas_call | solution.py:182
  1.7 3.0 %collective-permute-start = (bf16[64,2688]{1,0:T(8,128)(2,1)S(1)}, bf16[64,2688]{1,0:T(8,128)(2,1)S(1)}, u32[]{:S(2)}, u32[]{:S(2)}) collective-permute-start(bf16[64,2688]{1,0:T(8,128)(2,1)S(1)} %shard_map.64.refs_0_), channel_id=1, source_target_pairs={{0,2},{2,0},{4,6},{6,4},{1,3},{3,1},{5,7},{7,5},{8,10},{10,8},{12,... | collective-permute-start | bytes 1032200 | tf_op jit(solution)/shard_map/ppermute | solution.py:85
  4.7 1.5 %collective-permute-start.1 = (bf16[64,2688]{1,0:T(8,128)(2,1)S(1)}, bf16[64,2688]{1,0:T(8,128)(2,1)S(1)}, u32[]{:S(2)}, u32[]{:S(2)}) collective-permute-start(bf16[64,2688]{1,0:T(8,128)(2,1)S(1)} %shard_map.64.refs_0_), channel_id=1, source_target_pairs={{0,4},{2,6},{4,0},{6,2},{1,5},{3,7},{5,1},{7,3},{8,12},{10,14},{12... | collective-permute-start | bytes 1032200 | tf_op jit(solution)/shard_map/ppermute | solution.py:85
  6.2 2.6 %collective-permute-start.3 = (bf16[64,2688]{1,0:T(8,128)(2,1)S(1)}, bf16[64,2688]{1,0:T(8,128)(2,1)S(1)}, u32[]{:S(2)}, u32[]{:S(2)}) collective-permute-start(bf16[64,2688]{1,0:T(8,128)(2,1)S(1)} %shard_map.64.refs_0_), channel_id=1, source_target_pairs={{0,16},{8,24},{16,0},{24,8},{1,17},{9,25},{17,1},{25,9},{2,18},{10... | collective-permute-start | bytes 1032200 | tf_op jit(solution)/shard_map/ppermute | solution.py:85
  8.8 1.6 %collective-permute-start.2 = (bf16[64,2688]{1,0:T(8,128)(2,1)S(1)}, bf16[64,2688]{1,0:T(8,128)(2,1)S(1)}, u32[]{:S(2)}, u32[]{:S(2)}) collective-permute-start(bf16[64,2688]{1,0:T(8,128)(2,1)S(1)} %shard_map.64.refs_0_), channel_id=1, source_target_pairs={{0,8},{8,0},{16,24},{24,16},{1,9},{9,1},{17,25},{25,17},{2,10},{10... | collective-permute-start | bytes 1032200 | tf_op jit(solution)/shard_map/ppermute | solution.py:85
  10.4 2.4 %collective-permute-done.refs_1_ = bf16[64,2688]{1,0:T(8,128)(2,1)S(1)} collective-permute-done((bf16[64,2688]{1,0:T(8,128)(2,1)S(1)}, bf16[64,2688]{1,0:T(8,128)(2,1)S(1)}, u32[]{:S(2)}, u32[]{:S(2)}) %collective-permute-start) | collective-permute-done | bytes 344096 | tf_op jit(solution)/shard_map/ppermute | solution.py:85
  12.8 1.8 %collective-permute-start.4 = (bf16[32,2688]{1,0:T(8,128)(2,1)S(1)}, bf16[32,2688]{1,0:T(8,128)(2,1)S(1)}, u32[]{:S(2)}, u32[]{:S(2)}) collective-permute-start(bf16[32,2688]{1,0:T(8,128)(2,1)S(1)} %slice.84), channel_id=1, source_target_pairs={{0,4},{2,6},{4,0},{6,2},{1,5},{3,7},{5,1},{7,3},{8,12},{10,14},{12... | collective-permute-start | bytes 516104 | tf_op jit(solution)/shard_map/ppermute | solution.py:85
  14.6 1.6 %collective-permute-start.5 = (bf16[32,2688]{1,0:T(8,128)(2,1)S(1)}, bf16[32,2688]{1,0:T(8,128)(2,1)S(1)}, u32[]{:S(2)}, u32[]{:S(2)}) collective-permute-start(bf16[32,2688]{1,0:T(8,128)(2,1)S(1)} %slice.85), channel_id=1, source_target_pairs={{0,2},{2,0},{4,6},{6,4},{1,3},{3,1},{5,7},{7,5},{8,10},{10,8},{12,... | collective-permute-start | bytes 516104 | tf_op jit(solution)/shard_map/ppermute | solution.py:85
  16.2 5.6 %shard_map.65 = (bf16[1,2560,768]{2,1,0:T(8,128)(2,1)S(1)}, bf16[1,2560,768]{2,1,0:T(8,128)(2,1)S(1)}, bf16[1,768,2560]{2,1,0:T(8,128)(2,1)S(1)}, f32[64,2560]{1...) custom-call(s32[1]{0:T(128)} %bitcast.me_ref, bf16[64,2688]{1,0:T(8,128)(2,1)S(1)} %shard_map.64.refs_0_, ...), custom_call_target="tpu_custom_call" | custom-call | flops 2264924160 | bytes 3932160 | tf_op jit(solution)/shard_map/pallas_call | solution.py:142
  21.8 2.1 %collective-permute-done.3.refs_0_ = bf16[64,2688]{1,0:T(8,128)(2,1)S(1)} collective-permute-done((bf16[64,2688]{1,0:T(8,128)(2,1)S(1)}, bf16[64,2688]{1,0:T(8,128)(2,1)S(1)}, u32[]{:S(2)}, u32[]{:S(2)}) %collective-permute-start.3) | collective-permute-done | bytes 344096 | tf_op jit(solution)/shard_map/ppermute | solution.py:85
  26.5 6.2 %collective-permute-done.7.refs_2_ = bf16[64,2688]{1,0:T(8,128)(2,1)S(1)} collective-permute-done((bf16[64,2688]{1,0:T(8,128)(2,1)S(1)}, bf16[64,2688]{1,0:T(8,128)(2,1)S(1)}, u32[]{:S(2)}, u32[]{:S(2)}) %collective-permute-start.7) | collective-permute-done | bytes 344096 | tf_op jit(solution)/shard_map/ppermute | solution.py:85
  33.4 1.9 %collective-permute-start.13 = (bf16[32,2688]{1,0:T(8,128)(2,1)S(1)}, bf16[32,2688]{1,0:T(8,128)(2,1)S(1)}, u32[]{:S(2)}, u32[]{:S(2)}) collective-permute-start(bf16[32,2688]{1,0:T(8,128)(2,1)S(1)} %slice.87), channel_id=1, source_target_pairs={{0,2},{2,0},{4,6},{6,4},{1,3},{3,1},{5,7},{7,5},{8,10},{10,8},{12,... | collective-permute-start | bytes 516104 | tf_op jit(solution)/shard_map/ppermute | solution.py:85
  37.1 1.7 %collective-permute-start.9 = (bf16[128,2688]{1,0:T(8,128)(2,1)S(1)}, bf16[128,2688]{1,0:T(8,128)(2,1)S(1)}, u32[]{:S(2)}, u32[]{:S(2)}) collective-permute-start(bf16[128,2688]{1,0:T(8,128)(2,1)S(1)} %pad_maximum_fusion), channel_id=1, source_target_pairs={{0,8},{8,0},{16,24},{24,16},{1,9},{9,1},{17,25},{25,17},{2,10},{10... | collective-permute-start | bytes 2064392 | tf_op jit(solution)/shard_map/ppermute | solution.py:85
  40.7 4.0 %shard_map.66 = (f32[64,2560]{1,0:T(8,128)S(1)}, f32[64,2560]{1,0:T(8,128)S(1)}, bf16[128,2560]{1,0:T(8,128)(2,1)S(1)}, f32[64,2560]{1,0:T(8,128)S(1)}) custom-call(s32[1]{0:T(128)} %bitcast.me_ref, bf16[64,2688]{1,0:T(8,128)(2,1)S(1)} %collective-permute-done.3.refs_0_, bf16[64,2688]{1,0:T(8,128)(2,1)S(1)} %collective-permute-done.8.refs_1_, ...), custom_call_target="tpu_custom_call" | custom-call | flops 3774873600 | bytes 6553600 | tf_op jit(solution)/shard_map/pallas_call | solution.py:142
  44.8 1.6 %collective-permute-start.14 = (bf16[32,2688]{1,0:T(8,128)(2,1)S(1)}, bf16[32,2688]{1,0:T(8,128)(2,1)S(1)}, u32[]{:S(2)}, u32[]{:S(2)}) collective-permute-start(bf16[32,2688]{1,0:T(8,128)(2,1)S(1)} %slice.68), channel_id=1, source_target_pairs={{0,4},{2,6},{4,0},{6,2},{1,5},{3,7},{5,1},{7,3},{8,12},{10,14},{12... | collective-permute-start | bytes 516104 | tf_op jit(solution)/shard_map/ppermute | solution.py:85
  47.3 1.7 %collective-permute-start.16 = (bf16[64,2688]{1,0:T(8,128)(2,1)S(1)}, bf16[64,2688]{1,0:T(8,128)(2,1)S(1)}, u32[]{:S(2)}, u32[]{:S(2)}) collective-permute-start(bf16[64,2688]{1,0:T(8,128)(2,1)S(1)} %pad_maximum_fusion.1), channel_id=1, source_target_pairs={{0,8},{8,0},{16,24},{24,16},{1,9},{9,1},{17,25},{25,17},{2,10},{10... | collective-permute-start | bytes 1032200 | tf_op jit(solution)/shard_map/ppermute | solution.py:85
  49.0 1.6 %collective-permute-start.29 = (bf16[128,2560]{1,0:T(8,128)(2,1)S(1)}, bf16[128,2560]{1,0:T(8,128)(2,1)S(1)}, u32[]{:S(2)}, u32[]{:S(2)}) collective-permute-start(bf16[128,2560]{1,0:T(8,128)(2,1)S(1)} %get-tuple-element.65), channel_id=1, source_target_pairs={{0,2},{2,0},{4,6},{6,4},{1,3},{3,1},{5,7},{7,5},{8,10},{10,8},{12,... | collective-permute-start | bytes 1966088 | tf_op jit(solution)/shard_map/ppermute | solution.py:85
  50.5 4.6 %collective-permute-done.9.refs_1_ = bf16[128,2688]{1,0:T(8,128)(2,1)S(1)} collective-permute-done((bf16[128,2688]{1,0:T(8,128)(2,1)S(1)}, bf16[128,2688]{1,0:T(8,128)(2,1)S(1)}, u32[]{:S(2)}, u32[]{:S(2)}) %collective-permute-start.9) | collective-permute-done | bytes 688160 | tf_op jit(solution)/shard_map/ppermute | solution.py:85
  55.1 3.3 %shard_map.67 = (f32[64,2560]{1,0:T(8,128)S(1)}, f32[64,2560]{1,0:T(8,128)S(1)}, f32[64,2560]{1,0:T(8,128)S(1)}, bf16[32,2560]{1,0:T(8,128)(2,1)S(1)}, bf16[32,2560]{1,0:T(8,128)(2,1)S(1)}) custom-call(s32[1]{0:T(128)} %bitcast.me_ref, bf16[64,2688]{1,0:T(8,128)(2,1)S(1)} %collective-permute-done.6.refs_0_, ...), custom_call_target="tpu_custom_call" | custom-call | flops 3019898880 | bytes 5242880 | tf_op jit(solution)/shard_map/pallas_call | solution.py:142
  58.6 1.6 %collective-permute-start.18 = (bf16[32,2560]{1,0:T(8,128)(2,1)S(1)}, bf16[32,2560]{1,0:T(8,128)(2,1)S(1)}, u32[]{:S(2)}, u32[]{:S(2)}) collective-permute-start(bf16[32,2560]{1,0:T(8,128)(2,1)S(1)} %get-tuple-element.48), channel_id=1, source_target_pairs={{0,4},{2,6},{4,0},{6,2},{1,5},{3,7},{5,1},{7,3},{8,12},{10,14},{12... | collective-permute-start | bytes 491528 | tf_op jit(solution)/shard_map/ppermute | solution.py:85
  60.2 3.3 %shard_map.68 = (f32[64,2560]{1,0:T(8,128)S(1)}, bf16[64,2560]{1,0:T(8,128)(2,1)S(1)}, bf16[128,2560]{1,0:T(8,128)(2,1)S(1)}) custom-call(s32[1]{0:T(128)} %bitcast.me_ref, bf16[64,2688]{1,0:T(8,128)(2,1)S(1)} %collective-permute-done.2.refs_0_, bf16[128,2688]{1,0:T(8,128)(2,1)S(1)} %collective-permute-done.9.refs_1_, ...), custom_call_target="tpu_custom_call" | custom-call | flops 3019898880 | bytes 5242880 | tf_op jit(solution)/shard_map/pallas_call | solution.py:142
  63.5 1.8 %collective-permute-start.17 = (bf16[128,2560]{1,0:T(8,128)(2,1)S(1)}, bf16[128,2560]{1,0:T(8,128)(2,1)S(1)}, u32[]{:S(2)}, u32[]{:S(2)}) collective-permute-start(bf16[128,2560]{1,0:T(8,128)(2,1)S(1)} %get-tuple-element.51), channel_id=1, source_target_pairs={{0,8},{8,0},{16,24},{24,16},{1,9},{9,1},{17,25},{25,17},{2,10},{10... | collective-permute-start | bytes 1966088 | tf_op jit(solution)/shard_map/ppermute | solution.py:85
  65.3 2.7 %collective-permute-done.19 = bf16[32,2560]{1,0:T(8,128)(2,1)S(1)} collective-permute-done((bf16[32,2560]{1,0:T(8,128)(2,1)S(1)}, bf16[32,2560]{1,0:T(8,128)(2,1)S(1)}, u32[]{:S(2)}, u32[]{:S(2)}) %collective-permute-start.19) | collective-permute-done | bytes 163872 | tf_op jit(solution)/shard_map/ppermute | solution.py:85
  70.1 1.8 %collective-permute-start.30 = (bf16[64,2560]{1,0:T(8,128)(2,1)S(1)}, bf16[64,2560]{1,0:T(8,128)(2,1)S(1)}, u32[]{:S(2)}, u32[]{:S(2)}) collective-permute-start(bf16[64,2560]{1,0:T(8,128)(2,1)S(1)} %add_convert_fusion.2), channel_id=1, source_target_pairs={{0,4},{2,6},{4,0},{6,2},{1,5},{3,7},{5,1},{7,3},{8,12},{10,14},{12... | collective-permute-start | bytes 983048 | tf_op jit(solution)/shard_map/ppermute | solution.py:85
  71.9 6.9 %collective-permute-done.21 = bf16[64,2560]{1,0:T(8,128)(2,1)S(1)} collective-permute-done((bf16[64,2560]{1,0:T(8,128)(2,1)S(1)}, bf16[64,2560]{1,0:T(8,128)(2,1)S(1)}, u32[]{:S(2)}, u32[]{:S(2)}) %collective-permute-start.21) | collective-permute-done | bytes 327712 | tf_op jit(solution)/shard_map/ppermute | solution.py:85
  78.9 2.2 %collective-permute-start.27 = (bf16[64,2560]{1,0:T(8,128)(2,1)S(1)}, bf16[64,2560]{1,0:T(8,128)(2,1)S(1)}, u32[]{:S(2)}, u32[]{:S(2)}) collective-permute-start(bf16[64,2560]{1,0:T(8,128)(2,1)S(1)} %add_convert_fusion.3), channel_id=1, source_target_pairs={{0,8},{8,0},{16,24},{24,16},{1,9},{9,1},{17,25},{25,17},{2,10},{10... | collective-permute-start | bytes 983048 | tf_op jit(solution)/shard_map/ppermute | solution.py:85
  81.8 2.1 %collective-permute-start.22 = (bf16[32,2560]{1,0:T(8,128)(2,1)S(1)}, bf16[32,2560]{1,0:T(8,128)(2,1)S(1)}, u32[]{:S(2)}, u32[]{:S(2)}) collective-permute-start(bf16[32,2560]{1,0:T(8,128)(2,1)S(1)} %get-tuple-element.69), channel_id=1, source_target_pairs={{0,4},{2,6},{4,0},{6,2},{1,5},{3,7},{5,1},{7,3},{8,12},{10,14},{12... | collective-permute-start | bytes 491528 | tf_op jit(solution)/shard_map/ppermute | solution.py:85
  83.9 1.9 %collective-permute-done.30 = bf16[64,2560]{1,0:T(8,128)(2,1)S(1)} collective-permute-done((bf16[64,2560]{1,0:T(8,128)(2,1)S(1)}, bf16[64,2560]{1,0:T(8,128)(2,1)S(1)}, u32[]{:S(2)}, u32[]{:S(2)}) %collective-permute-start.30) | collective-permute-done | bytes 327712 | tf_op jit(solution)/shard_map/ppermute | solution.py:85
  85.8 2.6 %collective-permute-done.27 = bf16[64,2560]{1,0:T(8,128)(2,1)S(1)} collective-permute-done((bf16[64,2560]{1,0:T(8,128)(2,1)S(1)}, bf16[64,2560]{1,0:T(8,128)(2,1)S(1)}, u32[]{:S(2)}, u32[]{:S(2)}) %collective-permute-start.27) | collective-permute-done | bytes 327712 | tf_op jit(solution)/shard_map/ppermute | solution.py:85
  88.6 5.4 %collective-permute-start.31 = (bf16[64,2560]{1,0:T(8,128)(2,1)S(1)}, bf16[64,2560]{1,0:T(8,128)(2,1)S(1)}, u32[]{:S(2)}, u32[]{:S(2)}) collective-permute-start(bf16[64,2560]{1,0:T(8,128)(2,1)S(1)} %add_convert_fusion.1), channel_id=1, source_target_pairs={{0,16},{8,24},{16,0},{24,8},{1,17},{9,25},{17,1},{25,9},{2,18},{10... | collective-permute-start | bytes 983048 | tf_op jit(solution)/shard_map/ppermute | solution.py:85
  95.6 2.3 %collective-permute-start.23 = (bf16[64,2560]{1,0:T(8,128)(2,1)S(1)}, bf16[64,2560]{1,0:T(8,128)(2,1)S(1)}, u32[]{:S(2)}, u32[]{:S(2)}) collective-permute-start(bf16[64,2560]{1,0:T(8,128)(2,1)S(1)} %pad_maximum_fusion.4), channel_id=1, source_target_pairs={{0,2},{2,0},{4,6},{6,4},{1,3},{3,1},{5,7},{7,5},{8,10},{10,8},{12,... | collective-permute-start | bytes 983048 | tf_op jit(solution)/shard_map/ppermute | solution.py:85
  98.0 4.4 %collective-permute-done.31 = bf16[64,2560]{1,0:T(8,128)(2,1)S(1)} collective-permute-done((bf16[64,2560]{1,0:T(8,128)(2,1)S(1)}, bf16[64,2560]{1,0:T(8,128)(2,1)S(1)}, u32[]{:S(2)}, u32[]{:S(2)}) %collective-permute-start.31) | collective-permute-done | bytes 327712 | tf_op jit(solution)/shard_map/ppermute | solution.py:85
  (64 shorter events, 15.2 us)
Async XLA Ops:
  1.7 11.1 %collective-permute-start = (bf16[64,2688]{1,0:T(8,128)(2,1)S(1)}, bf16[64,2688]{1,0:T(8,128)(2,1)S(1)}, u32[]{:S(2)}, u32[]{:S(2)}) collective-permute-start(bf16[64,2688]{1,0:T(8,128)(2,1)S(1)} %shard_map.64.refs_0_), channel_id=1, source_target_pairs={{0,2},{2,0},{4,6},{6,4},{1,3},{3,1},{5,7},{7,5},{8,10},{10,8},{12,... | collective-permute-start | bytes 1032200 | tf_op jit(solution)/shard_map/ppermute | solution.py:85
  4.7 9.9 %collective-permute-start.1 = (bf16[64,2688]{1,0:T(8,128)(2,1)S(1)}, bf16[64,2688]{1,0:T(8,128)(2,1)S(1)}, u32[]{:S(2)}, u32[]{:S(2)}) collective-permute-start(bf16[64,2688]{1,0:T(8,128)(2,1)S(1)} %shard_map.64.refs_0_), channel_id=1, source_target_pairs={{0,4},{2,6},{4,0},{6,2},{1,5},{3,7},{5,1},{7,3},{8,12},{10,14},{12... | collective-permute-start | bytes 1032200 | tf_op jit(solution)/shard_map/ppermute | solution.py:85
  6.2 17.6 %collective-permute-start.3 = (bf16[64,2688]{1,0:T(8,128)(2,1)S(1)}, bf16[64,2688]{1,0:T(8,128)(2,1)S(1)}, u32[]{:S(2)}, u32[]{:S(2)}) collective-permute-start(bf16[64,2688]{1,0:T(8,128)(2,1)S(1)} %shard_map.64.refs_0_), channel_id=1, source_target_pairs={{0,16},{8,24},{16,0},{24,8},{1,17},{9,25},{17,1},{25,9},{2,18},{10... | collective-permute-start | bytes 1032200 | tf_op jit(solution)/shard_map/ppermute | solution.py:85
  8.8 15.2 %collective-permute-start.2 = (bf16[64,2688]{1,0:T(8,128)(2,1)S(1)}, bf16[64,2688]{1,0:T(8,128)(2,1)S(1)}, u32[]{:S(2)}, u32[]{:S(2)}) collective-permute-start(bf16[64,2688]{1,0:T(8,128)(2,1)S(1)} %shard_map.64.refs_0_), channel_id=1, source_target_pairs={{0,8},{8,0},{16,24},{24,16},{1,9},{9,1},{17,25},{25,17},{2,10},{10... | collective-permute-start | bytes 1032200 | tf_op jit(solution)/shard_map/ppermute | solution.py:85
  12.8 11.3 %collective-permute-start.4 = (bf16[32,2688]{1,0:T(8,128)(2,1)S(1)}, bf16[32,2688]{1,0:T(8,128)(2,1)S(1)}, u32[]{:S(2)}, u32[]{:S(2)}) collective-permute-start(bf16[32,2688]{1,0:T(8,128)(2,1)S(1)} %slice.84), channel_id=1, source_target_pairs={{0,4},{2,6},{4,0},{6,2},{1,5},{3,7},{5,1},{7,3},{8,12},{10,14},{12... | collective-permute-start | bytes 516104 | tf_op jit(solution)/shard_map/ppermute | solution.py:85
  14.6 9.4 %collective-permute-start.5 = (bf16[32,2688]{1,0:T(8,128)(2,1)S(1)}, bf16[32,2688]{1,0:T(8,128)(2,1)S(1)}, u32[]{:S(2)}, u32[]{:S(2)}) collective-permute-start(bf16[32,2688]{1,0:T(8,128)(2,1)S(1)} %slice.85), channel_id=1, source_target_pairs={{0,2},{2,0},{4,6},{6,4},{1,3},{3,1},{5,7},{7,5},{8,10},{10,8},{12,... | collective-permute-start | bytes 516104 | tf_op jit(solution)/shard_map/ppermute | solution.py:85
  24.0 8.7 %collective-permute-start.7 = (bf16[64,2688]{1,0:T(8,128)(2,1)S(1)}, bf16[64,2688]{1,0:T(8,128)(2,1)S(1)}, u32[]{:S(2)}, u32[]{:S(2)}) collective-permute-start(bf16[64,2688]{1,0:T(8,128)(2,1)S(1)} %collective-permute-done.3.refs_0_), channel_id=1, source_target_pairs={{0,2},{2,0},{4,6},{6,4},{1,3},{3,1},{5,7},{7,5},{8,10},{10,8},{12,... | collective-permute-start | bytes 1032200 | tf_op jit(solution)/shard_map/ppermute | solution.py:85
  24.6 8.8 %collective-permute-start.8 = (bf16[64,2688]{1,0:T(8,128)(2,1)S(1)}, bf16[64,2688]{1,0:T(8,128)(2,1)S(1)}, u32[]{:S(2)}, u32[]{:S(2)}) collective-permute-start(bf16[64,2688]{1,0:T(8,128)(2,1)S(1)} %collective-permute-done.3.refs_0_), channel_id=1, source_target_pairs={{0,4},{2,6},{4,0},{6,2},{1,5},{3,7},{5,1},{7,3},{8,12},{10,14},{12... | collective-permute-start | bytes 1032200 | tf_op jit(solution)/shard_map/ppermute | solution.py:85
  25.0 10.3 %collective-permute-start.6 = (bf16[64,2688]{1,0:T(8,128)(2,1)S(1)}, bf16[64,2688]{1,0:T(8,128)(2,1)S(1)}, u32[]{:S(2)}, u32[]{:S(2)}) collective-permute-start(bf16[64,2688]{1,0:T(8,128)(2,1)S(1)} %collective-permute-done.3.refs_0_), channel_id=1, source_target_pairs={{0,8},{8,0},{16,24},{24,16},{1,9},{9,1},{17,25},{25,17},{2,10},{10... | collective-permute-start | bytes 1032200 | tf_op jit(solution)/shard_map/ppermute | solution.py:85
  32.8 7.3 %collective-permute-start.12 = (bf16[32,2688]{1,0:T(8,128)(2,1)S(1)}, bf16[32,2688]{1,0:T(8,128)(2,1)S(1)}, u32[]{:S(2)}, u32[]{:S(2)}) collective-permute-start(bf16[32,2688]{1,0:T(8,128)(2,1)S(1)} %slice.86), channel_id=1, source_target_pairs={{0,4},{2,6},{4,0},{6,2},{1,5},{3,7},{5,1},{7,3},{8,12},{10,14},{12... | collective-permute-start | bytes 516104 | tf_op jit(solution)/shard_map/ppermute | solution.py:85
  33.4 7.4 %collective-permute-start.13 = (bf16[32,2688]{1,0:T(8,128)(2,1)S(1)}, bf16[32,2688]{1,0:T(8,128)(2,1)S(1)}, u32[]{:S(2)}, u32[]{:S(2)}) collective-permute-start(bf16[32,2688]{1,0:T(8,128)(2,1)S(1)} %slice.87), channel_id=1, source_target_pairs={{0,2},{2,0},{4,6},{6,4},{1,3},{3,1},{5,7},{7,5},{8,10},{10,8},{12,... | collective-permute-start | bytes 516104 | tf_op jit(solution)/shard_map/ppermute | solution.py:85
  35.3 9.5 %collective-permute-start.10 = (bf16[64,2688]{1,0:T(8,128)(2,1)S(1)}, bf16[64,2688]{1,0:T(8,128)(2,1)S(1)}, u32[]{:S(2)}, u32[]{:S(2)}) collective-permute-start(bf16[64,2688]{1,0:T(8,128)(2,1)S(1)} %collective-permute-done.6.refs_0_), channel_id=1, source_target_pairs={{0,2},{2,0},{4,6},{6,4},{1,3},{3,1},{5,7},{7,5},{8,10},{10,8},{12,... | collective-permute-start | bytes 1032200 | tf_op jit(solution)/shard_map/ppermute | solution.py:85
  35.6 9.2 %collective-permute-start.11 = (bf16[64,2688]{1,0:T(8,128)(2,1)S(1)}, bf16[64,2688]{1,0:T(8,128)(2,1)S(1)}, u32[]{:S(2)}, u32[]{:S(2)}) collective-permute-start(bf16[64,2688]{1,0:T(8,128)(2,1)S(1)} %collective-permute-done.6.refs_0_), channel_id=1, source_target_pairs={{0,4},{2,6},{4,0},{6,2},{1,5},{3,7},{5,1},{7,3},{8,12},{10,14},{12... | collective-permute-start | bytes 1032200 | tf_op jit(solution)/shard_map/ppermute | solution.py:85
  37.1 18.0 %collective-permute-start.9 = (bf16[128,2688]{1,0:T(8,128)(2,1)S(1)}, bf16[128,2688]{1,0:T(8,128)(2,1)S(1)}, u32[]{:S(2)}, u32[]{:S(2)}) collective-permute-start(bf16[128,2688]{1,0:T(8,128)(2,1)S(1)} %pad_maximum_fusion), channel_id=1, source_target_pairs={{0,8},{8,0},{16,24},{24,16},{1,9},{9,1},{17,25},{25,17},{2,10},{10... | collective-permute-start | bytes 2064392 | tf_op jit(solution)/shard_map/ppermute | solution.py:85
  44.8 10.3 %collective-permute-start.14 = (bf16[32,2688]{1,0:T(8,128)(2,1)S(1)}, bf16[32,2688]{1,0:T(8,128)(2,1)S(1)}, u32[]{:S(2)}, u32[]{:S(2)}) collective-permute-start(bf16[32,2688]{1,0:T(8,128)(2,1)S(1)} %slice.68), channel_id=1, source_target_pairs={{0,4},{2,6},{4,0},{6,2},{1,5},{3,7},{5,1},{7,3},{8,12},{10,14},{12... | collective-permute-start | bytes 516104 | tf_op jit(solution)/shard_map/ppermute | solution.py:85
  46.4 8.7 %collective-permute-start.15 = (bf16[32,2688]{1,0:T(8,128)(2,1)S(1)}, bf16[32,2688]{1,0:T(8,128)(2,1)S(1)}, u32[]{:S(2)}, u32[]{:S(2)}) collective-permute-start(bf16[32,2688]{1,0:T(8,128)(2,1)S(1)} %slice.69), channel_id=1, source_target_pairs={{0,2},{2,0},{4,6},{6,4},{1,3},{3,1},{5,7},{7,5},{8,10},{10,8},{12,... | collective-permute-start | bytes 516104 | tf_op jit(solution)/shard_map/ppermute | solution.py:85
  47.3 12.9 %collective-permute-start.16 = (bf16[64,2688]{1,0:T(8,128)(2,1)S(1)}, bf16[64,2688]{1,0:T(8,128)(2,1)S(1)}, u32[]{:S(2)}, u32[]{:S(2)}) collective-permute-start(bf16[64,2688]{1,0:T(8,128)(2,1)S(1)} %pad_maximum_fusion.1), channel_id=1, source_target_pairs={{0,8},{8,0},{16,24},{24,16},{1,9},{9,1},{17,25},{25,17},{2,10},{10... | collective-permute-start | bytes 1032200 | tf_op jit(solution)/shard_map/ppermute | solution.py:85
  49.0 21.1 %collective-permute-start.29 = (bf16[128,2560]{1,0:T(8,128)(2,1)S(1)}, bf16[128,2560]{1,0:T(8,128)(2,1)S(1)}, u32[]{:S(2)}, u32[]{:S(2)}) collective-permute-start(bf16[128,2560]{1,0:T(8,128)(2,1)S(1)} %get-tuple-element.65), channel_id=1, source_target_pairs={{0,2},{2,0},{4,6},{6,4},{1,3},{3,1},{5,7},{7,5},{8,10},{10,8},{12,... | collective-permute-start | bytes 1966088 | tf_op jit(solution)/shard_map/ppermute | solution.py:85
  58.4 9.6 %collective-permute-start.19 = (bf16[32,2560]{1,0:T(8,128)(2,1)S(1)}, bf16[32,2560]{1,0:T(8,128)(2,1)S(1)}, u32[]{:S(2)}, u32[]{:S(2)}) collective-permute-start(bf16[32,2560]{1,0:T(8,128)(2,1)S(1)} %get-tuple-element.54), channel_id=1, source_target_pairs={{0,2},{2,0},{4,6},{6,4},{1,3},{3,1},{5,7},{7,5},{8,10},{10,8},{12,... | collective-permute-start | bytes 491528 | tf_op jit(solution)/shard_map/ppermute | solution.py:85
  58.6 9.4 %collective-permute-start.18 = (bf16[32,2560]{1,0:T(8,128)(2,1)S(1)}, bf16[32,2560]{1,0:T(8,128)(2,1)S(1)}, u32[]{:S(2)}, u32[]{:S(2)}) collective-permute-start(bf16[32,2560]{1,0:T(8,128)(2,1)S(1)} %get-tuple-element.48), channel_id=1, source_target_pairs={{0,4},{2,6},{4,0},{6,2},{1,5},{3,7},{5,1},{7,3},{8,12},{10,14},{12... | collective-permute-start | bytes 491528 | tf_op jit(solution)/shard_map/ppermute | solution.py:85
  63.5 17.6 %collective-permute-start.17 = (bf16[128,2560]{1,0:T(8,128)(2,1)S(1)}, bf16[128,2560]{1,0:T(8,128)(2,1)S(1)}, u32[]{:S(2)}, u32[]{:S(2)}) collective-permute-start(bf16[128,2560]{1,0:T(8,128)(2,1)S(1)} %get-tuple-element.51), channel_id=1, source_target_pairs={{0,8},{8,0},{16,24},{24,16},{1,9},{9,1},{17,25},{25,17},{2,10},{10... | collective-permute-start | bytes 1966088 | tf_op jit(solution)/shard_map/ppermute | solution.py:85
  68.1 10.7 %collective-permute-start.21 = (bf16[64,2560]{1,0:T(8,128)(2,1)S(1)}, bf16[64,2560]{1,0:T(8,128)(2,1)S(1)}, u32[]{:S(2)}, u32[]{:S(2)}) collective-permute-start(bf16[64,2560]{1,0:T(8,128)(2,1)S(1)} %pad_maximum_fusion.3), channel_id=1, source_target_pairs={{0,4},{2,6},{4,0},{6,2},{1,5},{3,7},{5,1},{7,3},{8,12},{10,14},{12... | collective-permute-start | bytes 983048 | tf_op jit(solution)/shard_map/ppermute | solution.py:85
  69.1 9.7 %collective-permute-start.20 = (bf16[64,2560]{1,0:T(8,128)(2,1)S(1)}, bf16[64,2560]{1,0:T(8,128)(2,1)S(1)}, u32[]{:S(2)}, u32[]{:S(2)}) collective-permute-start(bf16[64,2560]{1,0:T(8,128)(2,1)S(1)} %pad_maximum_fusion.2), channel_id=1, source_target_pairs={{0,2},{2,0},{4,6},{6,4},{1,3},{3,1},{5,7},{7,5},{8,10},{10,8},{12,... | collective-permute-start | bytes 983048 | tf_op jit(solution)/shard_map/ppermute | solution.py:85
  70.1 15.7 %collective-permute-start.30 = (bf16[64,2560]{1,0:T(8,128)(2,1)S(1)}, bf16[64,2560]{1,0:T(8,128)(2,1)S(1)}, u32[]{:S(2)}, u32[]{:S(2)}) collective-permute-start(bf16[64,2560]{1,0:T(8,128)(2,1)S(1)} %add_convert_fusion.2), channel_id=1, source_target_pairs={{0,4},{2,6},{4,0},{6,2},{1,5},{3,7},{5,1},{7,3},{8,12},{10,14},{12... | collective-permute-start | bytes 983048 | tf_op jit(solution)/shard_map/ppermute | solution.py:85
  78.9 9.5 %collective-permute-start.27 = (bf16[64,2560]{1,0:T(8,128)(2,1)S(1)}, bf16[64,2560]{1,0:T(8,128)(2,1)S(1)}, u32[]{:S(2)}, u32[]{:S(2)}) collective-permute-start(bf16[64,2560]{1,0:T(8,128)(2,1)S(1)} %add_convert_fusion.3), channel_id=1, source_target_pairs={{0,8},{8,0},{16,24},{24,16},{1,9},{9,1},{17,25},{25,17},{2,10},{10... | collective-permute-start | bytes 983048 | tf_op jit(solution)/shard_map/ppermute | solution.py:85
  81.1 12.9 %collective-permute-start.26 = (bf16[64,2560]{1,0:T(8,128)(2,1)S(1)}, bf16[64,2560]{1,0:T(8,128)(2,1)S(1)}, u32[]{:S(2)}, u32[]{:S(2)}) collective-permute-start(bf16[64,2560]{1,0:T(8,128)(2,1)S(1)} %get-tuple-element.62), channel_id=1, source_target_pairs={{0,4},{2,6},{4,0},{6,2},{1,5},{3,7},{5,1},{7,3},{8,12},{10,14},{12... | collective-permute-start | bytes 983048 | tf_op jit(solution)/shard_map/ppermute | solution.py:85
  81.3 13.5 %collective-permute-start.24 = (bf16[32,2560]{1,0:T(8,128)(2,1)S(1)}, bf16[32,2560]{1,0:T(8,128)(2,1)S(1)}, u32[]{:S(2)}, u32[]{:S(2)}) collective-permute-start(bf16[32,2560]{1,0:T(8,128)(2,1)S(1)} %get-tuple-element.70), channel_id=1, source_target_pairs={{0,2},{2,0},{4,6},{6,4},{1,3},{3,1},{5,7},{7,5},{8,10},{10,8},{12,... | collective-permute-start | bytes 491528 | tf_op jit(solution)/shard_map/ppermute | solution.py:85
  81.8 13.7 %collective-permute-start.22 = (bf16[32,2560]{1,0:T(8,128)(2,1)S(1)}, bf16[32,2560]{1,0:T(8,128)(2,1)S(1)}, u32[]{:S(2)}, u32[]{:S(2)}) collective-permute-start(bf16[32,2560]{1,0:T(8,128)(2,1)S(1)} %get-tuple-element.69), channel_id=1, source_target_pairs={{0,4},{2,6},{4,0},{6,2},{1,5},{3,7},{5,1},{7,3},{8,12},{10,14},{12... | collective-permute-start | bytes 491528 | tf_op jit(solution)/shard_map/ppermute | solution.py:85
  88.6 13.8 %collective-permute-start.31 = (bf16[64,2560]{1,0:T(8,128)(2,1)S(1)}, bf16[64,2560]{1,0:T(8,128)(2,1)S(1)}, u32[]{:S(2)}, u32[]{:S(2)}) collective-permute-start(bf16[64,2560]{1,0:T(8,128)(2,1)S(1)} %add_convert_fusion.1), channel_id=1, source_target_pairs={{0,16},{8,24},{16,0},{24,8},{1,17},{9,25},{17,1},{25,9},{2,18},{10... | collective-permute-start | bytes 983048 | tf_op jit(solution)/shard_map/ppermute | solution.py:85
  94.1 9.6 %collective-permute-start.28 = (bf16[64,2560]{1,0:T(8,128)(2,1)S(1)}, bf16[64,2560]{1,0:T(8,128)(2,1)S(1)}, u32[]{:S(2)}, u32[]{:S(2)}) collective-permute-start(bf16[64,2560]{1,0:T(8,128)(2,1)S(1)} %add_convert_fusion.4), channel_id=1, source_target_pairs={{0,8},{8,0},{16,24},{24,16},{1,9},{9,1},{17,25},{25,17},{2,10},{10... | collective-permute-start | bytes 983048 | tf_op jit(solution)/shard_map/ppermute | solution.py:85
  94.9 8.8 %collective-permute-start.25 = (bf16[64,2560]{1,0:T(8,128)(2,1)S(1)}, bf16[64,2560]{1,0:T(8,128)(2,1)S(1)}, u32[]{:S(2)}, u32[]{:S(2)}) collective-permute-start(bf16[64,2560]{1,0:T(8,128)(2,1)S(1)} %pad_maximum_fusion.5), channel_id=1, source_target_pairs={{0,4},{2,6},{4,0},{6,2},{1,5},{3,7},{5,1},{7,3},{8,12},{10,14},{12... | collective-permute-start | bytes 983048 | tf_op jit(solution)/shard_map/ppermute | solution.py:85
  95.6 8.0 %collective-permute-start.23 = (bf16[64,2560]{1,0:T(8,128)(2,1)S(1)}, bf16[64,2560]{1,0:T(8,128)(2,1)S(1)}, u32[]{:S(2)}, u32[]{:S(2)}) collective-permute-start(bf16[64,2560]{1,0:T(8,128)(2,1)S(1)} %pad_maximum_fusion.4), channel_id=1, source_target_pairs={{0,2},{2,0},{4,6},{6,4},{1,3},{3,1},{5,7},{7,5},{8,10},{10,8},{12,... | collective-permute-start | bytes 983048 | tf_op jit(solution)/shard_map/ppermute | solution.py:85

commit v4 on v3

--- a/solution.py
+++ b/solution.py
@@ -135,7 +135,7 @@
 def experts(pieces, outs, me, weights, first=False):
     n_rows = sum(p.shape[0] for p in pieces)
     _, width, ff = weights[0].shape
-    ff_tile, out_tile = ff // 3, width // 5
+    ff_tile, out_tile = ff // 3, width // 2
     vmem = pl.BlockSpec(memory_space=pltpu.VMEM)
     if first:
         weights = [pltpu.with_memory_space_constraint(w, pltpu.HBM) for w in weights]

time: 105 us -> 105 us (level)
  no operation moved by 1% of the time
where the time goes in v4:
time: 105 us
  starting transfers between devices  46.8 us (45%)
  waiting for transfers between devices  37.8 us (36%)
  Pallas kernels  17.8 us (17%)
  other arithmetic  1.73 us (2%)
    ppermute x32, starting transfers between devices, over(): return lambda v: lax.ppermute(v, axis, pairs)  46.8 us
    ppermute x32, waiting for transfers between devices, over(): return lambda v: lax.ppermute(v, axis, pairs)  37.8 us
    pallas_call x4, Pallas kernels, experts(): pl.pallas_call(functools.partial(first_kernel if first else expert_kernel...  16.1 us
  transfers between devices with their start and end apart: 32, of which 14 were waited for; matrix products, arithmetic and copies ran while one was open for 1% of the time, Pallas kernels for 15%

profile of v4, /device:TPU:0, one launch (start us, length us, event | category | flops | bytes accessed | tf_op | source)
XLA Modules:
  0.0 104.6 jit_solution(14620574241774886684)
XLA Ops:
  0.0 1.7 %shard_map.64.refs_0_ = bf16[64,2688]{1,0:T(8,128)(2,1)S(1)} custom-call(bf16[64,2560]{1,0:T(8,128)(2,1)} %tokens_ref.1, bf16[8,64]{1,0:T(8,128)(2,1)} %bitcast.4, s32[8,64]{1,0:T(8,128)} %bitcast.3), custom_call_target="tpu_custom_call" | custom-call | tf_op jit(solution)/shard_map/pallas_call | solution.py:182
  1.7 3.0 %collective-permute-start = (bf16[64,2688]{1,0:T(8,128)(2,1)S(1)}, bf16[64,2688]{1,0:T(8,128)(2,1)S(1)}, u32[]{:S(2)}, u32[]{:S(2)}) collective-permute-start(bf16[64,2688]{1,0:T(8,128)(2,1)S(1)} %shard_map.64.refs_0_), channel_id=1, source_target_pairs={{0,2},{2,0},{4,6},{6,4},{1,3},{3,1},{5,7},{7,5},{8,10},{10,8},{12,... | collective-permute-start | bytes 1032200 | tf_op jit(solution)/shard_map/ppermute | solution.py:85
  4.7 1.5 %collective-permute-start.1 = (bf16[64,2688]{1,0:T(8,128)(2,1)S(1)}, bf16[64,2688]{1,0:T(8,128)(2,1)S(1)}, u32[]{:S(2)}, u32[]{:S(2)}) collective-permute-start(bf16[64,2688]{1,0:T(8,128)(2,1)S(1)} %shard_map.64.refs_0_), channel_id=1, source_target_pairs={{0,4},{2,6},{4,0},{6,2},{1,5},{3,7},{5,1},{7,3},{8,12},{10,14},{12... | collective-permute-start | bytes 1032200 | tf_op jit(solution)/shard_map/ppermute | solution.py:85
  6.2 2.6 %collective-permute-start.3 = (bf16[64,2688]{1,0:T(8,128)(2,1)S(1)}, bf16[64,2688]{1,0:T(8,128)(2,1)S(1)}, u32[]{:S(2)}, u32[]{:S(2)}) collective-permute-start(bf16[64,2688]{1,0:T(8,128)(2,1)S(1)} %shard_map.64.refs_0_), channel_id=1, source_target_pairs={{0,16},{8,24},{16,0},{24,8},{1,17},{9,25},{17,1},{25,9},{2,18},{10... | collective-permute-start | bytes 1032200 | tf_op jit(solution)/shard_map/ppermute | solution.py:85
  8.8 1.6 %collective-permute-start.2 = (bf16[64,2688]{1,0:T(8,128)(2,1)S(1)}, bf16[64,2688]{1,0:T(8,128)(2,1)S(1)}, u32[]{:S(2)}, u32[]{:S(2)}) collective-permute-start(bf16[64,2688]{1,0:T(8,128)(2,1)S(1)} %shard_map.64.refs_0_), channel_id=1, source_target_pairs={{0,8},{8,0},{16,24},{24,16},{1,9},{9,1},{17,25},{25,17},{2,10},{10... | collective-permute-start | bytes 1032200 | tf_op jit(solution)/shard_map/ppermute | solution.py:85
  10.4 2.4 %collective-permute-done.refs_1_ = bf16[64,2688]{1,0:T(8,128)(2,1)S(1)} collective-permute-done((bf16[64,2688]{1,0:T(8,128)(2,1)S(1)}, bf16[64,2688]{1,0:T(8,128)(2,1)S(1)}, u32[]{:S(2)}, u32[]{:S(2)}) %collective-permute-start) | collective-permute-done | bytes 344096 | tf_op jit(solution)/shard_map/ppermute | solution.py:85
  12.8 1.8 %collective-permute-start.4 = (bf16[32,2688]{1,0:T(8,128)(2,1)S(1)}, bf16[32,2688]{1,0:T(8,128)(2,1)S(1)}, u32[]{:S(2)}, u32[]{:S(2)}) collective-permute-start(bf16[32,2688]{1,0:T(8,128)(2,1)S(1)} %slice.84), channel_id=1, source_target_pairs={{0,4},{2,6},{4,0},{6,2},{1,5},{3,7},{5,1},{7,3},{8,12},{10,14},{12... | collective-permute-start | bytes 516104 | tf_op jit(solution)/shard_map/ppermute | solution.py:85
  14.6 1.6 %collective-permute-start.5 = (bf16[32,2688]{1,0:T(8,128)(2,1)S(1)}, bf16[32,2688]{1,0:T(8,128)(2,1)S(1)}, u32[]{:S(2)}, u32[]{:S(2)}) collective-permute-start(bf16[32,2688]{1,0:T(8,128)(2,1)S(1)} %slice.85), channel_id=1, source_target_pairs={{0,2},{2,0},{4,6},{6,4},{1,3},{3,1},{5,7},{7,5},{8,10},{10,8},{12,... | collective-permute-start | bytes 516104 | tf_op jit(solution)/shard_map/ppermute | solution.py:85
  16.2 5.6 %shard_map.65 = (bf16[1,2560,768]{2,1,0:T(8,128)(2,1)S(1)}, bf16[1,2560,768]{2,1,0:T(8,128)(2,1)S(1)}, bf16[1,768,2560]{2,1,0:T(8,128)(2,1)S(1)}, f32[64,2560]{1...) custom-call(s32[1]{0:T(128)} %bitcast.me_ref, bf16[64,2688]{1,0:T(8,128)(2,1)S(1)} %shard_map.64.refs_0_, ...), custom_call_target="tpu_custom_call" | custom-call | flops 2264924160 | bytes 3932160 | tf_op jit(solution)/shard_map/pallas_call | solution.py:142
  21.8 2.1 %collective-permute-done.3.refs_0_ = bf16[64,2688]{1,0:T(8,128)(2,1)S(1)} collective-permute-done((bf16[64,2688]{1,0:T(8,128)(2,1)S(1)}, bf16[64,2688]{1,0:T(8,128)(2,1)S(1)}, u32[]{:S(2)}, u32[]{:S(2)}) %collective-permute-start.3) | collective-permute-done | bytes 344096 | tf_op jit(solution)/shard_map/ppermute | solution.py:85
  26.5 6.2 %collective-permute-done.7.refs_2_ = bf16[64,2688]{1,0:T(8,128)(2,1)S(1)} collective-permute-done((bf16[64,2688]{1,0:T(8,128)(2,1)S(1)}, bf16[64,2688]{1,0:T(8,128)(2,1)S(1)}, u32[]{:S(2)}, u32[]{:S(2)}) %collective-permute-start.7) | collective-permute-done | bytes 344096 | tf_op jit(solution)/shard_map/ppermute | solution.py:85
  33.4 1.9 %collective-permute-start.13 = (bf16[32,2688]{1,0:T(8,128)(2,1)S(1)}, bf16[32,2688]{1,0:T(8,128)(2,1)S(1)}, u32[]{:S(2)}, u32[]{:S(2)}) collective-permute-start(bf16[32,2688]{1,0:T(8,128)(2,1)S(1)} %slice.87), channel_id=1, source_target_pairs={{0,2},{2,0},{4,6},{6,4},{1,3},{3,1},{5,7},{7,5},{8,10},{10,8},{12,... | collective-permute-start | bytes 516104 | tf_op jit(solution)/shard_map/ppermute | solution.py:85
  37.1 1.7 %collective-permute-start.9 = (bf16[128,2688]{1,0:T(8,128)(2,1)S(1)}, bf16[128,2688]{1,0:T(8,128)(2,1)S(1)}, u32[]{:S(2)}, u32[]{:S(2)}) collective-permute-start(bf16[128,2688]{1,0:T(8,128)(2,1)S(1)} %pad_maximum_fusion), channel_id=1, source_target_pairs={{0,8},{8,0},{16,24},{24,16},{1,9},{9,1},{17,25},{25,17},{2,10},{10... | collective-permute-start | bytes 2064392 | tf_op jit(solution)/shard_map/ppermute | solution.py:85
  40.7 4.0 %shard_map.66 = (f32[64,2560]{1,0:T(8,128)S(1)}, f32[64,2560]{1,0:T(8,128)S(1)}, bf16[128,2560]{1,0:T(8,128)(2,1)S(1)}, f32[64,2560]{1,0:T(8,128)S(1)}) custom-call(s32[1]{0:T(128)} %bitcast.me_ref, bf16[64,2688]{1,0:T(8,128)(2,1)S(1)} %collective-permute-done.3.refs_0_, bf16[64,2688]{1,0:T(8,128)(2,1)S(1)} %collective-permute-done.8.refs_1_, ...), custom_call_target="tpu_custom_call" | custom-call | flops 3774873600 | bytes 6553600 | tf_op jit(solution)/shard_map/pallas_call | solution.py:142
  44.8 1.6 %collective-permute-start.14 = (bf16[32,2688]{1,0:T(8,128)(2,1)S(1)}, bf16[32,2688]{1,0:T(8,128)(2,1)S(1)}, u32[]{:S(2)}, u32[]{:S(2)}) collective-permute-start(bf16[32,2688]{1,0:T(8,128)(2,1)S(1)} %slice.68), channel_id=1, source_target_pairs={{0,4},{2,6},{4,0},{6,2},{1,5},{3,7},{5,1},{7,3},{8,12},{10,14},{12... | collective-permute-start | bytes 516104 | tf_op jit(solution)/shard_map/ppermute | solution.py:85
  47.3 1.7 %collective-permute-start.16 = (bf16[64,2688]{1,0:T(8,128)(2,1)S(1)}, bf16[64,2688]{1,0:T(8,128)(2,1)S(1)}, u32[]{:S(2)}, u32[]{:S(2)}) collective-permute-start(bf16[64,2688]{1,0:T(8,128)(2,1)S(1)} %pad_maximum_fusion.1), channel_id=1, source_target_pairs={{0,8},{8,0},{16,24},{24,16},{1,9},{9,1},{17,25},{25,17},{2,10},{10... | collective-permute-start | bytes 1032200 | tf_op jit(solution)/shard_map/ppermute | solution.py:85
  49.0 1.6 %collective-permute-start.29 = (bf16[128,2560]{1,0:T(8,128)(2,1)S(1)}, bf16[128,2560]{1,0:T(8,128)(2,1)S(1)}, u32[]{:S(2)}, u32[]{:S(2)}) collective-permute-start(bf16[128,2560]{1,0:T(8,128)(2,1)S(1)} %get-tuple-element.65), channel_id=1, source_target_pairs={{0,2},{2,0},{4,6},{6,4},{1,3},{3,1},{5,7},{7,5},{8,10},{10,8},{12,... | collective-permute-start | bytes 1966088 | tf_op jit(solution)/shard_map/ppermute | solution.py:85
  50.5 4.6 %collective-permute-done.9.refs_1_ = bf16[128,2688]{1,0:T(8,128)(2,1)S(1)} collective-permute-done((bf16[128,2688]{1,0:T(8,128)(2,1)S(1)}, bf16[128,2688]{1,0:T(8,128)(2,1)S(1)}, u32[]{:S(2)}, u32[]{:S(2)}) %collective-permute-start.9) | collective-permute-done | bytes 688160 | tf_op jit(solution)/shard_map/ppermute | solution.py:85
  55.1 3.3 %shard_map.67 = (f32[64,2560]{1,0:T(8,128)S(1)}, f32[64,2560]{1,0:T(8,128)S(1)}, f32[64,2560]{1,0:T(8,128)S(1)}, bf16[32,2560]{1,0:T(8,128)(2,1)S(1)}, bf16[32,2560]{1,0:T(8,128)(2,1)S(1)}) custom-call(s32[1]{0:T(128)} %bitcast.me_ref, bf16[64,2688]{1,0:T(8,128)(2,1)S(1)} %collective-permute-done.6.refs_0_, ...), custom_call_target="tpu_custom_call" | custom-call | flops 3019898880 | bytes 5242880 | tf_op jit(solution)/shard_map/pallas_call | solution.py:142
  58.6 1.6 %collective-permute-start.18 = (bf16[32,2560]{1,0:T(8,128)(2,1)S(1)}, bf16[32,2560]{1,0:T(8,128)(2,1)S(1)}, u32[]{:S(2)}, u32[]{:S(2)}) collective-permute-start(bf16[32,2560]{1,0:T(8,128)(2,1)S(1)} %get-tuple-element.48), channel_id=1, source_target_pairs={{0,4},{2,6},{4,0},{6,2},{1,5},{3,7},{5,1},{7,3},{8,12},{10,14},{12... | collective-permute-start | bytes 491528 | tf_op jit(solution)/shard_map/ppermute | solution.py:85
  60.2 3.3 %shard_map.68 = (f32[64,2560]{1,0:T(8,128)S(1)}, bf16[64,2560]{1,0:T(8,128)(2,1)S(1)}, bf16[128,2560]{1,0:T(8,128)(2,1)S(1)}) custom-call(s32[1]{0:T(128)} %bitcast.me_ref, bf16[64,2688]{1,0:T(8,128)(2,1)S(1)} %collective-permute-done.2.refs_0_, bf16[128,2688]{1,0:T(8,128)(2,1)S(1)} %collective-permute-done.9.refs_1_, ...), custom_call_target="tpu_custom_call" | custom-call | flops 3019898880 | bytes 5242880 | tf_op jit(solution)/shard_map/pallas_call | solution.py:142
  63.5 1.8 %collective-permute-start.17 = (bf16[128,2560]{1,0:T(8,128)(2,1)S(1)}, bf16[128,2560]{1,0:T(8,128)(2,1)S(1)}, u32[]{:S(2)}, u32[]{:S(2)}) collective-permute-start(bf16[128,2560]{1,0:T(8,128)(2,1)S(1)} %get-tuple-element.51), channel_id=1, source_target_pairs={{0,8},{8,0},{16,24},{24,16},{1,9},{9,1},{17,25},{25,17},{2,10},{10... | collective-permute-start | bytes 1966088 | tf_op jit(solution)/shard_map/ppermute | solution.py:85
  65.3 2.7 %collective-permute-done.19 = bf16[32,2560]{1,0:T(8,128)(2,1)S(1)} collective-permute-done((bf16[32,2560]{1,0:T(8,128)(2,1)S(1)}, bf16[32,2560]{1,0:T(8,128)(2,1)S(1)}, u32[]{:S(2)}, u32[]{:S(2)}) %collective-permute-start.19) | collective-permute-done | bytes 163872 | tf_op jit(solution)/shard_map/ppermute | solution.py:85
  70.1 1.8 %collective-permute-start.30 = (bf16[64,2560]{1,0:T(8,128)(2,1)S(1)}, bf16[64,2560]{1,0:T(8,128)(2,1)S(1)}, u32[]{:S(2)}, u32[]{:S(2)}) collective-permute-start(bf16[64,2560]{1,0:T(8,128)(2,1)S(1)} %add_convert_fusion.2), channel_id=1, source_target_pairs={{0,4},{2,6},{4,0},{6,2},{1,5},{3,7},{5,1},{7,3},{8,12},{10,14},{12... | collective-permute-start | bytes 983048 | tf_op jit(solution)/shard_map/ppermute | solution.py:85
  71.9 6.9 %collective-permute-done.21 = bf16[64,2560]{1,0:T(8,128)(2,1)S(1)} collective-permute-done((bf16[64,2560]{1,0:T(8,128)(2,1)S(1)}, bf16[64,2560]{1,0:T(8,128)(2,1)S(1)}, u32[]{:S(2)}, u32[]{:S(2)}) %collective-permute-start.21) | collective-permute-done | bytes 327712 | tf_op jit(solution)/shard_map/ppermute | solution.py:85
  78.9 2.2 %collective-permute-start.27 = (bf16[64,2560]{1,0:T(8,128)(2,1)S(1)}, bf16[64,2560]{1,0:T(8,128)(2,1)S(1)}, u32[]{:S(2)}, u32[]{:S(2)}) collective-permute-start(bf16[64,2560]{1,0:T(8,128)(2,1)S(1)} %add_convert_fusion.3), channel_id=1, source_target_pairs={{0,8},{8,0},{16,24},{24,16},{1,9},{9,1},{17,25},{25,17},{2,10},{10... | collective-permute-start | bytes 983048 | tf_op jit(solution)/shard_map/ppermute | solution.py:85
  81.8 2.1 %collective-permute-start.22 = (bf16[32,2560]{1,0:T(8,128)(2,1)S(1)}, bf16[32,2560]{1,0:T(8,128)(2,1)S(1)}, u32[]{:S(2)}, u32[]{:S(2)}) collective-permute-start(bf16[32,2560]{1,0:T(8,128)(2,1)S(1)} %get-tuple-element.69), channel_id=1, source_target_pairs={{0,4},{2,6},{4,0},{6,2},{1,5},{3,7},{5,1},{7,3},{8,12},{10,14},{12... | collective-permute-start | bytes 491528 | tf_op jit(solution)/shard_map/ppermute | solution.py:85
  83.9 1.9 %collective-permute-done.30 = bf16[64,2560]{1,0:T(8,128)(2,1)S(1)} collective-permute-done((bf16[64,2560]{1,0:T(8,128)(2,1)S(1)}, bf16[64,2560]{1,0:T(8,128)(2,1)S(1)}, u32[]{:S(2)}, u32[]{:S(2)}) %collective-permute-start.30) | collective-permute-done | bytes 327712 | tf_op jit(solution)/shard_map/ppermute | solution.py:85
  85.8 2.6 %collective-permute-done.27 = bf16[64,2560]{1,0:T(8,128)(2,1)S(1)} collective-permute-done((bf16[64,2560]{1,0:T(8,128)(2,1)S(1)}, bf16[64,2560]{1,0:T(8,128)(2,1)S(1)}, u32[]{:S(2)}, u32[]{:S(2)}) %collective-permute-start.27) | collective-permute-done | bytes 327712 | tf_op jit(solution)/shard_map/ppermute | solution.py:85
  88.6 5.4 %collective-permute-start.31 = (bf16[64,2560]{1,0:T(8,128)(2,1)S(1)}, bf16[64,2560]{1,0:T(8,128)(2,1)S(1)}, u32[]{:S(2)}, u32[]{:S(2)}) collective-permute-start(bf16[64,2560]{1,0:T(8,128)(2,1)S(1)} %add_convert_fusion.1), channel_id=1, source_target_pairs={{0,16},{8,24},{16,0},{24,8},{1,17},{9,25},{17,1},{25,9},{2,18},{10... | collective-permute-start | bytes 983048 | tf_op jit(solution)/shard_map/ppermute | solution.py:85
  95.6 2.3 %collective-permute-start.23 = (bf16[64,2560]{1,0:T(8,128)(2,1)S(1)}, bf16[64,2560]{1,0:T(8,128)(2,1)S(1)}, u32[]{:S(2)}, u32[]{:S(2)}) collective-permute-start(bf16[64,2560]{1,0:T(8,128)(2,1)S(1)} %pad_maximum_fusion.4), channel_id=1, source_target_pairs={{0,2},{2,0},{4,6},{6,4},{1,3},{3,1},{5,7},{7,5},{8,10},{10,8},{12,... | collective-permute-start | bytes 983048 | tf_op jit(solution)/shard_map/ppermute | solution.py:85
  98.0 4.4 %collective-permute-done.31 = bf16[64,2560]{1,0:T(8,128)(2,1)S(1)} collective-permute-done((bf16[64,2560]{1,0:T(8,128)(2,1)S(1)}, bf16[64,2560]{1,0:T(8,128)(2,1)S(1)}, u32[]{:S(2)}, u32[]{:S(2)}) %collective-permute-start.31) | collective-permute-done | bytes 327712 | tf_op jit(solution)/shard_map/ppermute | solution.py:85
  (64 shorter events, 15.2 us)
Async XLA Ops:
  1.7 11.1 %collective-permute-start = (bf16[64,2688]{1,0:T(8,128)(2,1)S(1)}, bf16[64,2688]{1,0:T(8,128)(2,1)S(1)}, u32[]{:S(2)}, u32[]{:S(2)}) collective-permute-start(bf16[64,2688]{1,0:T(8,128)(2,1)S(1)} %shard_map.64.refs_0_), channel_id=1, source_target_pairs={{0,2},{2,0},{4,6},{6,4},{1,3},{3,1},{5,7},{7,5},{8,10},{10,8},{12,... | collective-permute-start | bytes 1032200 | tf_op jit(solution)/shard_map/ppermute | solution.py:85
  4.7 9.9 %collective-permute-start.1 = (bf16[64,2688]{1,0:T(8,128)(2,1)S(1)}, bf16[64,2688]{1,0:T(8,128)(2,1)S(1)}, u32[]{:S(2)}, u32[]{:S(2)}) collective-permute-start(bf16[64,2688]{1,0:T(8,128)(2,1)S(1)} %shard_map.64.refs_0_), channel_id=1, source_target_pairs={{0,4},{2,6},{4,0},{6,2},{1,5},{3,7},{5,1},{7,3},{8,12},{10,14},{12... | collective-permute-start | bytes 1032200 | tf_op jit(solution)/shard_map/ppermute | solution.py:85
  6.2 17.6 %collective-permute-start.3 = (bf16[64,2688]{1,0:T(8,128)(2,1)S(1)}, bf16[64,2688]{1,0:T(8,128)(2,1)S(1)}, u32[]{:S(2)}, u32[]{:S(2)}) collective-permute-start(bf16[64,2688]{1,0:T(8,128)(2,1)S(1)} %shard_map.64.refs_0_), channel_id=1, source_target_pairs={{0,16},{8,24},{16,0},{24,8},{1,17},{9,25},{17,1},{25,9},{2,18},{10... | collective-permute-start | bytes 1032200 | tf_op jit(solution)/shard_map/ppermute | solution.py:85
  8.8 15.2 %collective-permute-start.2 = (bf16[64,2688]{1,0:T(8,128)(2,1)S(1)}, bf16[64,2688]{1,0:T(8,128)(2,1)S(1)}, u32[]{:S(2)}, u32[]{:S(2)}) collective-permute-start(bf16[64,2688]{1,0:T(8,128)(2,1)S(1)} %shard_map.64.refs_0_), channel_id=1, source_target_pairs={{0,8},{8,0},{16,24},{24,16},{1,9},{9,1},{17,25},{25,17},{2,10},{10... | collective-permute-start | bytes 1032200 | tf_op jit(solution)/shard_map/ppermute | solution.py:85
  12.8 11.3 %collective-permute-start.4 = (bf16[32,2688]{1,0:T(8,128)(2,1)S(1)}, bf16[32,2688]{1,0:T(8,128)(2,1)S(1)}, u32[]{:S(2)}, u32[]{:S(2)}) collective-permute-start(bf16[32,2688]{1,0:T(8,128)(2,1)S(1)} %slice.84), channel_id=1, source_target_pairs={{0,4},{2,6},{4,0},{6,2},{1,5},{3,7},{5,1},{7,3},{8,12},{10,14},{12... | collective-permute-start | bytes 516104 | tf_op jit(solution)/shard_map/ppermute | solution.py:85
  14.6 9.4 %collective-permute-start.5 = (bf16[32,2688]{1,0:T(8,128)(2,1)S(1)}, bf16[32,2688]{1,0:T(8,128)(2,1)S(1)}, u32[]{:S(2)}, u32[]{:S(2)}) collective-permute-start(bf16[32,2688]{1,0:T(8,128)(2,1)S(1)} %slice.85), channel_id=1, source_target_pairs={{0,2},{2,0},{4,6},{6,4},{1,3},{3,1},{5,7},{7,5},{8,10},{10,8},{12,... | collective-permute-start | bytes 516104 | tf_op jit(solution)/shard_map/ppermute | solution.py:85
  24.0 8.7 %collective-permute-start.7 = (bf16[64,2688]{1,0:T(8,128)(2,1)S(1)}, bf16[64,2688]{1,0:T(8,128)(2,1)S(1)}, u32[]{:S(2)}, u32[]{:S(2)}) collective-permute-start(bf16[64,2688]{1,0:T(8,128)(2,1)S(1)} %collective-permute-done.3.refs_0_), channel_id=1, source_target_pairs={{0,2},{2,0},{4,6},{6,4},{1,3},{3,1},{5,7},{7,5},{8,10},{10,8},{12,... | collective-permute-start | bytes 1032200 | tf_op jit(solution)/shard_map/ppermute | solution.py:85
  24.6 8.8 %collective-permute-start.8 = (bf16[64,2688]{1,0:T(8,128)(2,1)S(1)}, bf16[64,2688]{1,0:T(8,128)(2,1)S(1)}, u32[]{:S(2)}, u32[]{:S(2)}) collective-permute-start(bf16[64,2688]{1,0:T(8,128)(2,1)S(1)} %collective-permute-done.3.refs_0_), channel_id=1, source_target_pairs={{0,4},{2,6},{4,0},{6,2},{1,5},{3,7},{5,1},{7,3},{8,12},{10,14},{12... | collective-permute-start | bytes 1032200 | tf_op jit(solution)/shard_map/ppermute | solution.py:85
  25.0 10.3 %collective-permute-start.6 = (bf16[64,2688]{1,0:T(8,128)(2,1)S(1)}, bf16[64,2688]{1,0:T(8,128)(2,1)S(1)}, u32[]{:S(2)}, u32[]{:S(2)}) collective-permute-start(bf16[64,2688]{1,0:T(8,128)(2,1)S(1)} %collective-permute-done.3.refs_0_), channel_id=1, source_target_pairs={{0,8},{8,0},{16,24},{24,16},{1,9},{9,1},{17,25},{25,17},{2,10},{10... | collective-permute-start | bytes 1032200 | tf_op jit(solution)/shard_map/ppermute | solution.py:85
  32.8 7.3 %collective-permute-start.12 = (bf16[32,2688]{1,0:T(8,128)(2,1)S(1)}, bf16[32,2688]{1,0:T(8,128)(2,1)S(1)}, u32[]{:S(2)}, u32[]{:S(2)}) collective-permute-start(bf16[32,2688]{1,0:T(8,128)(2,1)S(1)} %slice.86), channel_id=1, source_target_pairs={{0,4},{2,6},{4,0},{6,2},{1,5},{3,7},{5,1},{7,3},{8,12},{10,14},{12... | collective-permute-start | bytes 516104 | tf_op jit(solution)/shard_map/ppermute | solution.py:85
  33.4 7.4 %collective-permute-start.13 = (bf16[32,2688]{1,0:T(8,128)(2,1)S(1)}, bf16[32,2688]{1,0:T(8,128)(2,1)S(1)}, u32[]{:S(2)}, u32[]{:S(2)}) collective-permute-start(bf16[32,2688]{1,0:T(8,128)(2,1)S(1)} %slice.87), channel_id=1, source_target_pairs={{0,2},{2,0},{4,6},{6,4},{1,3},{3,1},{5,7},{7,5},{8,10},{10,8},{12,... | collective-permute-start | bytes 516104 | tf_op jit(solution)/shard_map/ppermute | solution.py:85
  35.3 9.5 %collective-permute-start.10 = (bf16[64,2688]{1,0:T(8,128)(2,1)S(1)}, bf16[64,2688]{1,0:T(8,128)(2,1)S(1)}, u32[]{:S(2)}, u32[]{:S(2)}) collective-permute-start(bf16[64,2688]{1,0:T(8,128)(2,1)S(1)} %collective-permute-done.6.refs_0_), channel_id=1, source_target_pairs={{0,2},{2,0},{4,6},{6,4},{1,3},{3,1},{5,7},{7,5},{8,10},{10,8},{12,... | collective-permute-start | bytes 1032200 | tf_op jit(solution)/shard_map/ppermute | solution.py:85
  35.6 9.2 %collective-permute-start.11 = (bf16[64,2688]{1,0:T(8,128)(2,1)S(1)}, bf16[64,2688]{1,0:T(8,128)(2,1)S(1)}, u32[]{:S(2)}, u32[]{:S(2)}) collective-permute-start(bf16[64,2688]{1,0:T(8,128)(2,1)S(1)} %collective-permute-done.6.refs_0_), channel_id=1, source_target_pairs={{0,4},{2,6},{4,0},{6,2},{1,5},{3,7},{5,1},{7,3},{8,12},{10,14},{12... | collective-permute-start | bytes 1032200 | tf_op jit(solution)/shard_map/ppermute | solution.py:85
  37.1 18.0 %collective-permute-start.9 = (bf16[128,2688]{1,0:T(8,128)(2,1)S(1)}, bf16[128,2688]{1,0:T(8,128)(2,1)S(1)}, u32[]{:S(2)}, u32[]{:S(2)}) collective-permute-start(bf16[128,2688]{1,0:T(8,128)(2,1)S(1)} %pad_maximum_fusion), channel_id=1, source_target_pairs={{0,8},{8,0},{16,24},{24,16},{1,9},{9,1},{17,25},{25,17},{2,10},{10... | collective-permute-start | bytes 2064392 | tf_op jit(solution)/shard_map/ppermute | solution.py:85
  44.8 10.3 %collective-permute-start.14 = (bf16[32,2688]{1,0:T(8,128)(2,1)S(1)}, bf16[32,2688]{1,0:T(8,128)(2,1)S(1)}, u32[]{:S(2)}, u32[]{:S(2)}) collective-permute-start(bf16[32,2688]{1,0:T(8,128)(2,1)S(1)} %slice.68), channel_id=1, source_target_pairs={{0,4},{2,6},{4,0},{6,2},{1,5},{3,7},{5,1},{7,3},{8,12},{10,14},{12... | collective-permute-start | bytes 516104 | tf_op jit(solution)/shard_map/ppermute | solution.py:85
  46.4 8.7 %collective-permute-start.15 = (bf16[32,2688]{1,0:T(8,128)(2,1)S(1)}, bf16[32,2688]{1,0:T(8,128)(2,1)S(1)}, u32[]{:S(2)}, u32[]{:S(2)}) collective-permute-start(bf16[32,2688]{1,0:T(8,128)(2,1)S(1)} %slice.69), channel_id=1, source_target_pairs={{0,2},{2,0},{4,6},{6,4},{1,3},{3,1},{5,7},{7,5},{8,10},{10,8},{12,... | collective-permute-start | bytes 516104 | tf_op jit(solution)/shard_map/ppermute | solution.py:85
  47.3 12.9 %collective-permute-start.16 = (bf16[64,2688]{1,0:T(8,128)(2,1)S(1)}, bf16[64,2688]{1,0:T(8,128)(2,1)S(1)}, u32[]{:S(2)}, u32[]{:S(2)}) collective-permute-start(bf16[64,2688]{1,0:T(8,128)(2,1)S(1)} %pad_maximum_fusion.1), channel_id=1, source_target_pairs={{0,8},{8,0},{16,24},{24,16},{1,9},{9,1},{17,25},{25,17},{2,10},{10... | collective-permute-start | bytes 1032200 | tf_op jit(solution)/shard_map/ppermute | solution.py:85
  49.0 21.1 %collective-permute-start.29 = (bf16[128,2560]{1,0:T(8,128)(2,1)S(1)}, bf16[128,2560]{1,0:T(8,128)(2,1)S(1)}, u32[]{:S(2)}, u32[]{:S(2)}) collective-permute-start(bf16[128,2560]{1,0:T(8,128)(2,1)S(1)} %get-tuple-element.65), channel_id=1, source_target_pairs={{0,2},{2,0},{4,6},{6,4},{1,3},{3,1},{5,7},{7,5},{8,10},{10,8},{12,... | collective-permute-start | bytes 1966088 | tf_op jit(solution)/shard_map/ppermute | solution.py:85
  58.4 9.6 %collective-permute-start.19 = (bf16[32,2560]{1,0:T(8,128)(2,1)S(1)}, bf16[32,2560]{1,0:T(8,128)(2,1)S(1)}, u32[]{:S(2)}, u32[]{:S(2)}) collective-permute-start(bf16[32,2560]{1,0:T(8,128)(2,1)S(1)} %get-tuple-element.54), channel_id=1, source_target_pairs={{0,2},{2,0},{4,6},{6,4},{1,3},{3,1},{5,7},{7,5},{8,10},{10,8},{12,... | collective-permute-start | bytes 491528 | tf_op jit(solution)/shard_map/ppermute | solution.py:85
  58.6 9.4 %collective-permute-start.18 = (bf16[32,2560]{1,0:T(8,128)(2,1)S(1)}, bf16[32,2560]{1,0:T(8,128)(2,1)S(1)}, u32[]{:S(2)}, u32[]{:S(2)}) collective-permute-start(bf16[32,2560]{1,0:T(8,128)(2,1)S(1)} %get-tuple-element.48), channel_id=1, source_target_pairs={{0,4},{2,6},{4,0},{6,2},{1,5},{3,7},{5,1},{7,3},{8,12},{10,14},{12... | collective-permute-start | bytes 491528 | tf_op jit(solution)/shard_map/ppermute | solution.py:85
  63.5 17.6 %collective-permute-start.17 = (bf16[128,2560]{1,0:T(8,128)(2,1)S(1)}, bf16[128,2560]{1,0:T(8,128)(2,1)S(1)}, u32[]{:S(2)}, u32[]{:S(2)}) collective-permute-start(bf16[128,2560]{1,0:T(8,128)(2,1)S(1)} %get-tuple-element.51), channel_id=1, source_target_pairs={{0,8},{8,0},{16,24},{24,16},{1,9},{9,1},{17,25},{25,17},{2,10},{10... | collective-permute-start | bytes 1966088 | tf_op jit(solution)/shard_map/ppermute | solution.py:85
  68.1 10.7 %collective-permute-start.21 = (bf16[64,2560]{1,0:T(8,128)(2,1)S(1)}, bf16[64,2560]{1,0:T(8,128)(2,1)S(1)}, u32[]{:S(2)}, u32[]{:S(2)}) collective-permute-start(bf16[64,2560]{1,0:T(8,128)(2,1)S(1)} %pad_maximum_fusion.3), channel_id=1, source_target_pairs={{0,4},{2,6},{4,0},{6,2},{1,5},{3,7},{5,1},{7,3},{8,12},{10,14},{12... | collective-permute-start | bytes 983048 | tf_op jit(solution)/shard_map/ppermute | solution.py:85
  69.1 9.7 %collective-permute-start.20 = (bf16[64,2560]{1,0:T(8,128)(2,1)S(1)}, bf16[64,2560]{1,0:T(8,128)(2,1)S(1)}, u32[]{:S(2)}, u32[]{:S(2)}) collective-permute-start(bf16[64,2560]{1,0:T(8,128)(2,1)S(1)} %pad_maximum_fusion.2), channel_id=1, source_target_pairs={{0,2},{2,0},{4,6},{6,4},{1,3},{3,1},{5,7},{7,5},{8,10},{10,8},{12,... | collective-permute-start | bytes 983048 | tf_op jit(solution)/shard_map/ppermute | solution.py:85
  70.1 15.7 %collective-permute-start.30 = (bf16[64,2560]{1,0:T(8,128)(2,1)S(1)}, bf16[64,2560]{1,0:T(8,128)(2,1)S(1)}, u32[]{:S(2)}, u32[]{:S(2)}) collective-permute-start(bf16[64,2560]{1,0:T(8,128)(2,1)S(1)} %add_convert_fusion.2), channel_id=1, source_target_pairs={{0,4},{2,6},{4,0},{6,2},{1,5},{3,7},{5,1},{7,3},{8,12},{10,14},{12... | collective-permute-start | bytes 983048 | tf_op jit(solution)/shard_map/ppermute | solution.py:85
  78.9 9.5 %collective-permute-start.27 = (bf16[64,2560]{1,0:T(8,128)(2,1)S(1)}, bf16[64,2560]{1,0:T(8,128)(2,1)S(1)}, u32[]{:S(2)}, u32[]{:S(2)}) collective-permute-start(bf16[64,2560]{1,0:T(8,128)(2,1)S(1)} %add_convert_fusion.3), channel_id=1, source_target_pairs={{0,8},{8,0},{16,24},{24,16},{1,9},{9,1},{17,25},{25,17},{2,10},{10... | collective-permute-start | bytes 983048 | tf_op jit(solution)/shard_map/ppermute | solution.py:85
  81.1 12.9 %collective-permute-start.26 = (bf16[64,2560]{1,0:T(8,128)(2,1)S(1)}, bf16[64,2560]{1,0:T(8,128)(2,1)S(1)}, u32[]{:S(2)}, u32[]{:S(2)}) collective-permute-start(bf16[64,2560]{1,0:T(8,128)(2,1)S(1)} %get-tuple-element.62), channel_id=1, source_target_pairs={{0,4},{2,6},{4,0},{6,2},{1,5},{3,7},{5,1},{7,3},{8,12},{10,14},{12... | collective-permute-start | bytes 983048 | tf_op jit(solution)/shard_map/ppermute | solution.py:85
  81.3 13.5 %collective-permute-start.24 = (bf16[32,2560]{1,0:T(8,128)(2,1)S(1)}, bf16[32,2560]{1,0:T(8,128)(2,1)S(1)}, u32[]{:S(2)}, u32[]{:S(2)}) collective-permute-start(bf16[32,2560]{1,0:T(8,128)(2,1)S(1)} %get-tuple-element.70), channel_id=1, source_target_pairs={{0,2},{2,0},{4,6},{6,4},{1,3},{3,1},{5,7},{7,5},{8,10},{10,8},{12,... | collective-permute-start | bytes 491528 | tf_op jit(solution)/shard_map/ppermute | solution.py:85
  81.8 13.7 %collective-permute-start.22 = (bf16[32,2560]{1,0:T(8,128)(2,1)S(1)}, bf16[32,2560]{1,0:T(8,128)(2,1)S(1)}, u32[]{:S(2)}, u32[]{:S(2)}) collective-permute-start(bf16[32,2560]{1,0:T(8,128)(2,1)S(1)} %get-tuple-element.69), channel_id=1, source_target_pairs={{0,4},{2,6},{4,0},{6,2},{1,5},{3,7},{5,1},{7,3},{8,12},{10,14},{12... | collective-permute-start | bytes 491528 | tf_op jit(solution)/shard_map/ppermute | solution.py:85
  88.6 13.8 %collective-permute-start.31 = (bf16[64,2560]{1,0:T(8,128)(2,1)S(1)}, bf16[64,2560]{1,0:T(8,128)(2,1)S(1)}, u32[]{:S(2)}, u32[]{:S(2)}) collective-permute-start(bf16[64,2560]{1,0:T(8,128)(2,1)S(1)} %add_convert_fusion.1), channel_id=1, source_target_pairs={{0,16},{8,24},{16,0},{24,8},{1,17},{9,25},{17,1},{25,9},{2,18},{10... | collective-permute-start | bytes 983048 | tf_op jit(solution)/shard_map/ppermute | solution.py:85
  94.1 9.6 %collective-permute-start.28 = (bf16[64,2560]{1,0:T(8,128)(2,1)S(1)}, bf16[64,2560]{1,0:T(8,128)(2,1)S(1)}, u32[]{:S(2)}, u32[]{:S(2)}) collective-permute-start(bf16[64,2560]{1,0:T(8,128)(2,1)S(1)} %add_convert_fusion.4), channel_id=1, source_target_pairs={{0,8},{8,0},{16,24},{24,16},{1,9},{9,1},{17,25},{25,17},{2,10},{10... | collective-permute-start | bytes 983048 | tf_op jit(solution)/shard_map/ppermute | solution.py:85
  94.9 8.8 %collective-permute-start.25 = (bf16[64,2560]{1,0:T(8,128)(2,1)S(1)}, bf16[64,2560]{1,0:T(8,128)(2,1)S(1)}, u32[]{:S(2)}, u32[]{:S(2)}) collective-permute-start(bf16[64,2560]{1,0:T(8,128)(2,1)S(1)} %pad_maximum_fusion.5), channel_id=1, source_target_pairs={{0,4},{2,6},{4,0},{6,2},{1,5},{3,7},{5,1},{7,3},{8,12},{10,14},{12... | collective-permute-start | bytes 983048 | tf_op jit(solution)/shard_map/ppermute | solution.py:85
  95.6 8.0 %collective-permute-start.23 = (bf16[64,2560]{1,0:T(8,128)(2,1)S(1)}, bf16[64,2560]{1,0:T(8,128)(2,1)S(1)}, u32[]{:S(2)}, u32[]{:S(2)}) collective-permute-start(bf16[64,2560]{1,0:T(8,128)(2,1)S(1)} %pad_maximum_fusion.4), channel_id=1, source_target_pairs={{0,2},{2,0},{4,6},{6,4},{1,3},{3,1},{5,7},{7,5},{8,10},{10,8},{12,... | collective-permute-start | bytes 983048 | tf_op jit(solution)/shard_map/ppermute | solution.py:85
